TPU v7x, 32 devices: a whole 2x2x4 slice. The times are simulated.
32 devices in a mesh: dp: 8 (over z, core), seq: 4 (over y, x).
Axes of the slice: x: 2, y: 2, z: 4, core: 2. Of those that a mesh axis runs over, the one named last changes fastest.
Arguments:
- inputs: float32 [2, 8, 1024, 960], P(None, 'dp', 'seq'), may hold values from -6 to 6
- cotangent: float32 [2, 8, 1024, 960], P(None, 'dp', 'seq'), may hold values from -6 to 6
- segments: int32 [2, 8, 1024], P(None, 'dp', 'seq'), may hold values from 0 to 2, as said below
- depths: int32 [2, 8, 1024], P(None, 'dp', 'seq'), may hold values from 1 to 3
- query_weight: bfloat16 [960, 960], P('dp', 'seq'), may hold values from -0.1875 to 0.1875
- key_weight: bfloat16 [960, 320], P('dp', 'seq'), may hold values from -0.1875 to 0.1875
- value_weight: bfloat16 [960, 320], P('dp', 'seq'), may hold values from -0.1875 to 0.1875
- out_weight: bfloat16 [960, 960], P('dp', 'seq'), may hold values from -0.75 to 0.75
- gate_weight: bfloat16 [960, 2560], P('dp', 'seq'), may hold values from -0.1875 to 0.1875
- up_weight: bfloat16 [960, 2560], P('dp', 'seq'), may hold values from -0.1875 to 0.1875
- down_weight: bfloat16 [2560, 960], P('dp', 'seq'), may hold values from -0.125 to 0.125
- attn_gain: bfloat16 [960], P('dp'), may hold values from 0.25 to 1.75
- ffn_gain: bfloat16 [960], P('dp'), may hold values from 0.25 to 1.75
- router_weight: bfloat16 [960, 3], P('dp'), may hold values from -0.1875 to 0.1875
Outputs:
- outputs: float32 [2, 8, 1024, 960], P(None, 'dp', 'seq')
- input_grad: float32 [2, 8, 1024, 960], P(None, 'dp', 'seq')
- query_grad: float32 [960, 960], P('dp', 'seq')
- key_grad: float32 [960, 320], P('dp', 'seq')
- value_grad: float32 [960, 320], P('dp', 'seq')
- out_grad: float32 [960, 960], P('dp', 'seq')
- gate_grad: float32 [960, 2560], P('dp', 'seq')
- up_grad: float32 [960, 2560], P('dp', 'seq')
- down_grad: float32 [2560, 960], P('dp', 'seq')
- attn_gain_grad: float32 [960], P('dp')
- ffn_gain_grad: float32 [960], P('dp')
- router_grad: float32 [960, 3], P('dp')
Inputs may be any that keep to these rules, and one draw needn't show every extreme that they name: `segments`: segment numbers never fall along a pack.
All inputs are finite; a program needn't handle non-finite values.
Results may differ from a plain program's by a relative error of at most 0.028.
Values may be sent and summed in bfloat16 or wider, within the bound.
A program may use at most 384 MiB of HBM per device.

v0:
```python
import jax
import jax.numpy as jnp
from jax import lax
from jax.sharding import PartitionSpec as P

HEADS = 15
KV_HEADS = 5
HEAD_DIM = 64
RECUR = 3


epsilon = 1e-05
rope_base = 10000.0


def root_norm(values_in, gain_vec):
    inverse = lax.rsqrt(jnp.mean(values_in * values_in, axis=-1, keepdims=True) + epsilon)
    return values_in * inverse * gain_vec


def rotate(values_in, positions, turn_sign):
    row_count = values_in.shape[0]
    head_count = values_in.shape[1] // HEAD_DIM
    half_dim = HEAD_DIM // 2
    frequency = rope_base ** (-(jnp.arange(half_dim, dtype=jnp.float32) * 2.0 / HEAD_DIM))
    angles = positions.astype(jnp.float32)[:, None] * frequency[None, :]
    cosine = jnp.cos(angles)[:, None, :]
    sine_part = turn_sign * jnp.sin(angles)[:, None, :]
    pieces = values_in.reshape(row_count, head_count, HEAD_DIM)
    first_half = pieces[:, :, :half_dim]
    second = pieces[:, :, half_dim:]
    turned = jnp.concatenate(
        [first_half * cosine - second * sine_part, second * cosine + first_half * sine_part],
        axis=-1,
    )
    return turned.reshape(row_count, head_count * HEAD_DIM)


def score_table(queries, keys_all, visible):
    query_rows = queries.shape[0]
    groups = HEADS // KV_HEADS
    query_heads = queries.reshape(query_rows, KV_HEADS, groups, HEAD_DIM)
    key_heads = keys_all.reshape(keys_all.shape[0], KV_HEADS, HEAD_DIM)
    scaled = jnp.einsum(
        "qkgd,tkd->kgqt", query_heads, key_heads, preferred_element_type=jnp.float32
    ) * HEAD_DIM ** (-0.5)
    return (jnp.where(visible[None, None], scaled, -1e30), query_heads, key_heads)


def attend_back(queries, keys_all, values_all, visible, log_total, grad_attended):
    masked, query_heads, key_heads = score_table(queries, keys_all, visible)
    probs = jnp.exp(masked - log_total)
    query_rows = queries.shape[0]
    key_rows = keys_all.shape[0]
    grad_heads = grad_attended.reshape(query_heads.shape)
    value_heads = values_all.reshape(key_rows, KV_HEADS, HEAD_DIM)
    grad_probs = jnp.einsum(
        "qkgd,tkd->kgqt", grad_heads, value_heads, preferred_element_type=jnp.float32
    )
    grad_values = jnp.einsum(
        "kgqt,qkgd->tkd", probs.astype(jnp.bfloat16), grad_heads, preferred_element_type=jnp.float32
    ).reshape(key_rows, KV_HEADS * HEAD_DIM)
    grad_scores = (
        probs * (grad_probs - jnp.sum(grad_probs * probs, axis=-1, keepdims=True))
    ).astype(jnp.bfloat16)
    score_scale = HEAD_DIM ** (-0.5)
    grad_queries = (
        jnp.einsum(
            "kgqt,tkd->qkgd", grad_scores, key_heads, preferred_element_type=jnp.float32
        ).reshape(query_rows, HEADS * HEAD_DIM)
        * score_scale
    )
    grad_keys = (
        jnp.einsum(
            "kgqt,qkgd->tkd", grad_scores, query_heads, preferred_element_type=jnp.float32
        ).reshape(key_rows, KV_HEADS * HEAD_DIM)
        * score_scale
    )
    return (grad_queries, grad_keys, grad_values)


def gather_weights(
    query_weight,
    key_weight,
    value_weight,
    out_weight,
    gate_weight,
    up_weight,
    down_weight,
    attn_gain,
    ffn_gain,
    router_weight,
):
    query_cols, key_cols, value_cols, out_cols, gate_cols, up_cols, down_cols = (
        lax.all_gather(query_weight, "seq", axis=1, tiled=True),
        lax.all_gather(key_weight, "seq", axis=1, tiled=True),
        lax.all_gather(value_weight, "seq", axis=1, tiled=True),
        lax.all_gather(out_weight, "seq", axis=1, tiled=True),
        lax.all_gather(gate_weight, "seq", axis=1, tiled=True),
        lax.all_gather(up_weight, "seq", axis=1, tiled=True),
        lax.all_gather(down_weight, "seq", axis=1, tiled=True),
    )
    return (
        lax.all_gather(query_cols, "dp", axis=0, tiled=True),
        lax.all_gather(key_cols, "dp", axis=0, tiled=True),
        lax.all_gather(value_cols, "dp", axis=0, tiled=True),
        lax.all_gather(out_cols, "dp", axis=0, tiled=True),
        lax.all_gather(gate_cols, "dp", axis=0, tiled=True),
        lax.all_gather(up_cols, "dp", axis=0, tiled=True),
        lax.all_gather(down_cols, "dp", axis=0, tiled=True),
        lax.all_gather(attn_gain, "dp", axis=0, tiled=True),
        lax.all_gather(ffn_gain, "dp", axis=0, tiled=True),
        lax.all_gather(router_weight, "dp", axis=0, tiled=True),
    )


def reduce_grads(grads):
    (
        query_sum,
        key_sum,
        value_sum,
        out_sum,
        gate_sum,
        up_sum,
        down_sum,
        attn_sum,
        ffn_sum,
        router_sum,
    ) = grads
    (
        query_sum,
        key_sum,
        value_sum,
        out_sum,
        gate_sum,
        up_sum,
        down_sum,
        attn_sum,
        ffn_sum,
        router_sum,
    ) = (
        lax.psum_scatter(
            query_sum.astype(jnp.bfloat16), "dp", scatter_dimension=0, tiled=True
        ).astype(jnp.float32),
        lax.psum_scatter(
            key_sum.astype(jnp.bfloat16), "dp", scatter_dimension=0, tiled=True
        ).astype(jnp.float32),
        lax.psum_scatter(
            value_sum.astype(jnp.bfloat16), "dp", scatter_dimension=0, tiled=True
        ).astype(jnp.float32),
        lax.psum_scatter(
            out_sum.astype(jnp.bfloat16), "dp", scatter_dimension=0, tiled=True
        ).astype(jnp.float32),
        lax.psum_scatter(
            gate_sum.astype(jnp.bfloat16), "dp", scatter_dimension=0, tiled=True
        ).astype(jnp.float32),
        lax.psum_scatter(up_sum.astype(jnp.bfloat16), "dp", scatter_dimension=0, tiled=True).astype(
            jnp.float32
        ),
        lax.psum_scatter(
            down_sum.astype(jnp.bfloat16), "dp", scatter_dimension=0, tiled=True
        ).astype(jnp.float32),
        lax.psum_scatter(
            attn_sum.astype(jnp.bfloat16), "dp", scatter_dimension=0, tiled=True
        ).astype(jnp.float32),
        lax.psum_scatter(
            ffn_sum.astype(jnp.bfloat16), "dp", scatter_dimension=0, tiled=True
        ).astype(jnp.float32),
        lax.psum_scatter(
            router_sum.astype(jnp.bfloat16), "dp", scatter_dimension=0, tiled=True
        ).astype(jnp.float32),
    )
    query_sum, key_sum, value_sum, out_sum, gate_sum, up_sum, down_sum = (
        lax.psum_scatter(
            query_sum.astype(jnp.bfloat16), "seq", scatter_dimension=1, tiled=True
        ).astype(jnp.float32),
        lax.psum_scatter(
            key_sum.astype(jnp.bfloat16), "seq", scatter_dimension=1, tiled=True
        ).astype(jnp.float32),
        lax.psum_scatter(
            value_sum.astype(jnp.bfloat16), "seq", scatter_dimension=1, tiled=True
        ).astype(jnp.float32),
        lax.psum_scatter(
            out_sum.astype(jnp.bfloat16), "seq", scatter_dimension=1, tiled=True
        ).astype(jnp.float32),
        lax.psum_scatter(
            gate_sum.astype(jnp.bfloat16), "seq", scatter_dimension=1, tiled=True
        ).astype(jnp.float32),
        lax.psum_scatter(
            up_sum.astype(jnp.bfloat16), "seq", scatter_dimension=1, tiled=True
        ).astype(jnp.float32),
        lax.psum_scatter(
            down_sum.astype(jnp.bfloat16), "seq", scatter_dimension=1, tiled=True
        ).astype(jnp.float32),
    )
    attn_sum, ffn_sum, router_sum = lax.psum((attn_sum, ffn_sum, router_sum), "seq")
    return (
        query_sum,
        key_sum,
        value_sum,
        out_sum,
        gate_sum,
        up_sum,
        down_sum,
        attn_sum,
        ffn_sum,
        router_sum,
    )


def micro_pass(inputs_mb, cotangent_mb, segments_mb, depths_mb, weights):
    query_w, key_w, value_w, out_w, gate_w, up_w, down_w, attn_g, ffn_g, router_w = weights
    tokens_dev = inputs_mb.shape[0]
    pack_length = tokens_dev * lax.axis_size("seq")
    positions = lax.axis_index("seq") * tokens_dev + jnp.arange(tokens_dev, dtype=jnp.int32)
    all_positions = jnp.arange(pack_length, dtype=jnp.int32)
    all_segments, all_depths = (
        lax.all_gather(segments_mb, "seq", axis=0, tiled=True),
        lax.all_gather(depths_mb, "seq", axis=0, tiled=True),
    )
    attn_gain_f = attn_g.astype(jnp.float32)
    ffn_gain_f = ffn_g.astype(jnp.float32)
    router_f = router_w.astype(jnp.float32)
    same_doc = (segments_mb[:, None] == all_segments[None, :]) & (
        all_positions[None, :] <= positions[:, None]
    )
    is_self = all_positions[None, :] == positions[:, None]
    state = inputs_mb
    saved = []
    for recursion in range(RECUR):
        active = (depths_mb > recursion).astype(jnp.float32)
        visible = same_doc & ((all_depths[None, :] > recursion) | is_self)
        attn_input = root_norm(state, attn_gain_f).astype(jnp.bfloat16)
        queries = rotate(
            jnp.dot(attn_input, query_w, preferred_element_type=jnp.float32), positions, 1.0
        ).astype(jnp.bfloat16)
        keys_own = rotate(
            jnp.dot(attn_input, key_w, preferred_element_type=jnp.float32), positions, 1.0
        ).astype(jnp.bfloat16)
        values_own = jnp.dot(attn_input, value_w, preferred_element_type=jnp.float32).astype(
            jnp.bfloat16
        )
        keys_all, values_all = (
            lax.all_gather(keys_own, "seq", axis=0, tiled=True),
            lax.all_gather(values_own, "seq", axis=0, tiled=True),
        )
        masked, query_heads, key_heads = score_table(queries, keys_all, visible)
        top_score = jnp.max(masked, axis=-1, keepdims=True)
        exp_scores = jnp.exp(masked - top_score)
        totals = jnp.sum(exp_scores, axis=-1, keepdims=True)
        probs = exp_scores / totals
        log_total = top_score + jnp.log(totals)
        value_heads = values_all.reshape(pack_length, KV_HEADS, HEAD_DIM)
        attended = (
            jnp.einsum(
                "kgqt,tkd->qkgd",
                probs.astype(jnp.bfloat16),
                value_heads,
                preferred_element_type=jnp.float32,
            )
            .reshape(tokens_dev, HEADS * HEAD_DIM)
            .astype(jnp.bfloat16)
        )
        attn_branch = jnp.dot(attended, out_w, preferred_element_type=jnp.float32)
        midway = state + attn_branch
        ffn_input = root_norm(midway, ffn_gain_f).astype(jnp.bfloat16)
        gate_pre = jnp.dot(ffn_input, gate_w, preferred_element_type=jnp.float32)
        up_pre = jnp.dot(ffn_input, up_w, preferred_element_type=jnp.float32)
        hidden = (jax.nn.silu(gate_pre) * up_pre).astype(jnp.bfloat16)
        ffn_branch = jnp.dot(hidden, down_w, preferred_element_type=jnp.float32)
        router_gate = jax.nn.sigmoid(jnp.sum(state * router_f[:, recursion][None, :], axis=-1))
        update = attn_branch + ffn_branch
        saved.append(
            (
                state,
                attn_input,
                queries,
                keys_all,
                values_all,
                visible,
                log_total,
                attended,
                midway,
                ffn_input,
                gate_pre,
                up_pre,
                hidden,
                update,
                router_gate,
                active,
            )
        )
        state = state + (active * router_gate)[:, None] * update
    grad_state = cotangent_mb
    query_sum = jnp.zeros(query_w.shape, jnp.float32)
    key_sum = jnp.zeros(key_w.shape, jnp.float32)
    value_sum = jnp.zeros(value_w.shape, jnp.float32)
    out_sum = jnp.zeros(out_w.shape, jnp.float32)
    gate_sum = jnp.zeros(gate_w.shape, jnp.float32)
    up_sum = jnp.zeros(up_w.shape, jnp.float32)
    down_sum = jnp.zeros(down_w.shape, jnp.float32)
    attn_sum = jnp.zeros(attn_g.shape, jnp.float32)
    ffn_sum = jnp.zeros(ffn_g.shape, jnp.float32)
    router_cols = []
    for recursion in reversed(range(RECUR)):
        (
            state_in,
            attn_input,
            queries,
            keys_all,
            values_all,
            visible,
            log_total,
            attended,
            midway,
            ffn_input,
            gate_pre,
            up_pre,
            hidden,
            update,
            router_gate,
            active,
        ) = saved[recursion]
        grad_update = grad_state * (active * router_gate)[:, None]
        grad_logit = (
            jnp.sum(grad_state * update, axis=-1) * active * router_gate * (1.0 - router_gate)
        )
        router_cols.append(jnp.sum(grad_logit[:, None] * state_in, axis=0))
        grad_ffn = grad_update.astype(jnp.bfloat16)
        down_sum = down_sum + jnp.einsum(
            "tf,td->fd", hidden, grad_ffn, preferred_element_type=jnp.float32
        )
        grad_hidden = jnp.einsum("td,fd->tf", grad_ffn, down_w, preferred_element_type=jnp.float32)
        swiglu_out, swiglu_pull = jax.vjp(
            lambda gate_in, up_in: jax.nn.silu(gate_in) * up_in, gate_pre, up_pre
        )
        grad_gate, grad_up = swiglu_pull(grad_hidden)
        grad_gate = grad_gate.astype(jnp.bfloat16)
        grad_up = grad_up.astype(jnp.bfloat16)
        gate_sum = gate_sum + jnp.einsum(
            "td,tf->df", ffn_input, grad_gate, preferred_element_type=jnp.float32
        )
        up_sum = up_sum + jnp.einsum(
            "td,tf->df", ffn_input, grad_up, preferred_element_type=jnp.float32
        )
        grad_ffn_input = jnp.einsum(
            "tf,df->td", grad_gate, gate_w, preferred_element_type=jnp.float32
        ) + jnp.einsum("tf,df->td", grad_up, up_w, preferred_element_type=jnp.float32)
        norm_out, norm_pull = jax.vjp(root_norm, midway, ffn_gain_f)
        grad_midway, grad_ffn_gain = norm_pull(grad_ffn_input)
        ffn_sum = ffn_sum + grad_ffn_gain
        grad_branch = (grad_update + grad_midway).astype(jnp.bfloat16)
        out_sum = out_sum + jnp.einsum(
            "tc,td->cd", attended, grad_branch, preferred_element_type=jnp.float32
        )
        grad_attended = jnp.einsum(
            "td,cd->tc", grad_branch, out_w, preferred_element_type=jnp.float32
        ).astype(jnp.bfloat16)
        grad_queries, grad_keys_all, grad_values_all = attend_back(
            queries, keys_all, values_all, visible, log_total, grad_attended
        )
        grad_keys, grad_values = (
            lax.psum_scatter(
                grad_keys_all.astype(jnp.bfloat16), "seq", scatter_dimension=0, tiled=True
            ).astype(jnp.float32),
            lax.psum_scatter(
                grad_values_all.astype(jnp.bfloat16), "seq", scatter_dimension=0, tiled=True
            ).astype(jnp.float32),
        )
        grad_query_pre = rotate(grad_queries, positions, -1.0).astype(jnp.bfloat16)
        grad_key_pre = rotate(grad_keys, positions, -1.0).astype(jnp.bfloat16)
        grad_value_pre = grad_values.astype(jnp.bfloat16)
        query_sum = query_sum + jnp.einsum(
            "td,tc->dc", attn_input, grad_query_pre, preferred_element_type=jnp.float32
        )
        key_sum = key_sum + jnp.einsum(
            "td,tc->dc", attn_input, grad_key_pre, preferred_element_type=jnp.float32
        )
        value_sum = value_sum + jnp.einsum(
            "td,tc->dc", attn_input, grad_value_pre, preferred_element_type=jnp.float32
        )
        grad_attn_input = jnp.einsum(
            "tc,dc->td", grad_query_pre, query_w, preferred_element_type=jnp.float32
        )
        grad_attn_input = grad_attn_input + jnp.einsum(
            "tc,dc->td", grad_key_pre, key_w, preferred_element_type=jnp.float32
        )
        grad_attn_input = grad_attn_input + jnp.einsum(
            "tc,dc->td", grad_value_pre, value_w, preferred_element_type=jnp.float32
        )
        first_out, first_pull = jax.vjp(root_norm, state_in, attn_gain_f)
        grad_norm_in, grad_attn_gain = first_pull(grad_attn_input)
        attn_sum = attn_sum + grad_attn_gain
        grad_state = (
            grad_state
            + grad_logit[:, None] * router_f[:, recursion][None, :]
            + grad_midway
            + grad_norm_in
        )
    router_sum = jnp.stack(router_cols[::-1], axis=1)
    grads = (
        query_sum,
        key_sum,
        value_sum,
        out_sum,
        gate_sum,
        up_sum,
        down_sum,
        attn_sum,
        ffn_sum,
        router_sum,
    )
    return (state, grad_state, grads)


def local(
    inputs,
    cotangent,
    segments,
    depths,
    query_weight,
    key_weight,
    value_weight,
    out_weight,
    gate_weight,
    up_weight,
    down_weight,
    attn_gain,
    ffn_gain,
    router_weight,
):
    micro_count = inputs.shape[0]
    output_list = []
    input_list = []
    totals = ()
    for micro in range(micro_count):
        weights = gather_weights(
            query_weight,
            key_weight,
            value_weight,
            out_weight,
            gate_weight,
            up_weight,
            down_weight,
            attn_gain,
            ffn_gain,
            router_weight,
        )
        outputs_mb, input_grad_mb, grads = micro_pass(
            inputs[micro, 0], cotangent[micro, 0], segments[micro, 0], depths[micro, 0], weights
        )
        output_list.append(outputs_mb)
        input_list.append(input_grad_mb)
        if micro == 0:
            totals = grads
        else:
            totals = tuple((earlier + latest for earlier, latest in zip(totals, grads)))
    totals = reduce_grads(totals)
    outputs = jnp.stack(output_list, axis=0)[:, None]
    input_grad = jnp.stack(input_list, axis=0)[:, None]
    return (
        outputs,
        input_grad,
        totals[0],
        totals[1],
        totals[2],
        totals[3],
        totals[4],
        totals[5],
        totals[6],
        totals[7],
        totals[8],
        totals[9],
    )


def solution(mesh):
    in_specs = (
        P(None, "dp", "seq", None),
        P(None, "dp", "seq", None),
        P(None, "dp", "seq"),
        P(None, "dp", "seq"),
        P("dp", "seq"),
        P("dp", "seq"),
        P("dp", "seq"),
        P("dp", "seq"),
        P("dp", "seq"),
        P("dp", "seq"),
        P("dp", "seq"),
        P("dp"),
        P("dp"),
        P("dp", None),
    )
    out_specs = (
        P(None, "dp", "seq", None),
        P(None, "dp", "seq", None),
        P("dp", "seq"),
        P("dp", "seq"),
        P("dp", "seq"),
        P("dp", "seq"),
        P("dp", "seq"),
        P("dp", "seq"),
        P("dp", "seq"),
        P("dp"),
        P("dp"),
        P("dp", None),
    )
    return jax.shard_map(local, mesh=mesh, in_specs=in_specs, out_specs=out_specs, check_vma=False)
```

profile of v0, /device:TPU:0, one launch (start us, length us, event | category | flops | bytes accessed | tf_op | source)
XLA Modules:
  0.0 1589.4 jit_solution(6918667052732127036)
XLA Ops:
  70.4 14.3 all-reduce.14
  102.5 18.4 %all-gather.5 = bf16[8,120,320]{1,2,0:T(8,128)(2,1)S(1)} all-gather(bf16[1,120,320]{1,2,0:T(8,128)(2,1)S(1)} %bitcast.954), channel_id=1, replica_groups=mesh['dp'=8,'seq'=4] {'dp'}, dimensions={0}, use_global_device_ids=true | all-gather | bytes 691200 | tf_op jit(solution)/shard_map/all_gather | solution.py:106
  134.1 14.9 all-gather.6
  156.8 17.1 %all_gather.144 = bf16[1024,320]{0,1:T(8,128)(2,1)} all-gather(bf16[256,320]{0,1:T(8,128)(2,1)S(1)} %bitcast.948), channel_id=1, replica_groups=mesh['dp'=8,'seq'=4] {'seq'}, dimensions={0}, use_global_device_ids=true | all-gather | bytes 819200 | tf_op jit(solution)/shard_map/all_gather | solution.py:244
  204.9 13.4 all_gather.141
  218.3 15.2 all_gather.125
  233.5 13.2 all_gather.120
  298.8 15.9 %fusion.132 = bf16[5,64,3,256]{3,1,2,0:T(8,128)(2,1)S(1)} fusion(bf16[1024,5,64,1]{0,2,3,1:T(8,128)(2,1)S(1)} %bitcast.871, f32[5,3,256,1024]{2,3,1,0:T(8,128)} %get-tuple-element.307, f32[5,3,256]{2,1,0:T(4,128)S(1)} %fusion.21, f32[5,3,256]{2,1,0:T(4,128)S(1)} %get-tuple-element.306), kind=kOutput, calls=%fused_computation.231 | convolution fusion | flops 515358720 | bytes 16906240 | tf_op jit(solution)/shard_map/kgqt,tkd->qkgd/dot_general | solution.py:255
  351.6 13.9 all_gather.138
  404.1 13.0 all_gather.146
  474.8 13.0 all_gather.140
  505.3 15.7 all_gather.139
  543.5 13.8 all_gather.147
  658.9 12.8 fusion.6
  757.9 13.5 fusion.12
  821.4 21.7 %reduce-scatter.42.cloned.1.call-done = bf16[256,320]{0,1:T(8,128)(2,1)} async-done(((bf16[1024,320]{0,1:T(8,128)(2,1)}), bf16[256,320]{0,1:T(8,128)(2,1)}) %reduce-scatter.42.cloned.1.call-update) | async-done | bytes 163856 | tf_op jit(solution)/shard_map/reduce_scatter | solution.py:366
  925.5 24.8 %reduce-scatter.54.cloned.1.call-done = bf16[256,320]{0,1:T(8,128)(2,1)} async-done(((bf16[1024,320]{0,1:T(8,128)(2,1)}), bf16[256,320]{0,1:T(8,128)(2,1)}) %reduce-scatter.54.cloned.1.call-update) | async-done | bytes 163856 | tf_op jit(solution)/shard_map/reduce_scatter | solution.py:366
  993.5 12.8 fusion.9
  1056.2 18.0 %reduce-scatter.58.cloned.1.call-done = bf16[256,320]{0,1:T(8,128)(2,1)} async-done(((bf16[1024,320]{0,1:T(8,128)(2,1)}), bf16[256,320]{0,1:T(8,128)(2,1)}) %reduce-scatter.58.cloned.1.call-update) | async-done | bytes 163856 | tf_op jit(solution)/shard_map/reduce_scatter | solution.py:366
  1079.6 23.0 %reduce-scatter.46.cloned.1.call-done = bf16[256,320]{0,1:T(8,128)(2,1)} async-done(((bf16[1024,320]{0,1:T(8,128)(2,1)}), bf16[256,320]{0,1:T(8,128)(2,1)}) %reduce-scatter.46.cloned.1.call-update) | async-done | bytes 163856 | tf_op jit(solution)/shard_map/reduce_scatter | solution.py:366
  1148.3 20.3 %add_convert_fusion = bf16[2560,960]{1,0:T(8,128)(2,1)} fusion(f32[2560,960]{1,0:T(8,128)} %fusion.192, f32[2560,960]{1,0:T(8,128)} %fusion.189, f32[2560,960]{1,0:T(8,128)} %fusion.187, f32[2560,960]{1,0:T(8,128)} %fusion.196, f32[2560,960]{1,0:T(8,128)} %fusion.185, bf16[256,2560]{1,0:T(8,128)(2,1)S(1)} %copy-done.220, f32[256,960]{0,1:T(8,128)S(1)} %copy-done.61, ...), kind=kOutput, calls=%fused_computation.66 | convolution fusion | flops 1273528320 | bytes 56361984 | tf_op jit(solution)/shard_map/tf,td->fd/dot_general | solution.py:330
  1196.9 19.8 %add_convert_fusion.1 = bf16[960,2560]{1,0:T(8,128)(2,1)} fusion(f32[960,2560]{1,0:T(8,128)} %fusion.269, f32[960,2560]{1,0:T(8,128)} %fusion.270, f32[960,2560]{1,0:T(8,128)} %fusion.268, f32[960,2560]{1,0:T(8,128)} %fusion.266, f32[960,2560]{1,0:T(8,128)} %fusion.267, bf16[256,960]{0,1:T(8,128)(2,1)} %get-tuple-element.290, ...), kind=kOutput, calls=%fused_computation.67 | convolution fusion | flops 1273036800 | bytes 55869440 | tf_op jit(solution)/shard_map/td,tf->df/dot_general | solution.py:343
  1244.1 20.1 %add_convert_fusion.2 = bf16[960,2560]{1,0:T(8,128)(2,1)} fusion(f32[960,2560]{1,0:T(8,128)} %fusion.264, f32[960,2560]{1,0:T(8,128)} %fusion.265, f32[960,2560]{1,0:T(8,128)} %fusion.263, f32[960,2560]{1,0:T(8,128)} %fusion.261, f32[960,2560]{1,0:T(8,128)} %fusion.262, bf16[256,960]{0,1:T(8,128)(2,1)S(1)} %copy-done.95, bf16[256,2560]{1,0:T(8,128)(2,1)} %copy-done.205), kind=kOutput, calls=%fused_computation.68 | convolution fusion | flops 1273036800 | bytes 55869440 | tf_op jit(solution)/shard_map/td,tf->df/dot_general | solution.py:340
  1279.3 21.1 %reduce-scatter.68.cloned.1.call-done = bf16[320,960]{1,0:T(8,128)(2,1)} async-done(((bf16[2560,960]{1,0:T(8,128)(2,1)}), bf16[320,960]{1,0:T(8,128)(2,1)}) %reduce-scatter.68.cloned.1.call-update) | async-done | bytes 614416 | tf_op jit(solution)/shard_map/reduce_scatter | solution.py:160
  1306.5 51.4 %reduce-scatter.66.cloned.1.call-done = bf16[120,2560]{1,0:T(8,128)(2,1)} async-done(((bf16[960,2560]{1,0:T(8,128)(2,1)}), bf16[120,2560]{1,0:T(8,128)(2,1)}) %reduce-scatter.66.cloned.1.call-update) | async-done | bytes 614416 | tf_op jit(solution)/shard_map/reduce_scatter | solution.py:157
  1363.7 27.6 %all-reduce.13 = (bf16[960]{0:T(1024)(128)(2,1)S(1)}, bf16[960]{0:T(1024)(128)(2,1)S(1)}, bf16[960,3]{0,1:T(4,128)(2,1)S(1)}) all-reduce(bf16[960]{0:T(1024)(128)(2,1)S(1)} %add_convert_fusion.32, bf16[960]{0:T(1024)(128)(2,1)S(1)} %add_convert_fusion.31, bf16[960,3]{0,1:T(4,128)(2,1)S(1)} %fusion.200), channel_id=32, replica_groups=mesh['dp'=8,'seq'=4] {'dp'}, use_global_device_ids=true, to_apply=%region_86.87.clone | all-reduce | flops 4800 | bytes 19200
  1402.1 13.9 reduce-scatter.64.cloned.1.call-done
  1423.2 16.9 %reduce-scatter.76.cloned.1.call-done = bf16[120,80]{0,1:T(8,128)(2,1)} async-done(((bf16[120,320]{0,1:T(8,128)(2,1)}), bf16[120,80]{0,1:T(8,128)(2,1)}) %reduce-scatter.76.cloned.1.call-update) | async-done | bytes 19216
  1441.4 24.7 %reduce-scatter.74.cloned.1.call-done = bf16[120,80]{0,1:T(8,128)(2,1)} async-done(((bf16[120,320]{0,1:T(8,128)(2,1)}), bf16[120,80]{0,1:T(8,128)(2,1)}) %reduce-scatter.74.cloned.1.call-update) | async-done | bytes 19216
  1467.4 56.4 %all-reduce.22.cloned.1.call-done = (bf16[120,960]{1,0:T(8,128)(2,1)}, bf16[120,960]{1,0:T(8,128)(2,1)}, bf16[320,960]{1,0:T(8,128)(2,1)}) async-done(((bf16[120,960]{1,0:T(8,128)(2,1)}, bf16[120,960]{1,0:T(8,128)(2,1)}, bf16[320,960]{1,0:T(8,128)(2,1)}), (bf16[120,960]{1,0:T(8,128)(2,1)}, bf16[120,960]{1,0:T(8,128)(2,1)}, bf16[320,960]{1,0:T(8,128)(2,1)})) %all-reduce.22.cloned.1.call-update) | async-done | bytes 1075216
  1528.8 23.4 %reduce-scatter.72.cloned.1.call-done = bf16[640,120]{1,0:T(8,128)(2,1)} async-done(((bf16[2560,120]{1,0:T(8,128)(2,1)}), bf16[640,120]{1,0:T(8,128)(2,1)}) %reduce-scatter.72.cloned.1.call-update) | async-done | bytes 153616
  1554.1 26.5 %reduce-scatter.70.cloned.1.call-done = bf16[640,120]{1,0:T(8,128)(2,1)} async-done(((bf16[2560,120]{1,0:T(8,128)(2,1)}), bf16[640,120]{1,0:T(8,128)(2,1)}) %reduce-scatter.70.cloned.1.call-update) | async-done | bytes 153616
  (1295 shorter events, 926.5 us)
Async XLA Ops:
  7.2 242.4 %all-gather.14.cloned.1.call-start = ((), (), s32[]{:S(2)}) async-start(), calls=%async_computation.21 | async-start | bytes 2211840 | tf_op jit(solution)/shard_map/all_gather | solution.py:104
  19.5 260.6 %all-gather.16.cloned.1.call-start = ((), (), s32[]{:S(2)}) async-start(), calls=%async_computation.22 | async-start | bytes 2211840 | tf_op jit(solution)/shard_map/all_gather | solution.py:107
  30.5 289.2 %all-gather.18.cloned.1.call-start = ((), (), s32[]{:S(2)}) async-start(), calls=%async_computation.23 | async-start | bytes 5529600 | tf_op jit(solution)/shard_map/all_gather | solution.py:108
  42.2 286.4 %all-gather.20.cloned.1.call-start = ((), (), s32[]{:S(2)}) async-start(), calls=%async_computation.24 | async-start | bytes 5529600 | tf_op jit(solution)/shard_map/all_gather | solution.py:109
  54.8 284.9 %all-gather.22.cloned.1.call-start = ((), (), s32[]{:S(2)}) async-start(), calls=%async_computation.25 | async-start | bytes 5898240 | tf_op jit(solution)/shard_map/all_gather | solution.py:110
  66.9 661.8 %reduce-scatter.36.cloned.1.call-start = ((), (), s32[]{:S(2)}) async-start(), calls=%async_computation.26 | async-start | bytes 819200 | tf_op jit(solution)/shard_map/reduce_scatter | solution.py:363
  84.7 385.2 %copy-start.221 = (f32[960]{0:T(1024)}, f32[960]{0:T(1024)S(1)}, u32[]{:S(2)}) copy-start(f32[960]{0:T(1024)S(1)} %convert_element_type.673) | copy-start | bytes 11524
  121.9 229.2 %copy-start.7 = (bf16[960,320]{0,1:T(8,128)(2,1)}, bf16[960,320]{0,1:T(8,128)(2,1)S(1)}, u32[]{:S(2)}) copy-start(bf16[960,320]{0,1:T(8,128)(2,1)S(1)} %reshape.1518) | copy-start | bytes 1843204
  156.7 333.1 %copy-start.106 = (f32[256,32]{0,1:T(8,128)}, f32[256,32]{0,1:T(8,128)S(1)}, u32[]{:S(2)}) copy-start(f32[256,32]{0,1:T(8,128)S(1)} %get-tuple-element.298) | copy-start | bytes 98308
  246.7 205.8 %copy-start.227 = (f32[960]{0:T(1024)}, f32[960]{0:T(1024)S(1)}, u32[]{:S(2)}) copy-start(f32[960]{0:T(1024)S(1)} %convert_element_type.685) | copy-start | bytes 11524
  651.2 81.2 %reduce-scatter.38.cloned.1.call-start = ((), (), s32[]{:S(2)}) async-start(), calls=%async_computation.27 | async-start | bytes 819200 | tf_op jit(solution)/shard_map/reduce_scatter | solution.py:366
  697.4 54.7 %reduce-scatter.48.cloned.1.call-start = ((), (), s32[]{:S(2)}) async-start(), calls=%async_computation.32 | async-start | bytes 819200 | tf_op jit(solution)/shard_map/reduce_scatter | solution.py:363
  710.5 101.4 %reduce-scatter.50.cloned.1.call-start = ((), (), s32[]{:S(2)}) async-start(), calls=%async_computation.33 | async-start | bytes 819200 | tf_op jit(solution)/shard_map/reduce_scatter | solution.py:366
  725.2 89.3 %reduce-scatter.40.cloned.1.call-start = ((), (), s32[]{:S(2)}) async-start(), calls=%async_computation.28 | async-start | bytes 819200 | tf_op jit(solution)/shard_map/reduce_scatter | solution.py:363
  789.0 54.1 %reduce-scatter.42.cloned.1.call-start = ((), (), s32[]{:S(2)}) async-start(), calls=%async_computation.29 | async-start | bytes 819200 | tf_op jit(solution)/shard_map/reduce_scatter | solution.py:366
  803.9 117.8 %reduce-scatter.52.cloned.1.call-start = ((), (), s32[]{:S(2)}) async-start(), calls=%async_computation.34 | async-start | bytes 819200 | tf_op jit(solution)/shard_map/reduce_scatter | solution.py:363
  896.2 54.1 %reduce-scatter.54.cloned.1.call-start = ((), (), s32[]{:S(2)}) async-start(), calls=%async_computation.35 | async-start | bytes 819200 | tf_op jit(solution)/shard_map/reduce_scatter | solution.py:366
  908.1 143.2 %reduce-scatter.56.cloned.1.call-start = ((), (), s32[]{:S(2)}) async-start(), calls=%async_computation.36 | async-start | bytes 819200 | tf_op jit(solution)/shard_map/reduce_scatter | solution.py:363
  991.5 60.8 %reduce-scatter.44.cloned.1.call-start = ((), (), s32[]{:S(2)}) async-start(), calls=%async_computation.30 | async-start | bytes 819200 | tf_op jit(solution)/shard_map/reduce_scatter | solution.py:363
  1020.6 53.6 %reduce-scatter.58.cloned.1.call-start = ((), (), s32[]{:S(2)}) async-start(), calls=%async_computation.37 | async-start | bytes 819200 | tf_op jit(solution)/shard_map/reduce_scatter | solution.py:366
  1033.8 68.8 %reduce-scatter.46.cloned.1.call-start = ((), (), s32[]{:S(2)}) async-start(), calls=%async_computation.31 | async-start | bytes 819200 | tf_op jit(solution)/shard_map/reduce_scatter | solution.py:366
  1048.1 224.2 %all-reduce.20.cloned.1.call-start = ((), (), s32[]{:S(2)}) async-start(), calls=%async_computation.47 | async-start | bytes 2621440
  1105.7 173.5 %reduce-scatter.62.cloned.1.call-start = ((), (), s32[]{:S(2)}) async-start(), calls=%async_computation.39 | async-start | bytes 2211840 | tf_op jit(solution)/shard_map/reduce_scatter | solution.py:151
  1115.3 164.0 %reduce-scatter.60.cloned.1.call-start = ((), (), s32[]{:S(2)}) async-start(), calls=%async_computation.38 | async-start | bytes 2211840 | tf_op jit(solution)/shard_map/reduce_scatter | solution.py:142
  1129.9 170.5 %reduce-scatter.68.cloned.1.call-start = ((), (), s32[]{:S(2)}) async-start(), calls=%async_computation.42 | async-start | bytes 5898240 | tf_op jit(solution)/shard_map/reduce_scatter | solution.py:160
  1168.7 189.2 %reduce-scatter.66.cloned.1.call-start = ((), (), s32[]{:S(2)}) async-start(), calls=%async_computation.41 | async-start | bytes 5529600 | tf_op jit(solution)/shard_map/reduce_scatter | solution.py:157
  1216.7 199.3 %reduce-scatter.64.cloned.1.call-start = ((), (), s32[]{:S(2)}) async-start(), calls=%async_computation.40 | async-start | bytes 5529600 | tf_op jit(solution)/shard_map/reduce_scatter | solution.py:154
  1264.2 175.8 %reduce-scatter.76.cloned.1.call-start = ((), (), s32[]{:S(2)}) async-start(), calls=%async_computation.46 | async-start | bytes 102400
  1274.1 192.0 %reduce-scatter.74.cloned.1.call-start = ((), (), s32[]{:S(2)}) async-start(), calls=%async_computation.45 | async-start | bytes 102400
  1279.1 244.7 %all-reduce.22.cloned.1.call-start = ((), (), s32[]{:S(2)}) async-start(), calls=%async_computation.48 | async-start | bytes 2293760
  1300.4 251.9 %reduce-scatter.72.cloned.1.call-start = ((), (), s32[]{:S(2)}) async-start(), calls=%async_computation.44 | async-start | bytes 819200
  1360.1 220.5 %reduce-scatter.70.cloned.1.call-start = ((), (), s32[]{:S(2)}) async-start(), calls=%async_computation.43 | async-start | bytes 819200
  (431 other events, 5726.3 us)
Sparse Core Ops, SparseCore 0:
  19.7 28.2 all-gather.13
  49.6 27.5 all-gather.15
  78.8 58.1 all-gather.17
  138.5 52.1 all-gather.19
  192.2 54.8 all-gather.21
  651.3 26.2 reduce-scatter.35
  697.5 26.2 reduce-scatter.37
  726.7 25.3 reduce-scatter.47
  755.2 25.3 reduce-scatter.49
  789.1 25.3 reduce-scatter.39
  817.7 25.3 reduce-scatter.41
  896.3 25.4 reduce-scatter.51
  924.9 25.3 reduce-scatter.53
  991.6 25.3 reduce-scatter.55
  1020.7 25.2 reduce-scatter.43
  1048.7 25.4 reduce-scatter.57
  1077.2 25.3 reduce-scatter.45
  1105.8 60.2 all-reduce.19
  1168.4 34.4 reduce-scatter.61
  1205.8 33.8 reduce-scatter.59
  1242.0 58.2 reduce-scatter.67
  1302.7 55.1 reduce-scatter.65
  1360.2 55.7 reduce-scatter.63
  1419.2 20.8 reduce-scatter.75
  1443.4 22.6 reduce-scatter.73
  1469.3 54.5 all-reduce.21
  1526.8 25.4 reduce-scatter.71
  1555.1 25.3 reduce-scatter.69
where the time goes:
time: 1600 us; the launch traced here: 1590 us
  matrix products  670 us (42%)
  blocking collectives  360 us (22%)
  waiting for transfers between devices  334 us (21%)
  other arithmetic  143 us (9%)
  local copies, waits for them, and re-layouts  57 us (4%)
  between operations  22.4 us (1%)
    unnamed x34, waiting for transfers between devices  148 us
    reduce_scatter x6, waiting for transfers between devices, micro_pass(): lax.psum_scatter(grad_values_all.astype(jnp.bfloat16), 'seq', scatter_dim...  87.6 us
    all_gather x6, blocking collectives, micro_pass(): lax.all_gather(keys_own, 'seq', axis=0, tiled=True)  84.5 us
    all_gather x6, blocking collectives, micro_pass(): lax.all_gather(values_own, 'seq', axis=0, tiled=True)  80.9 us
    dot_general x6, matrix products, attend_back(): jnp.einsum('qkgd,tkd->kgqt', grad_heads, value_heads, preferred_element_t...  60.8 us
    dot_general x6, matrix products, micro_pass(): jnp.einsum('kgqt,tkd->qkgd', probs.astype(jnp.bfloat16), value_heads, pre...  54 us
    dot_general x6, matrix products, attend_back(): jnp.einsum('kgqt,qkgd->tkd', probs.astype(jnp.bfloat16), grad_heads, pref...  54 us
    reduce_scatter x1, waiting for transfers between devices, reduce_grads(): lax.psum_scatter(up_sum.astype(jnp.bfloat16), 'dp', scatter_dimension=0,...  51.4 us
  transfers between devices with their start and end apart: 28, of which 15 were waited for; matrix products, arithmetic and copies ran while one was open for 35% of the time, Pallas kernels for 0%

commit v1 on v0

v1 whole, which is shorter than its diff:
```python
import functools

import jax
import jax.numpy as jnp
from jax import lax
from jax.experimental import pallas as pl
from jax.experimental.pallas import tpu as pltpu
from jax.sharding import PartitionSpec as P

HEADS = 15
KV_HEADS = 5
HEAD_DIM = 64
RECUR = 3
GROUP = HEADS // KV_HEADS
KW = KV_HEADS * HEAD_DIM
QW = HEADS * HEAD_DIM
LANE = 128
MIB = 2**20

epsilon = 1e-05
rope_base = 10000.0

NN = (((1,), (0,)), ((), ()))
NT = (((1,), (1,)), ((), ()))
BF = jnp.bfloat16
F32 = jnp.float32

vmem = pl.BlockSpec(memory_space=pltpu.VMEM)


def dot(left, right, dims=NN):
    return lax.dot_general(left, right, dims, preferred_element_type=F32)


def ceil_to(size, unit):
    return -(-size // unit) * unit


def shape(dims, dtype):
    return jax.ShapeDtypeStruct(dims, dtype)


def params(limit):
    return pltpu.CompilerParams(vmem_limit_bytes=limit * MIB)


def turn(block, cosine, sine):
    lanes = lax.broadcasted_iota(jnp.int32, block.shape, 1) % HEAD_DIM
    partner = jnp.where(
        lanes < HEAD_DIM // 2,
        pltpu.roll(block, LANE - HEAD_DIM // 2, 1),
        pltpu.roll(block, HEAD_DIM // 2, 1),
    )
    return block * cosine + partner * sine


def norm_back(grad_out, values_in, gain):
    inverse = lax.rsqrt(jnp.mean(values_in * values_in, axis=-1, keepdims=True) + epsilon)
    weighted = grad_out * gain
    inner = jnp.mean(weighted * values_in, axis=-1, keepdims=True)
    grad_gain = jnp.sum(grad_out * values_in * inverse, axis=0, keepdims=True)
    return weighted * inverse - values_in * (inverse * inverse * inverse * inner), grad_gain


def pre_kernel(cols, state, gain, weight, cosine, sine, normed, queries, pair, qbuf, kbuf):
    qc, kc = cols
    values_in = state[...]
    inverse = lax.rsqrt(jnp.mean(values_in * values_in, axis=-1, keepdims=True) + epsilon)
    low = (values_in * inverse * gain[...]).astype(BF)
    normed[...] = low
    for piece in range(weight.shape[0]):
        made = dot(low, weight[piece])
        qbuf[:, piece * qc : (piece + 1) * qc] = made[:, :qc]
        kbuf[:, piece * kc : (piece + 1) * kc] = made[:, qc : qc + kc]
        pair[:, KW + piece * kc : KW + (piece + 1) * kc] = made[:, qc + kc : qc + 2 * kc].astype(BF)
    for buf, out, width, scale in ((qbuf, queries, QW, HEAD_DIM**-0.5), (kbuf, pair, KW, 1.0)):
        for start in range(0, width, LANE):
            stop = min(start + LANE, width)
            turned = turn(buf[:, start : start + LANE], cosine[...], sine[...]) * scale
            out[:, start:stop] = turned[:, : stop - start].astype(BF)


def pre_part(state, gain, weight, cosine, sine, cols):
    tokens, width = state.shape
    return pl.pallas_call(
        functools.partial(pre_kernel, cols),
        out_shape=(
            shape((tokens, width), BF),
            shape((tokens, QW), BF),
            shape((tokens, 2 * KW), BF),
        ),
        in_specs=[vmem] * 5,
        out_specs=(vmem,) * 3,
        scratch_shapes=[
            pltpu.VMEM((tokens, ceil_to(QW, LANE)), F32),
            pltpu.VMEM((tokens, ceil_to(KW, LANE)), F32),
        ],
        compiler_params=params(40),
        name="pre",
    )(state, gain, weight, cosine, sine)


def fill_bias(info, bias, recursion):
    keys, tokens = bias.shape
    columns = info[...].T
    place = lax.broadcasted_iota(jnp.int32, (keys, tokens), 0)
    query = lax.broadcasted_iota(jnp.int32, (keys, tokens), 1)
    apart = place % tokens - place // tokens * tokens - query
    same = columns[:, 0:1] == info[0:1, 0:tokens]
    live = columns[:, 1:2] > recursion
    seen = same & (((apart < 0) & live) | (apart == 0))
    bias[...] = jnp.where(seen, 0.0, -1e30)


def head_cols(head):
    return slice(head * HEAD_DIM, (head + 1) * HEAD_DIM)


def stack_heads(ref, group):
    heads = range(group * GROUP, (group + 1) * GROUP)
    return jnp.concatenate([ref[:, head_cols(head)] for head in heads], axis=0)


def attend_kernel(blocks, recursion, *refs):
    queries, pairs = refs[0], refs[1 : 1 + blocks]
    info, attended, logs, bias = refs[1 + blocks :]
    tokens = queries.shape[0]
    keys = blocks * tokens
    fill_bias(info, bias, recursion)
    logs[...] = jnp.zeros(logs.shape, F32)
    for group in range(KV_HEADS):
        key = jnp.concatenate([ref[:, head_cols(group)] for ref in pairs], axis=0)
        value = jnp.concatenate([ref[:, head_cols(KV_HEADS + group)] for ref in pairs], axis=0)
        value_t = jnp.concatenate([value.T, jnp.ones((16, keys), BF)], axis=0)
        query = stack_heads(queries, group)
        scores = dot(key, query, NT) + jnp.concatenate([bias[...]] * GROUP, axis=1)
        top = jnp.max(scores, axis=0, keepdims=True)
        weights = jnp.exp(scores - top).astype(BF)
        mixed = dot(value_t, weights)
        total = mixed[HEAD_DIM : HEAD_DIM + 1]
        mixed = mixed[:HEAD_DIM] * (1.0 / total)
        log_total = top + jnp.log(total)
        for offset in range(GROUP):
            head = group * GROUP + offset
            span = slice(offset * tokens, (offset + 1) * tokens)
            attended[:, head_cols(head)] = mixed[:, span].T.astype(BF)
            logs[head : head + 1, :] = log_total[:, span]


def attend(queries, pairs, info, recursion):
    tokens = queries.shape[0]
    blocks = len(pairs)
    return pl.pallas_call(
        functools.partial(attend_kernel, blocks, recursion),
        out_shape=(shape((tokens, QW), BF), shape((ceil_to(HEADS, 8), tokens), F32)),
        in_specs=[vmem] * (2 + blocks),
        out_specs=(vmem, vmem),
        scratch_shapes=[pltpu.VMEM((blocks * tokens, tokens), F32)],
        compiler_params=params(40),
        name="attend",
    )(queries, *pairs, info)


def attend_back_kernel(blocks, recursion, *refs):
    queries, pairs = refs[0], refs[1 : 1 + blocks]
    info, attended, logs, grad, grad_queries = refs[1 + blocks : 6 + blocks]
    grad_pairs, bias = refs[6 + blocks : 6 + 2 * blocks], refs[6 + 2 * blocks]
    tokens = queries.shape[0]
    fill_bias(info, bias, recursion)
    product = (attended[...].astype(F32) * grad[...].astype(F32)).T
    for group in range(KV_HEADS):
        key = jnp.concatenate([ref[:, head_cols(group)] for ref in pairs], axis=0)
        value = jnp.concatenate([ref[:, head_cols(KV_HEADS + group)] for ref in pairs], axis=0)
        key_t = key.T
        query = stack_heads(queries, group)
        grad_mixed = stack_heads(grad, group)
        heads = range(group * GROUP, (group + 1) * GROUP)
        delta = jnp.concatenate(
            [jnp.sum(product[head_cols(head)], axis=0, keepdims=True) for head in heads], axis=1
        )
        log_total = jnp.concatenate([logs[head : head + 1, :] for head in heads], axis=1)
        scores = dot(key, query, NT) + jnp.concatenate([bias[...]] * GROUP, axis=1)
        probs = jnp.exp(scores - log_total)
        grad_probs = dot(value, grad_mixed, NT)
        grad_scores = (probs * (grad_probs - delta)).astype(BF)
        grad_value = dot(probs.astype(BF), grad_mixed)
        grad_key = dot(grad_scores, query)
        grad_query = dot(key_t, grad_scores) * HEAD_DIM**-0.5
        for offset, head in enumerate(heads):
            span = slice(offset * tokens, (offset + 1) * tokens)
            grad_queries[:, head_cols(head)] = grad_query[:, span].T
        for block, ref in enumerate(grad_pairs):
            rows = slice(block * tokens, (block + 1) * tokens)
            ref[:, head_cols(group)] = grad_key[rows].astype(ref.dtype)
            ref[:, head_cols(KV_HEADS + group)] = grad_value[rows].astype(ref.dtype)


def attend_back(queries, pairs, info, attended, logs, grad, recursion):
    tokens = queries.shape[0]
    blocks = len(pairs)
    return pl.pallas_call(
        functools.partial(attend_back_kernel, blocks, recursion),
        out_shape=(shape((tokens, QW), F32), shape((tokens, 2 * KW), F32))
        + (shape((tokens, 2 * KW), BF),) * (blocks - 1),
        in_specs=[vmem] * (5 + blocks),
        out_specs=(vmem,) * (1 + blocks),
        scratch_shapes=[pltpu.VMEM((blocks * tokens, tokens), F32)],
        compiler_params=params(48),
        name="attend_back",
    )(queries, *pairs, info, attended, logs, grad)


def post_kernel(
    shift, state, attended, out_w, gain, router, active, gate_w, up_w, down_w,
    state_out, normed, gate_out, up_out, hidden_out, midway_out, update_out, routed,
    branch, total,
):
    pieces, cols = down_w.shape[0], down_w.shape[2]
    step = pl.program_id(0)

    @pl.when(step == 0)
    def _():
        for piece in range(pieces):
            made = dot(attended[...], out_w[piece])
            branch[:, piece * cols : (piece + 1) * cols] = made[:, shift : shift + cols]
        midway = state[...] + branch[...]
        midway_out[...] = midway
        inverse = lax.rsqrt(jnp.mean(midway * midway, axis=-1, keepdims=True) + epsilon)
        normed[...] = (midway * inverse * gain[...]).astype(BF)
        total[...] = jnp.zeros(total.shape, F32)

    low = normed[...]
    gate = dot(low, gate_w[0])
    up = dot(low, up_w[0])
    gate_out[0] = gate.astype(BF)
    up_out[0] = up.astype(BF)
    hidden = (gate / (1.0 + jnp.exp(-gate)) * up).astype(BF)
    hidden_out[0] = hidden
    for piece in range(pieces):
        total[piece] += dot(hidden, down_w[piece])

    @pl.when(step == pl.num_programs(0) - 1)
    def _():
        for piece in range(pieces):
            span = slice(piece * cols, (piece + 1) * cols)
            branch[:, span] = branch[:, span] + total[piece]
        update = branch[...]
        update_out[...] = update
        before = state[...]
        chance = 1.0 / (1.0 + jnp.exp(-jnp.sum(before * router[...], axis=-1, keepdims=True)))
        routed[...] = jnp.broadcast_to(chance, routed.shape)
        state_out[...] = before + (active[:, 0:1] * chance) * update


def post_part(state, attended, out_w, gain, router, active, gate_w, up_w, down_w, shift):
    tokens, width = state.shape
    pieces, _, part = gate_w.shape
    cols = down_w.shape[2]

    def whole(*dims):
        return pl.BlockSpec(dims, lambda f: (0,) * len(dims))

    chunk = pl.BlockSpec((1, tokens, part), lambda f: (f, 0, 0))
    weight = pl.BlockSpec((1, width, part), lambda f: (f, 0, 0))
    row = whole(tokens, width)
    return pl.pallas_call(
        functools.partial(post_kernel, shift),
        grid=(pieces,),
        out_shape=(
            shape((tokens, width), F32),
            shape((tokens, width), BF),
            shape((pieces, tokens, part), BF),
            shape((pieces, tokens, part), BF),
            shape((pieces, tokens, part), BF),
            shape((tokens, width), F32),
            shape((tokens, width), F32),
            shape((tokens, LANE), F32),
        ),
        in_specs=[
            row, whole(tokens, QW), whole(*out_w.shape), whole(1, width), whole(1, width),
            whole(tokens, LANE), weight, weight,
            pl.BlockSpec((pieces, part, cols), lambda f: (0, f, 0)),
        ],
        out_specs=(row, row, chunk, chunk, chunk, row, row, whole(tokens, LANE)),
        scratch_shapes=[pltpu.VMEM((tokens, width), F32), pltpu.VMEM((pieces, tokens, cols), F32)],
        compiler_params=params(48),
        name="post",
    )(state, attended, out_w, gain, router, active, gate_w, up_w, down_w)


def post_back_kernel(
    shift, grad_state, update, routed, active, state, midway, gain, router, out_w, gate_pre, up_pre,
    gate_w, up_w, down_w,
    grad_ffn, grad_gate_out, grad_up_out, grad_branch, grad_attended, partial, gain_grad, router_grad,
    total, scaled, logit,
):
    pieces, cols = down_w.shape[0], down_w.shape[2]
    step = pl.program_id(0)

    @pl.when(step == 0)
    def _():
        chance = routed[:, 0:1]
        weight = active[:, 0:1] * chance
        grad = grad_state[...]
        change = grad * weight
        scaled[...] = change
        slope = jnp.sum(grad * update[...], axis=-1, keepdims=True) * weight * (1.0 - chance)
        logit[...] = jnp.broadcast_to(slope, logit.shape)
        router_grad[...] = jnp.sum(state[...] * slope, axis=0, keepdims=True)
        low = change.astype(BF)
        for piece in range(pieces):
            grad_ffn[piece] = low[:, piece * cols : (piece + 1) * cols]
        total[...] = jnp.zeros(total.shape, F32)

    grad_hidden = dot(grad_ffn[0], down_w[0], NT)
    for piece in range(1, pieces):
        grad_hidden += dot(grad_ffn[piece], down_w[piece], NT)
    gate = gate_pre[0].astype(F32)
    chance = 1.0 / (1.0 + jnp.exp(-gate))
    smooth = gate * chance
    grad_gate = (grad_hidden * up_pre[0].astype(F32) * (chance + smooth * (1.0 - chance))).astype(BF)
    grad_up = (grad_hidden * smooth).astype(BF)
    grad_gate_out[0] = grad_gate
    grad_up_out[0] = grad_up
    total[...] += dot(grad_gate, gate_w[0], NT) + dot(grad_up, up_w[0], NT)

    @pl.when(step == pl.num_programs(0) - 1)
    def _():
        grad_midway, grad_gain = norm_back(total[...], midway[...], gain[...])
        gain_grad[...] = grad_gain
        partial[...] = grad_state[...] + logit[:, 0:1] * router[...] + grad_midway
        low = (scaled[...] + grad_midway).astype(BF)
        grad = None
        for piece in range(pieces):
            if grad_branch.shape[2] > cols:
                grad_branch[piece] = jnp.zeros(grad_branch.shape[1:], BF)
            grad_branch[piece, :, shift : shift + cols] = low[:, piece * cols : (piece + 1) * cols]
            made = dot(grad_branch[piece], out_w[piece], NT)
            grad = made if grad is None else grad + made
        grad_attended[...] = grad.astype(BF)


def post_back(
    grad_state, update, routed, active, state, midway, gain, router, out_w, gate_pre, up_pre,
    gate_w, up_w, down_w, shift,
):
    tokens, width = state.shape
    pieces, _, part = gate_w.shape
    cols = down_w.shape[2]

    def whole(*dims):
        return pl.BlockSpec(dims, lambda f: (0,) * len(dims))

    chunk = pl.BlockSpec((1, tokens, part), lambda f: (f, 0, 0))
    weight = pl.BlockSpec((1, width, part), lambda f: (f, 0, 0))
    row, thin, line = whole(tokens, width), whole(tokens, LANE), whole(1, width)
    branch_dims = (pieces, tokens, out_w.shape[2])
    return pl.pallas_call(
        functools.partial(post_back_kernel, shift),
        grid=(pieces,),
        out_shape=(
            shape((pieces, tokens, cols), BF),
            shape((pieces, tokens, part), BF),
            shape((pieces, tokens, part), BF),
            shape(branch_dims, BF),
            shape((tokens, QW), BF),
            shape((tokens, width), F32),
            shape((1, width), F32),
            shape((1, width), F32),
        ),
        in_specs=[
            row, row, thin, thin, row, row, line, line, whole(*out_w.shape), chunk, chunk,
            weight, weight, pl.BlockSpec((pieces, part, cols), lambda f: (0, f, 0)),
        ],
        out_specs=(
            whole(pieces, tokens, cols), chunk, chunk, whole(*branch_dims), whole(tokens, QW),
            row, line, line,
        ),
        scratch_shapes=[
            pltpu.VMEM((tokens, width), F32),
            pltpu.VMEM((tokens, width), F32),
            pltpu.VMEM((tokens, LANE), F32),
        ],
        compiler_params=params(48),
        name="post_back",
    )(grad_state, update, routed, active, state, midway, gain, router, out_w, gate_pre, up_pre,
      gate_w, up_w, down_w)


def pre_back_kernel(cols, blocks, *refs):
    qc, kc = cols
    grad_queries, own, others = refs[0], refs[1], refs[2 : 1 + blocks]
    partial, state, gain, weight, cosine, sine = refs[1 + blocks : 7 + blocks]
    packed, grad_state, gain_grad, qbuf, kbuf = refs[7 + blocks :]
    summed = own[...]
    for ref in others:
        summed = summed + ref[...].astype(F32)
    kbuf[:, :KW] = summed[:, :KW]
    qbuf[:, :QW] = grad_queries[...]
    for buf in (qbuf, kbuf):
        for start in range(0, buf.shape[1], LANE):
            span = slice(start, start + LANE)
            buf[:, span] = turn(buf[:, span], cosine[...], -sine[...])
    low_q = qbuf[...].astype(BF)
    low_k = kbuf[...].astype(BF)
    low_v = summed[:, KW:].astype(BF)
    total = None
    for piece in range(weight.shape[0]):
        packed[piece] = jnp.zeros(packed.shape[1:], BF)
        packed[piece, :, :qc] = low_q[:, piece * qc : (piece + 1) * qc]
        packed[piece, :, qc : qc + kc] = low_k[:, piece * kc : (piece + 1) * kc]
        packed[piece, :, qc + kc : qc + 2 * kc] = low_v[:, piece * kc : (piece + 1) * kc]
        made = dot(packed[piece], weight[piece], NT)
        total = made if total is None else total + made
    grad_in, grad_gain = norm_back(total, state[...], gain[...])
    gain_grad[...] = grad_gain
    grad_state[...] = partial[...] + grad_in


def pre_back(grad_queries, grad_pairs, partial, state, gain, weight, cosine, sine, cols):
    tokens, width = state.shape
    return pl.pallas_call(
        functools.partial(pre_back_kernel, cols, len(grad_pairs)),
        out_shape=(
            shape((weight.shape[0], tokens, weight.shape[2]), BF),
            shape((tokens, width), F32),
            shape((1, width), F32),
        ),
        in_specs=[vmem] * (7 + len(grad_pairs)),
        out_specs=(vmem,) * 3,
        scratch_shapes=[
            pltpu.VMEM((tokens, ceil_to(QW, LANE)), F32),
            pltpu.VMEM((tokens, ceil_to(KW, LANE)), F32),
        ],
        compiler_params=params(40),
        name="pre_back",
    )(grad_queries, *grad_pairs, partial, state, gain, weight, cosine, sine)


def attn_sums_kernel(count, low_col, *refs):
    normed, packed = refs[:count], refs[count : 2 * count]
    attended, branch = refs[2 * count : 3 * count], refs[3 * count : 4 * count]
    out, left, right = refs[4 * count :]

    @pl.when(pl.program_id(0) == 0)
    def _():
        left[...] = jnp.concatenate([ref[...].T for ref in normed], axis=1)
        right[...] = jnp.concatenate([ref[...].T for ref in attended], axis=1)

    first = dot(left[...], jnp.concatenate([ref[0] for ref in packed], axis=0))
    second = dot(right[...], jnp.concatenate([ref[0] for ref in branch], axis=0))
    high_col = first.shape[1]
    if low_col:
        out[0, :, :low_col] = first[:, :low_col].astype(BF)
    out[0, :, low_col:high_col] = (first[:, low_col:] + second[:, : high_col - low_col]).astype(BF)
    if high_col < out.shape[2]:
        out[0, :, high_col:] = second[:, high_col - low_col :].astype(BF)


def attn_sums(normed, packed, attended, branch, low_col, total_cols):
    count = len(normed)
    tokens, width = normed[0].shape
    pieces = packed[0].shape[0]
    row = pl.BlockSpec((tokens, width), lambda s: (0, 0))
    part = pl.BlockSpec((1, tokens, packed[0].shape[2]), lambda s: (s, 0, 0))
    thin = pl.BlockSpec((1, tokens, branch[0].shape[2]), lambda s: (s, 0, 0))
    return pl.pallas_call(
        functools.partial(attn_sums_kernel, count, low_col),
        grid=(pieces,),
        out_shape=shape((pieces, width, total_cols), BF),
        in_specs=[row] * count + [part] * count + [row] * count + [thin] * count,
        out_specs=pl.BlockSpec((1, width, total_cols), lambda s: (s, 0, 0)),
        scratch_shapes=[pltpu.VMEM((width, count * tokens), BF)] * 2,
        compiler_params=params(56),
        name="attn_sums",
    )(*normed, *packed, *attended, *branch)


def pair_sums_kernel(count, *refs):
    normed, first, second = refs[:count], refs[count : 2 * count], refs[2 * count : 3 * count]
    first_out, second_out, left = refs[3 * count :]

    @pl.when(pl.program_id(0) == 0)
    def _():
        left[...] = jnp.concatenate([ref[...].T for ref in normed], axis=1)

    for source, out in ((first, first_out), (second, second_out)):
        out[0] = dot(left[...], jnp.concatenate([ref[0] for ref in source], axis=0)).astype(BF)


def pair_sums(normed, first, second):
    count = len(normed)
    tokens, width = normed[0].shape
    pieces, _, part = first[0].shape
    row = pl.BlockSpec((tokens, width), lambda s: (0, 0))
    chunk = pl.BlockSpec((1, tokens, part), lambda s: (s, 0, 0))
    result = pl.BlockSpec((1, width, part), lambda s: (s, 0, 0))
    return pl.pallas_call(
        functools.partial(pair_sums_kernel, count),
        grid=(pieces,),
        out_shape=(shape((pieces, width, part), BF),) * 2,
        in_specs=[row] * count + [chunk] * (2 * count),
        out_specs=(result, result),
        scratch_shapes=[pltpu.VMEM((width, count * tokens), BF)],
        compiler_params=params(56),
        name="pair_sums",
    )(*normed, *first, *second)


def down_sums_kernel(count, *refs):
    hidden, grads, out, right = refs[:count], refs[count : 2 * count], refs[-2], refs[-1]

    @pl.when(pl.program_id(0) == 0)
    def _():
        for piece in range(out.shape[0]):
            right[piece] = jnp.concatenate([ref[piece] for ref in grads], axis=0)

    left = jnp.concatenate([ref[0].T for ref in hidden], axis=1)
    for piece in range(out.shape[0]):
        out[piece] = dot(left, right[piece]).astype(BF)


def down_sums(hidden, grads):
    count = len(hidden)
    pieces, tokens, part = hidden[0].shape
    cols = grads[0].shape[2]
    return pl.pallas_call(
        functools.partial(down_sums_kernel, count),
        grid=(pieces,),
        out_shape=shape((pieces, pieces * part, cols), BF),
        in_specs=[pl.BlockSpec((1, tokens, part), lambda f: (f, 0, 0))] * count
        + [pl.BlockSpec((pieces, tokens, cols), lambda f: (0, 0, 0))] * count,
        out_specs=pl.BlockSpec((pieces, part, cols), lambda f: (0, f, 0)),
        scratch_shapes=[pltpu.VMEM((pieces, count * tokens, cols), BF)],
        compiler_params=params(56),
        name="down_sums",
    )(*hidden, *grads)


def rope_tables(tokens):
    half = HEAD_DIM // 2
    frequency = rope_base ** (-(jnp.arange(half, dtype=F32) * 2.0 / HEAD_DIM))
    positions = lax.axis_index("seq") * tokens + jnp.arange(tokens, dtype=jnp.int32)
    angles = positions.astype(F32)[:, None] * frequency[None, :]
    cosine, sine = jnp.cos(angles), jnp.sin(angles)
    repeat = LANE // HEAD_DIM
    return (
        jnp.concatenate([cosine, cosine] * repeat, axis=1),
        jnp.concatenate([-sine, sine] * repeat, axis=1),
    )


def pass_on(array, step, count):
    return lax.ppermute(array, "seq", [(i, i + step) for i in range(count - step)])


def pass_back(array, step, count):
    return lax.ppermute(array, "seq", [(i + step, i) for i in range(count - step)])


def local(
    inputs, cotangent, segments, depths, query_weight, key_weight, value_weight, out_weight,
    gate_weight, up_weight, down_weight, attn_gain, ffn_gain, router_weight,
):
    micros, _, tokens, width = inputs.shape
    seq = lax.axis_size("seq")
    mine = lax.axis_index("seq")
    rows = query_weight.shape[0]
    qc, kc = query_weight.shape[1], key_weight.shape[1]
    cols = (qc, kc)

    attn_local = jnp.concatenate([query_weight, key_weight, value_weight, out_weight], axis=1)
    both = ("seq", "dp")

    def gather(local_part):
        full = lax.all_gather(local_part, both, axis=0, tiled=False)
        return full.reshape(seq, -1, full.shape[-1])

    attn_w = gather(attn_local)
    gate_w, up_w, down_w = gather(gate_weight), gather(up_weight), gather(down_weight)
    small = jnp.concatenate([attn_gain[:, None], ffn_gain[:, None], router_weight], axis=1)
    small = lax.all_gather(small, "dp", axis=0, tiled=True).astype(F32).T
    attn_g, ffn_g = small[0:1], small[1:2]
    routers = [small[2 + r : 3 + r] for r in range(RECUR)]
    used = qc + 2 * kc
    total_cols = attn_w.shape[2]
    high_col = min(ceil_to(used, LANE), total_cols)
    low_col = used // LANE * LANE
    shift = used - low_col
    qkv_w, out_w = attn_w[:, :, :high_col], attn_w[:, :, low_col:]

    marks = jnp.stack([segments[:, 0], depths[:, 0]], axis=1)
    marks = lax.all_gather(marks, "seq", axis=0, tiled=False).astype(F32)
    order = mine - jnp.arange(seq)
    marks = jnp.where((order >= 0)[:, None, None, None], marks[order % seq], -1.0)
    marks = marks.transpose(1, 2, 0, 3).reshape(micros, 2, seq * tokens)
    infos = [jnp.pad(marks[m], ((0, 6), (0, 0))) for m in range(micros)]
    cosine, sine = rope_tables(tokens)

    states = [inputs[m, 0] for m in range(micros)]
    actives = [
        [
            jnp.broadcast_to((depths[m, 0] > r).astype(F32)[:, None], (tokens, LANE))
            for r in range(RECUR)
        ]
        for m in range(micros)
    ]
    saved = [[None] * RECUR for _ in range(micros)]
    for r in range(RECUR):
        made = []
        for m in range(micros):
            normed, queries, pair = pre_part(states[m], attn_g, qkv_w, cosine, sine, cols)
            pairs = [pair] + [pass_on(pair, step, seq) for step in range(1, seq)]
            made.append((normed, queries, pairs))
        for m in range(micros):
            normed, queries, pairs = made[m]
            attended, logs = attend(queries, pairs, infos[m], r)
            state_out, ffn_in, gate, up, hidden, midway, update, routed = post_part(
                states[m], attended, out_w, ffn_g, routers[r], actives[m][r], gate_w, up_w, down_w, shift
            )
            saved[m][r] = dict(
                state=states[m], normed=normed, queries=queries, pairs=pairs, attended=attended,
                logs=logs, ffn_in=ffn_in, gate=gate, up=up, hidden=hidden, midway=midway,
                update=update, routed=routed,
            )
            states[m] = state_out

    grads = [cotangent[m, 0] for m in range(micros)]
    attn_gain_sum, ffn_gain_sum, router_sums = 0.0, 0.0, [0.0] * RECUR
    for r in reversed(range(RECUR)):
        partials = []
        for m in range(micros):
            s = saved[m][r]
            grad_ffn, grad_gate, grad_up, grad_branch, grad_attended, partial, gain_grad, router_grad = (
                post_back(
                    grads[m], s["update"], s["routed"], actives[m][r], s["state"], s["midway"], ffn_g,
                    routers[r], out_w, s["gate"], s["up"], gate_w, up_w, down_w, shift,
                )
            )
            ffn_gain_sum = ffn_gain_sum + gain_grad
            router_sums[r] = router_sums[r] + router_grad
            s.update(grad_ffn=grad_ffn, grad_gate=grad_gate, grad_up=grad_up, grad_branch=grad_branch)
            grad_queries, *grad_pairs = attend_back(
                s["queries"], s["pairs"], infos[m], s["attended"], s["logs"], grad_attended, r
            )
            grad_pairs = [grad_pairs[0]] + [
                pass_back(grad_pairs[step], step, seq) for step in range(1, seq)
            ]
            partials.append((partial, grad_queries, grad_pairs))
        for m in range(micros):
            s = saved[m][r]
            partial, grad_queries, grad_pairs = partials[m]
            packed, grads[m], gain_grad = pre_back(
                grad_queries, grad_pairs, partial, s["state"], attn_g, qkv_w, cosine, sine, cols
            )
            attn_gain_sum = attn_gain_sum + gain_grad
            s.update(packed=packed)

    flat = [saved[m][r] for r in reversed(range(RECUR)) for m in range(micros)]

    def every(name):
        return [s[name] for s in flat]

    down_sum = down_sums(every("hidden"), every("grad_ffn"))
    gate_sum, up_sum = pair_sums(every("ffn_in"), every("grad_gate"), every("grad_up"))
    attn_sum = attn_sums(
        every("normed"), every("packed"), every("attended"), every("grad_branch"), low_col, total_cols
    )

    def reduce(partial):
        partial = partial.reshape(seq, lax.axis_size("dp"), -1, partial.shape[-1])
        part = lax.psum_scatter(partial, "seq", scatter_dimension=0, tiled=False)
        return lax.psum_scatter(part, "dp", scatter_dimension=0, tiled=False).astype(F32)

    down_grad, gate_grad, up_grad, attn_grad = (
        reduce(partial) for partial in (down_sum, gate_sum, up_sum, attn_sum)
    )
    small_sum = jnp.concatenate([attn_gain_sum, ffn_gain_sum, *router_sums], axis=0)
    small_sum = lax.psum(small_sum, both)
    small_own = lax.dynamic_slice_in_dim(small_sum, lax.axis_index("dp") * rows, rows, axis=1)

    outputs = jnp.stack(states, axis=0)[:, None]
    input_grad = jnp.stack(grads, axis=0)[:, None]
    return (
        outputs,
        input_grad,
        attn_grad[:, :qc],
        attn_grad[:, qc : qc + kc],
        attn_grad[:, qc + kc : used],
        attn_grad[:, used:],
        gate_grad,
        up_grad,
        down_grad,
        small_own[0],
        small_own[1],
        small_own[2:].T,
    )


def solution(mesh):
    data = P(None, "dp", "seq", None)
    marks = P(None, "dp", "seq")
    weight = P("dp", "seq")
    in_specs = (data, data, marks, marks) + (weight,) * 7 + (P("dp"), P("dp"), P("dp", None))
    out_specs = (data, data) + (weight,) * 7 + (P("dp"), P("dp"), P("dp", None))
    return jax.shard_map(local, mesh=mesh, in_specs=in_specs, out_specs=out_specs, check_vma=False)
```

time: 1600 us -> 1140 us (0.71)
  matrix products: 670 us -> 0 us
  Pallas kernels: 0 us -> 367 us
  blocking collectives: 360 us -> 62.3 us
  waiting for transfers between devices: 334 us -> 484 us
  other arithmetic: 143 us -> 14.2 us
  local copies, waits for them, and re-layouts: 57 us -> 119 us
  starting transfers between devices: 3.23 us -> 65.2 us
    dot_general x162 -> x0, matrix products: 670 us -> none  [the longest x6 60.8 us: attend_back(): jnp.einsum('qkgd,tkd->kgqt', grad_heads, value_heads, preferred_element_t...]
    pallas_call x0 -> x39, Pallas kernels: none -> 367 us  [the longest x6 94 us: post_back(): pl.pallas_call(functools.partial(post_back_kernel, shift), grid=(pieces,)...]
    all_gather x26 -> x2, blocking collectives: 307 us -> 22.5 us  [the longest x1 12.9 us: local(): small = lax.all_gather(small, 'dp', axis=0, tiled=True).astype(F32).T]
    all_gather x5 -> x4, waiting for transfers between devices: 0.01 us -> 202 us  [gather(): full = lax.all_gather(local_part, both, axis=0, tiled=False)]
    reduce_scatter x17 -> x1, waiting for transfers between devices: 185 us -> 32.1 us  [reduce(): lax.psum_scatter(part, 'dp', scatter_dimension=0, tiled=False).astype(F32)]
    unnamed x34 -> x19, waiting for transfers between devices: 148 us -> 220 us
    ppermute x0 -> x36, starting transfers between devices: none -> 64.7 us  [the longest x18 40.5 us: pass_on(): lax.ppermute(array, 'seq', [(i, i + step) for i in range(count - step)])]
    unnamed x887 -> x420, local copies, waits for them, and re-layouts: 47.3 us -> 105 us
  transfers between devices with their start and end apart: 28 -> 48, of which waited for: 15 -> 13; matrix products, arithmetic and copies ran while one was open for 35% -> 3% of each run, Pallas kernels for 0% -> 29%
where the time goes in v1:
time: 1140 us; the launch traced here: 1130 us
  waiting for transfers between devices  484 us (42%)
  Pallas kernels  367 us (32%)
  local copies, waits for them, and re-layouts  119 us (10%)
  starting transfers between devices  65.2 us (6%)
  blocking collectives  62.3 us (5%)
  between operations  16.7 us (1%)
  other arithmetic  14.2 us (1%)
    unnamed x19, waiting for transfers between devices  220 us
    all_gather x4, waiting for transfers between devices, gather(): full = lax.all_gather(local_part, both, axis=0, tiled=False)  202 us
    unnamed x420, local copies, waits for them, and re-layouts  105 us
    pallas_call x6, Pallas kernels, post_back(): pl.pallas_call(functools.partial(post_back_kernel, shift), grid=(pieces,)...  94 us
    pallas_call x6, Pallas kernels, post_part(): pl.pallas_call(functools.partial(post_kernel, shift), grid=(pieces,), out...  74.7 us
    pallas_call x6, Pallas kernels, attend_back(): pl.pallas_call(functools.partial(attend_back_kernel, blocks, recursion),...  69.7 us
    pallas_call x6, Pallas kernels, attend(): pl.pallas_call(functools.partial(attend_kernel, blocks, recursion), out_s...  42.2 us
    ppermute x18, starting transfers between devices, pass_on(): lax.ppermute(array, 'seq', [(i, i + step) for i in range(count - step)])  40.5 us
  transfers between devices with their start and end apart: 48, of which 13 were waited for; matrix products, arithmetic and copies ran while one was open for 3% of the time, Pallas kernels for 29%

profile of v1, /device:TPU:0, one launch (start us, length us, event | category | flops | bytes accessed | tf_op | source)
XLA Modules:
  0.0 1128.6 jit_solution(15196193752404068876)
XLA Ops:
  23.7 12.9 %all-gather.5 = bf16[8,120,5]{1,2,0:T(8,128)(2,1)S(1)} all-gather(bf16[1,120,5]{1,2,0:T(8,128)(2,1)S(1)} %maximum_bitcast_fusion.2), channel_id=1, replica_groups=mesh['dp'=8,'seq'=4] {'dp'}, dimensions={0}, use_global_device_ids=true | all-gather | bytes 10800 | tf_op jit(solution)/shard_map/all_gather | solution.py:582
  42.4 36.1 %all-gather.11.cloned.1.call-done = bf16[3840,640]{1,0:T(8,128)(2,1)} async-done(((bf16[120,640]{1,0:T(8,128)(2,1)}), bf16[3840,640]{1,0:T(8,128)(2,1)}) %all-gather.11.cloned.1.call-update) | async-done | bytes 4915216 | tf_op jit(solution)/shard_map/all_gather | solution.py:576
  119.7 33.1 %all-gather.13.cloned.1.call-done = bf16[3840,640]{1,0:T(8,128)(2,1)} async-done(((bf16[120,640]{1,0:T(8,128)(2,1)}), bf16[3840,640]{1,0:T(8,128)(2,1)}) %all-gather.13.cloned.1.call-update) | async-done | bytes 4915216 | tf_op jit(solution)/shard_map/all_gather | solution.py:576
  152.8 66.1 %all-gather.15.cloned.1.call-done = bf16[3840,640]{1,0:T(8,128)(2,1)} async-done(((bf16[120,640]{1,0:T(8,128)(2,1)}), bf16[3840,640]{1,0:T(8,128)(2,1)}) %all-gather.15.cloned.1.call-update) | async-done | bytes 4915216 | tf_op jit(solution)/shard_map/all_gather | solution.py:576
  218.8 66.9 %all-gather.17.cloned.1.call-done = bf16[10240,240]{1,0:T(8,128)(2,1)} async-done(((bf16[320,240]{1,0:T(8,128)(2,1)}), bf16[10240,240]{1,0:T(8,128)(2,1)}) %all-gather.17.cloned.1.call-update) | async-done | bytes 4915216 | tf_op jit(solution)/shard_map/all_gather | solution.py:576
  287.0 12.5 %post.6 = (f32[256,960]{1,0:T(8,128)S(1)}, bf16[256,960]{1,0:T(8,128)(2,1)S(1)}, bf16[4,256,640]{2,1,0:T(8,128)(2,1)}, bf16[4,256,640]{2,1,0:T(8,128)(2,1)}, bf1...) custom-call(f32[256,960]{1,0:T(8,128)S(1)} %bitcast.65, ...), custom_call_target="tpu_custom_call" | custom-call | tf_op jit(solution)/shard_map/post/pallas_call | solution.py:266
  317.7 12.5 %post.9 = (f32[256,960]{1,0:T(8,128)S(1)}, bf16[256,960]{1,0:T(8,128)(2,1)S(1)}, bf16[4,256,640]{2,1,0:T(8,128)(2,1)}, bf16[4,256,640]{2,1,0:T(8,128)(2,1)}, bf1...) custom-call(f32[256,960]{1,0:T(8,128)S(1)} %bitcast.69, ...), custom_call_target="tpu_custom_call" | custom-call | tf_op jit(solution)/shard_map/post/pallas_call | solution.py:266
  344.5 12.5 %post.7 = (f32[256,960]{1,0:T(8,128)S(1)}, bf16[256,960]{1,0:T(8,128)(2,1)S(1)}, bf16[4,256,640]{2,1,0:T(8,128)(2,1)}, bf16[4,256,640]{2,1,0:T(8,128)(2,1)}, bf1...) custom-call(f32[256,960]{1,0:T(8,128)S(1)} %get-tuple-element.191.state.ref, ...), custom_call_target="tpu_custom_call" | custom-call | tf_op jit(solution)/shard_map/post/pallas_call | solution.py:266
  374.1 12.5 %post.10 = (f32[256,960]{1,0:T(8,128)S(1)}, bf16[256,960]{1,0:T(8,128)(2,1)S(1)}, bf16[4,256,640]{2,1,0:T(8,128)(2,1)}, bf16[4,256,640]{2,1,0:T(8,128)(2,1)}, bf...) custom-call(f32[256,960]{1,0:T(8,128)S(1)} %get-tuple-element.203.state.re, ...), custom_call_target="tpu_custom_call" | custom-call | tf_op jit(solution)/shard_map/post/pallas_call | solution.py:266
  408.6 12.4 %post.8 = (f32[256,960]{1,0:T(8,128)S(1)}, bf16[256,960]{1,0:T(8,128)(2,1)S(1)}, bf16[4,256,640]{2,1,0:T(8,128)(2,1)}, bf16[4,256,640]{2,1,0:T(8,128)(2,1)}, bf1...) custom-call(f32[256,960]{1,0:T(8,128)S(1)} %copy-done.10, ...), custom_call_target="tpu_custom_call" | custom-call | tf_op jit(solution)/shard_map/post/pallas_call | solution.py:266
  423.8 15.6 %post_back.6 = (bf16[4,256,240]{2,1,0:T(8,128)(2,1)S(1)}, bf16[4,256,640]{2,1,0:T(8,128)(2,1)}, bf16[4,256,640]{2,1,0:T(8,128)(2,1)}, bf16[4,256,256]{2,1,0:T(8,...) custom-call(f32[256,960]{1,0:T(8,128)S(1)} %bitcast.72, ...), custom_call_target="tpu_custom_call" | custom-call | tf_op jit(solution)/shard_map/post_back/pallas_call | solution.py:358
  442.0 12.0 %attend_back.6 = (f32[256,960]{1,0:T(8,128)S(1)}, f32[256,640]{1,0:T(8,128)S(1)}, bf16[256,640]{1,0:T(8,128)(2,1)}, bf16[256,640]{1,0:T(8,128)(2,1)}, bf16[256,640]{1,0:T(8,128)(2,1)}) custom-call(bf16[256,960]{1,0:T(8,128)(2,1)S(1)} %copy-done.39, bf16[256,640]{1,0:T(8,128)(2,1)} %get-tuple-element.197.refs_1_, ...), custom_call_target="tpu_custom_call" | custom-call | tf_op jit(solution)/shard_map/attend_back/pallas_call | solution.py:201
  471.4 12.5 %post.11 = (f32[256,960]{1,0:T(8,128)S(1)}, bf16[256,960]{1,0:T(8,128)(2,1)S(1)}, bf16[4,256,640]{2,1,0:T(8,128)(2,1)}, bf16[4,256,640]{2,1,0:T(8,128)(2,1)}, bf...) custom-call(f32[256,960]{1,0:T(8,128)S(1)} %copy-done.8, ...), custom_call_target="tpu_custom_call" | custom-call | tf_op jit(solution)/shard_map/post/pallas_call | solution.py:266
  488.9 15.7 %post_back.9 = (bf16[4,256,240]{2,1,0:T(8,128)(2,1)S(1)}, bf16[4,256,640]{2,1,0:T(8,128)(2,1)}, bf16[4,256,640]{2,1,0:T(8,128)(2,1)}, bf16[4,256,256]{2,1,0:T(8,...) custom-call(f32[256,960]{1,0:T(8,128)S(1)} %bitcast.73, ...), custom_call_target="tpu_custom_call" | custom-call | tf_op jit(solution)/shard_map/post_back/pallas_call | solution.py:358
  509.0 12.1 %attend_back.9 = (f32[256,960]{1,0:T(8,128)S(1)}, f32[256,640]{1,0:T(8,128)S(1)}, bf16[256,640]{1,0:T(8,128)(2,1)}, bf16[256,640]{1,0:T(8,128)(2,1)}, bf16[256,640]{1,0:T(8,128)(2,1)}) custom-call(bf16[256,960]{1,0:T(8,128)(2,1)S(1)} %copy-done.36, bf16[256,640]{1,0:T(8,128)(2,1)} %get-tuple-element.209.refs_1_, ...), custom_call_target="tpu_custom_call" | custom-call | tf_op jit(solution)/shard_map/attend_back/pallas_call | solution.py:201
  538.3 15.9 %post_back.7 = (bf16[4,256,240]{2,1,0:T(8,128)(2,1)S(1)}, bf16[4,256,640]{2,1,0:T(8,128)(2,1)}, bf16[4,256,640]{2,1,0:T(8,128)(2,1)}, bf16[4,256,256]{2,1,0:T(8,...) custom-call(f32[256,960]{1,0:T(8,128)S(1)} %copy-done.90, ...), custom_call_target="tpu_custom_call" | custom-call | tf_op jit(solution)/shard_map/post_back/pallas_call | solution.py:358
  587.6 15.6 %post_back.10 = (bf16[4,256,240]{2,1,0:T(8,128)(2,1)S(1)}, bf16[4,256,640]{2,1,0:T(8,128)(2,1)}, bf16[4,256,640]{2,1,0:T(8,128)(2,1)}, bf16[4,256,256]{2,1,0:T(8...) custom-call(f32[256,960]{1,0:T(8,128)S(1)} %copy-done.88, ...), custom_call_target="tpu_custom_call" | custom-call | tf_op jit(solution)/shard_map/post_back/pallas_call | solution.py:358
  635.4 15.8 %post_back.8 = (bf16[4,256,240]{2,1,0:T(8,128)(2,1)S(1)}, bf16[4,256,640]{2,1,0:T(8,128)(2,1)}, bf16[4,256,640]{2,1,0:T(8,128)(2,1)}, bf16[4,256,256]{2,1,0:T(8,...) custom-call(f32[256,960]{1,0:T(8,128)S(1)} %copy-done.92, ...), custom_call_target="tpu_custom_call" | custom-call | tf_op jit(solution)/shard_map/post_back/pallas_call | solution.py:358
  659.8 15.3 %post_back.11 = (bf16[4,256,240]{2,1,0:T(8,128)(2,1)S(1)}, bf16[4,256,640]{2,1,0:T(8,128)(2,1)}, bf16[4,256,640]{2,1,0:T(8,128)(2,1)}, bf16[4,256,256]{2,1,0:T(8...) custom-call(f32[256,960]{1,0:T(8,128)S(1)} %get-tuple-element.282.gr, ...), custom_call_target="tpu_custom_call" | custom-call | tf_op jit(solution)/shard_map/post_back/pallas_call | solution.py:358
  678.3 24.7 %pair_sums.1 = (bf16[4,960,640]{2,1,0:T(8,128)(2,1)}, bf16[4,960,640]{2,1,0:T(8,128)(2,1)}) custom-call(bf16[256,960]{1,0:T(8,128)(2,1)} %copy-done.145, bf16[256,960]{1,0:T(8,128)(2,1)} %copy-done.148, bf16[256,960]{1,0:T(8,128)(2,1)} %copy-done.141, bf16[256,960]{1,0:T(8,128)(2,1)} %copy-done.143, bf16[256,960]{1,0:T(8,128)(2,1)} %copy-done.138, ...), custom_call_target="tpu_custom_call" | custom-call | tf_op jit(solution)/shard_map/pair_sums/pallas_call | solution.py:498
  703.7 13.2 %down_sums.1 = bf16[4,2560,240]{2,1,0:T(8,128)(2,1)} custom-call(bf16[4,256,640]{2,1,0:T(8,128)(2,1)} %get-tuple-element.334.refs_0_, bf16[4,256,640]{2,1,0:T(8,128)(2,1)} %get-tuple-element.335.refs_1_, bf16[4,256,640]{2,1,0:T(8,128)(2,1)} %get-tuple-element.336.refs_2_, bf16[4,256,640]{2,1,0:T(8,128)(2,1)} %get-tuple-element.337.refs_3_, ...), custom_call_target="tpu_custom_call" | custom-call | tf_op jit(solution)/shard_map/down_sums/pallas_call | solution.py:527
  722.1 12.0 %attend_back.8 = (f32[256,960]{1,0:T(8,128)S(1)}, f32[256,640]{1,0:T(8,128)S(1)}, bf16[256,640]{1,0:T(8,128)(2,1)}, bf16[256,640]{1,0:T(8,128)(2,1)}, bf16[256,640]{1,0:T(8,128)(2,1)}) custom-call(bf16[256,960]{1,0:T(8,128)(2,1)S(1)} %copy-done.26, bf16[256,640]{1,0:T(8,128)(2,1)S(1)} %copy-done.41, bf16[256,640]{1,0:T(8,128)(2,1)} %collective-permute-done.refs_2_, ...), custom_call_target="tpu_custom_call" | custom-call | tf_op jit(solution)/shard_map/attend_back/pallas_call | solution.py:201
  740.3 12.2 %attend_back.11 = (f32[256,960]{1,0:T(8,128)S(1)}, f32[256,640]{1,0:T(8,128)S(1)}, bf16[256,640]{1,0:T(8,128)(2,1)}, bf16[256,640]{1,0:T(8,128)(2,1)}, bf16[256,640]{1,0:T(8,128)(2,1)}) custom-call(bf16[256,960]{1,0:T(8,128)(2,1)S(1)} %copy-done.29, bf16[256,640]{1,0:T(8,128)(2,1)} %get-tuple-element.201.refs_1_, ...), custom_call_target="tpu_custom_call" | custom-call | tf_op jit(solution)/shard_map/attend_back/pallas_call | solution.py:201
  778.6 14.1 %collective-permute-done.35.refs_4_ = bf16[256,640]{1,0:T(8,128)(2,1)S(1)} collective-permute-done((bf16[256,640]{1,0:T(8,128)(2,1)}, bf16[256,640]{1,0:T(8,128)(2,1)S(1)}, u32[]{:S(2)}, u32[]{:S(2)}) %collective-permute-start.35) | collective-permute-done | bytes 327712 | tf_op jit(solution)/shard_map/ppermute | solution.py:558
  796.8 16.6 %attn_sums.1 = bf16[4,960,640]{2,1,0:T(8,128)(2,1)} custom-call(bf16[256,960]{1,0:T(8,128)(2,1)} %copy-done.135, bf16[256,960]{1,0:T(8,128)(2,1)} %copy-done.136, bf16[256,960]{1,0:T(8,128)(2,1)} %copy-done.133, bf16[256,960]{1,0:T(8,128)(2,1)} %copy-done.134, bf16[256,960]{1,0:T(8,128)(2,1)} %copy-done.131, bf16[256,960]{1,0:T(8,128)(2,1)} %copy-done.132, ...), custom_call_target="tpu_custom_call" | custom-call | tf_op jit(solution)/shard_map/attn_sums/pallas_call | solution.py:467
  814.2 39.5 %reduce-scatter.33.cloned.1.call-done = bf16[1,8,120,640]{3,2,1,0:T(8,128)(2,1)} async-done(((bf16[4,8,120,640]{3,2,1,0:T(8,128)(2,1)}), bf16[1,8,120,640]{3,2,1,0:T(8,128)(2,1)}) %reduce-scatter.33.cloned.1.call-update) | async-done | bytes 1228816
  853.8 64.3 %reduce-scatter.37.cloned.1.call-done = bf16[1,8,320,240]{3,2,1,0:T(8,128)(2,1)} async-done(((bf16[4,8,320,240]{3,2,1,0:T(8,128)(2,1)}), bf16[1,8,320,240]{3,2,1,0:T(8,128)(2,1)}) %reduce-scatter.37.cloned.1.call-update) | async-done | bytes 1228816
  918.2 61.7 %reduce-scatter.25.cloned.1.call-done = bf16[1,8,120,640]{3,2,1,0:T(8,128)(2,1)} async-done(((bf16[4,8,120,640]{3,2,1,0:T(8,128)(2,1)}), bf16[1,8,120,640]{3,2,1,0:T(8,128)(2,1)}) %reduce-scatter.25.cloned.1.call-update) | async-done | bytes 1228816
  989.0 39.8 %psum.7 = f32[5,960]{1,0:T(8,128)S(1)} all-reduce(f32[5,960]{1,0:T(8,128)S(1)} %concatenate.19), channel_id=1, replica_groups=mesh['dp'=8,'seq'=4] {'seq','dp'}, use_global_device_ids=true, to_apply=%region_8.9 | all-reduce | flops 4800 | bytes 38400 | tf_op jit(solution)/shard_map/psum | solution.py:679
  1031.6 18.8 %reduce-scatter.35.cloned.1.call-done = bf16[1,120,640]{2,1,0:T(8,128)(2,1)} async-done(((bf16[8,120,640]{2,1,0:T(8,128)(2,1)}), bf16[1,120,640]{2,1,0:T(8,128)(2,1)}) %reduce-scatter.35.cloned.1.call-update) | async-done | bytes 153616
  1052.1 32.1 %reduce-scatter.23.cloned.1.call-done = bf16[1,320,240]{2,1,0:T(8,128)(2,1)} async-done(((bf16[8,320,240]{2,1,0:T(8,128)(2,1)}), bf16[1,320,240]{2,1,0:T(8,128)(2,1)}) %reduce-scatter.23.cloned.1.call-update) | async-done | bytes 153616 | tf_op jit(solution)/shard_map/reduce_scatter | solution.py:673
  1085.8 32.3 %reduce-scatter.27.cloned.1.call-done = bf16[1,120,640]{2,1,0:T(8,128)(2,1)} async-done(((bf16[8,120,640]{2,1,0:T(8,128)(2,1)}), bf16[1,120,640]{2,1,0:T(8,128)(2,1)}) %reduce-scatter.27.cloned.1.call-update) | async-done | bytes 153616
  (585 shorter events, 322.6 us)
Async XLA Ops:
  7.2 71.4 %all-gather.11.cloned.1.call-start = ((), (), s32[]{:S(2)}) async-start(), calls=%async_computation.9 | async-start | bytes 5068800 | tf_op jit(solution)/shard_map/all_gather | solution.py:576
  10.6 142.2 %all-gather.13.cloned.1.call-start = ((), (), s32[]{:S(2)}) async-start(), calls=%async_computation.10 | async-start | bytes 5068800 | tf_op jit(solution)/shard_map/all_gather | solution.py:576
  11.3 207.5 %all-gather.15.cloned.1.call-start = ((), (), s32[]{:S(2)}) async-start(), calls=%async_computation.11 | async-start | bytes 5068800 | tf_op jit(solution)/shard_map/all_gather | solution.py:576
  12.1 273.7 %all-gather.17.cloned.1.call-start = ((), (), s32[]{:S(2)}) async-start(), calls=%async_computation.12 | async-start | bytes 5406720 | tf_op jit(solution)/shard_map/all_gather | solution.py:576
  12.6 800.8 %reduce-scatter.29.cloned.1.call-start = ((), (), s32[]{:S(2)}) async-start(), calls=%async_computation.15 | async-start | bytes 6144000
  101.5 205.7 %collective-permute-start.11 = (bf16[256,640]{1,0:T(8,128)(2,1)}, bf16[256,640]{1,0:T(8,128)(2,1)}, u32[]{:S(2)}, u32[]{:S(2)}) collective-permute-start(bf16[256,640]{1,0:T(8,128)(2,1)} %get-tuple-element.201.refs_1_), channel_id=1, source_target_pairs={{0,3},{4,7},{8,11},{12,15},{16,19},{20,23},{24,27},{28,31}} | collective-permute-start | bytes 983048 | tf_op jit(solution)/shard_map/ppermute | solution.py:554
  103.5 206.6 %collective-permute-start.10 = (bf16[256,640]{1,0:T(8,128)(2,1)}, bf16[256,640]{1,0:T(8,128)(2,1)}, u32[]{:S(2)}, u32[]{:S(2)}) collective-permute-start(bf16[256,640]{1,0:T(8,128)(2,1)} %get-tuple-element.201.refs_1_), channel_id=1, source_target_pairs={{0,2},{1,3},{4,6},{5,7},{8,10},{9,11},{12,14},{13,15},{16,18},{17,... | collective-permute-start | bytes 983048 | tf_op jit(solution)/shard_map/ppermute | solution.py:554
  106.2 203.8 %collective-permute-start.9 = (bf16[256,640]{1,0:T(8,128)(2,1)}, bf16[256,640]{1,0:T(8,128)(2,1)}, u32[]{:S(2)}, u32[]{:S(2)}) collective-permute-start(bf16[256,640]{1,0:T(8,128)(2,1)} %get-tuple-element.201.refs_1_), channel_id=1, source_target_pairs={{0,1},{1,2},{2,3},{4,5},{5,6},{6,7},{8,9},{9,10},{10,11},{12,13},{... | collective-permute-start | bytes 983048 | tf_op jit(solution)/shard_map/ppermute | solution.py:554
  302.3 34.2 %collective-permute-start.5 = (bf16[256,640]{1,0:T(8,128)(2,1)S(1)}, bf16[256,640]{1,0:T(8,128)(2,1)S(1)}, u32[]{:S(2)}, u32[]{:S(2)}) collective-permute-start(bf16[256,640]{1,0:T(8,128)(2,1)S(1)} %get-tuple-element.193.refs_1_), channel_id=1, source_target_pairs={{0,3},{4,7},{8,11},{12,15},{16,19},{20,23},{24,27},{28,31}} | collective-permute-start | bytes 983048 | tf_op jit(solution)/shard_map/ppermute | solution.py:554
  360.5 37.0 %collective-permute-start.8 = (bf16[256,640]{1,0:T(8,128)(2,1)}, bf16[256,640]{1,0:T(8,128)(2,1)}, u32[]{:S(2)}, u32[]{:S(2)}) collective-permute-start(bf16[256,640]{1,0:T(8,128)(2,1)} %get-tuple-element.197.refs_1_), channel_id=1, source_target_pairs={{0,3},{4,7},{8,11},{12,15},{16,19},{20,23},{24,27},{28,31}} | collective-permute-start | bytes 983048 | tf_op jit(solution)/shard_map/ppermute | solution.py:554
  362.6 37.3 %collective-permute-start.7 = (bf16[256,640]{1,0:T(8,128)(2,1)}, bf16[256,640]{1,0:T(8,128)(2,1)}, u32[]{:S(2)}, u32[]{:S(2)}) collective-permute-start(bf16[256,640]{1,0:T(8,128)(2,1)} %get-tuple-element.197.refs_1_), channel_id=1, source_target_pairs={{0,2},{1,3},{4,6},{5,7},{8,10},{9,11},{12,14},{13,15},{16,18},{17,... | collective-permute-start | bytes 983048 | tf_op jit(solution)/shard_map/ppermute | solution.py:554
  364.6 35.3 %collective-permute-start.6 = (bf16[256,640]{1,0:T(8,128)(2,1)}, bf16[256,640]{1,0:T(8,128)(2,1)}, u32[]{:S(2)}, u32[]{:S(2)}) collective-permute-start(bf16[256,640]{1,0:T(8,128)(2,1)} %get-tuple-element.197.refs_1_), channel_id=1, source_target_pairs={{0,1},{1,2},{2,3},{4,5},{5,6},{6,7},{8,9},{9,10},{10,11},{12,13},{... | collective-permute-start | bytes 983048 | tf_op jit(solution)/shard_map/ppermute | solution.py:554
  389.4 69.1 %collective-permute-start.17 = (bf16[256,640]{1,0:T(8,128)(2,1)}, bf16[256,640]{1,0:T(8,128)(2,1)}, u32[]{:S(2)}, u32[]{:S(2)}) collective-permute-start(bf16[256,640]{1,0:T(8,128)(2,1)} %get-tuple-element.209.refs_1_), channel_id=1, source_target_pairs={{0,3},{4,7},{8,11},{12,15},{16,19},{20,23},{24,27},{28,31}} | collective-permute-start | bytes 983048 | tf_op jit(solution)/shard_map/ppermute | solution.py:554
  395.4 67.3 %collective-permute-start.16 = (bf16[256,640]{1,0:T(8,128)(2,1)}, bf16[256,640]{1,0:T(8,128)(2,1)}, u32[]{:S(2)}, u32[]{:S(2)}) collective-permute-start(bf16[256,640]{1,0:T(8,128)(2,1)} %get-tuple-element.209.refs_1_), channel_id=1, source_target_pairs={{0,2},{1,3},{4,6},{5,7},{8,10},{9,11},{12,14},{13,15},{16,18},{17,... | collective-permute-start | bytes 983048 | tf_op jit(solution)/shard_map/ppermute | solution.py:554
  397.5 65.2 %collective-permute-start.15 = (bf16[256,640]{1,0:T(8,128)(2,1)}, bf16[256,640]{1,0:T(8,128)(2,1)}, u32[]{:S(2)}, u32[]{:S(2)}) collective-permute-start(bf16[256,640]{1,0:T(8,128)(2,1)} %get-tuple-element.209.refs_1_), channel_id=1, source_target_pairs={{0,1},{1,2},{2,3},{4,5},{5,6},{6,7},{8,9},{9,10},{10,11},{12,13},{... | collective-permute-start | bytes 983048 | tf_op jit(solution)/shard_map/ppermute | solution.py:554
  455.8 69.7 %collective-permute-start.18 = (bf16[256,640]{1,0:T(8,128)(2,1)}, bf16[256,640]{1,0:T(8,128)(2,1)}, u32[]{:S(2)}, u32[]{:S(2)}) collective-permute-start(bf16[256,640]{1,0:T(8,128)(2,1)} %get-tuple-element.223), channel_id=1, source_target_pairs={{1,0},{2,1},{3,2},{5,4},{6,5},{7,6},{9,8},{10,9},{11,10},{13,12},{... | collective-permute-start | bytes 983048 | tf_op jit(solution)/shard_map/ppermute | solution.py:558
  457.1 69.7 %collective-permute-start.19 = (bf16[256,640]{1,0:T(8,128)(2,1)}, bf16[256,640]{1,0:T(8,128)(2,1)}, u32[]{:S(2)}, u32[]{:S(2)}) collective-permute-start(bf16[256,640]{1,0:T(8,128)(2,1)} %get-tuple-element.224), channel_id=1, source_target_pairs={{2,0},{3,1},{6,4},{7,5},{10,8},{11,9},{14,12},{15,13},{18,16},{19,... | collective-permute-start | bytes 983048 | tf_op jit(solution)/shard_map/ppermute | solution.py:558
  458.4 68.4 %collective-permute-start.20 = (bf16[256,640]{1,0:T(8,128)(2,1)}, bf16[256,640]{1,0:T(8,128)(2,1)}, u32[]{:S(2)}, u32[]{:S(2)}) collective-permute-start(bf16[256,640]{1,0:T(8,128)(2,1)} %get-tuple-element.225), channel_id=1, source_target_pairs={{3,0},{7,4},{11,8},{15,12},{19,16},{23,20},{27,24},{31,28}} | collective-permute-start | bytes 983048 | tf_op jit(solution)/shard_map/ppermute | solution.py:558
  522.9 51.0 %collective-permute-start.27 = (bf16[256,640]{1,0:T(8,128)(2,1)}, bf16[256,640]{1,0:T(8,128)(2,1)}, u32[]{:S(2)}, u32[]{:S(2)}) collective-permute-start(bf16[256,640]{1,0:T(8,128)(2,1)} %get-tuple-element.265), channel_id=1, source_target_pairs={{1,0},{2,1},{3,2},{5,4},{6,5},{7,6},{9,8},{10,9},{11,10},{13,12},{... | collective-permute-start | bytes 983048 | tf_op jit(solution)/shard_map/ppermute | solution.py:558
  524.2 51.1 %collective-permute-start.28 = (bf16[256,640]{1,0:T(8,128)(2,1)}, bf16[256,640]{1,0:T(8,128)(2,1)}, u32[]{:S(2)}, u32[]{:S(2)}) collective-permute-start(bf16[256,640]{1,0:T(8,128)(2,1)} %get-tuple-element.266), channel_id=1, source_target_pairs={{2,0},{3,1},{6,4},{7,5},{10,8},{11,9},{14,12},{15,13},{18,16},{19,... | collective-permute-start | bytes 983048 | tf_op jit(solution)/shard_map/ppermute | solution.py:558
  525.5 49.9 %collective-permute-start.29 = (bf16[256,640]{1,0:T(8,128)(2,1)}, bf16[256,640]{1,0:T(8,128)(2,1)}, u32[]{:S(2)}, u32[]{:S(2)}) collective-permute-start(bf16[256,640]{1,0:T(8,128)(2,1)} %get-tuple-element.267), channel_id=1, source_target_pairs={{3,0},{7,4},{11,8},{15,12},{19,16},{23,20},{27,24},{31,28}} | collective-permute-start | bytes 983048 | tf_op jit(solution)/shard_map/ppermute | solution.py:558
  571.3 51.5 %collective-permute-start.21 = (bf16[256,640]{1,0:T(8,128)(2,1)}, bf16[256,640]{1,0:T(8,128)(2,1)S(1)}, u32[]{:S(2)}, u32[]{:S(2)}) collective-permute-start(bf16[256,640]{1,0:T(8,128)(2,1)} %get-tuple-element.236), channel_id=1, source_target_pairs={{1,0},{2,1},{3,2},{5,4},{6,5},{7,6},{9,8},{10,9},{11,10},{13,12},{... | collective-permute-start | bytes 983048 | tf_op jit(solution)/shard_map/ppermute | solution.py:558
  572.6 52.3 %collective-permute-start.22 = (bf16[256,640]{1,0:T(8,128)(2,1)}, bf16[256,640]{1,0:T(8,128)(2,1)}, u32[]{:S(2)}, u32[]{:S(2)}) collective-permute-start(bf16[256,640]{1,0:T(8,128)(2,1)} %get-tuple-element.237), channel_id=1, source_target_pairs={{2,0},{3,1},{6,4},{7,5},{10,8},{11,9},{14,12},{15,13},{18,16},{19,... | collective-permute-start | bytes 983048 | tf_op jit(solution)/shard_map/ppermute | solution.py:558
  573.9 51.0 %collective-permute-start.23 = (bf16[256,640]{1,0:T(8,128)(2,1)}, bf16[256,640]{1,0:T(8,128)(2,1)}, u32[]{:S(2)}, u32[]{:S(2)}) collective-permute-start(bf16[256,640]{1,0:T(8,128)(2,1)} %get-tuple-element.238), channel_id=1, source_target_pairs={{3,0},{7,4},{11,8},{15,12},{19,16},{23,20},{27,24},{31,28}} | collective-permute-start | bytes 983048 | tf_op jit(solution)/shard_map/ppermute | solution.py:558
  703.1 150.6 %reduce-scatter.33.cloned.1.call-start = ((), (), s32[]{:S(2)}) async-start(), calls=%async_computation.17 | async-start | bytes 6144000
  703.7 214.5 %reduce-scatter.37.cloned.1.call-start = ((), (), s32[]{:S(2)}) async-start(), calls=%async_computation.19 | async-start | bytes 6553600
  717.0 263.0 %reduce-scatter.25.cloned.1.call-start = ((), (), s32[]{:S(2)}) async-start(), calls=%async_computation.13 | async-start | bytes 6144000
  755.1 37.7 %collective-permute-start.35 = (bf16[256,640]{1,0:T(8,128)(2,1)}, bf16[256,640]{1,0:T(8,128)(2,1)S(1)}, u32[]{:S(2)}, u32[]{:S(2)}) collective-permute-start(bf16[256,640]{1,0:T(8,128)(2,1)} %get-tuple-element.293), channel_id=1, source_target_pairs={{3,0},{7,4},{11,8},{15,12},{19,16},{23,20},{27,24},{31,28}} | collective-permute-start | bytes 983048 | tf_op jit(solution)/shard_map/ppermute | solution.py:558
  813.4 216.6 %reduce-scatter.31.cloned.1.call-start = ((), (), s32[]{:S(2)}) async-start(), calls=%async_computation.16 | async-start | bytes 1382400
  814.1 236.3 %reduce-scatter.35.cloned.1.call-start = ((), (), s32[]{:S(2)}) async-start(), calls=%async_computation.18 | async-start | bytes 1382400
  853.8 230.4 %reduce-scatter.23.cloned.1.call-start = ((), (), s32[]{:S(2)}) async-start(), calls=%async_computation.8 | async-start | bytes 1474560 | tf_op jit(solution)/shard_map/reduce_scatter | solution.py:673
  918.2 199.9 %reduce-scatter.27.cloned.1.call-start = ((), (), s32[]{:S(2)}) async-start(), calls=%async_computation.14 | async-start | bytes 1382400
  (221 other events, 2393.2 us)
Sparse Core Ops, SparseCore 0:
  11.4 67.0 all-gather.10
  81.4 71.3 all-gather.12
  155.6 63.1 all-gather.14
  221.5 64.1 all-gather.16
  703.2 88.0 reduce-scatter.28
  794.2 59.5 reduce-scatter.32
  856.7 61.4 reduce-scatter.36
  921.2 58.7 reduce-scatter.24
  982.3 33.7 reduce-scatter.30
  1018.2 32.1 reduce-scatter.34
  1052.7 31.3 reduce-scatter.22
  1086.3 31.7 reduce-scatter.26

commit v2 on v1

--- a/solution.py
+++ b/solution.py
@@ -537,6 +537,248 @@
     )(*hidden, *grads)
 
 
+MESH = pl.DeviceIdType.MESH
+
+
+class Place:
+    def __init__(self, layers):
+        dp, seq = lax.axis_index("dp"), lax.axis_index("seq")
+        self.layers = layers
+        self.z, self.core = lax.div(dp, 2), lax.rem(dp, 2)
+        self.y, self.x = lax.div(seq, 2), lax.rem(seq, 2)
+        self.sibling = (self.z * 2 + 1 - self.core, seq)
+        self.over_x = (dp, self.y * 2 + 1 - self.x)
+        self.over_y = (dp, (1 - self.y) * 2 + self.x)
+        self.up = [(lax.rem(self.z + k, layers) * 2 + self.core, seq) for k in range(layers)]
+        self.down = [
+            (lax.rem(self.z + layers - k, layers) * 2 + self.core, seq) for k in range(layers)
+        ]
+        self.peers = [self.sibling, self.over_x, self.over_y] + self.up[1:]
+
+    def greet(self):
+        barrier = pltpu.get_barrier_semaphore()
+        for peer in self.peers:
+            pl.semaphore_signal(barrier, inc=1, device_id=peer, device_id_type=MESH)
+        pl.semaphore_wait(barrier, len(self.peers))
+
+
+def remote(source, target, sems, peer):
+    return pltpu.make_async_remote_copy(
+        src_ref=source, dst_ref=target, send_sem=sems[0], recv_sem=sems[1],
+        device_id=peer, device_id_type=MESH,
+    )
+
+
+def gather_kernel(count, layers, *refs):
+    ins, outs = refs[:count], refs[count : 2 * count]
+    send, recv, keep = refs[2 * count :]
+    here = Place(layers)
+    here.greet()
+    y, x, z, core = here.y, here.x, here.z, here.core
+    sent = []
+
+    def slot(a, index):
+        return send.at[a, index], recv.at[a, index]
+
+    def start(a, index, source, target, peer):
+        copy = remote(source, target, slot(a, index), peer)
+        copy.start()
+        sent.append(copy)
+
+    def arrive(a, index, landing):
+        remote(landing, landing, slot(a, index), here.sibling).wait_recv()
+
+    def layer(k):
+        return lax.rem(z + layers - k, layers)
+
+    def sides(a):
+        if a % 2 == 0:
+            return here.over_x, here.over_y, (y, 1 - x), ((1 - y, x), (1 - y, 1 - x))
+        return here.over_y, here.over_x, (1 - y, x), ((y, 1 - x), (1 - y, 1 - x))
+
+    own = [pltpu.make_async_copy(ins[a], outs[a].at[y, x, z, core], keep.at[a]) for a in range(count)]
+    for copy in own:
+        copy.start()
+
+    def first(k):
+        for a in range(count):
+            spot = outs[a].at[y, x, layer(k), core]
+            source = ins[a] if k == 0 else spot
+            if k:
+                arrive(a, k, spot)
+            start(a, layers + k, source, spot, sides(a)[0])
+            start(a, 2 * layers + k, source, spot, sides(a)[1])
+
+    def second(k):
+        for a in range(count):
+            side = sides(a)[2]
+            spot = outs[a].at[side[0], side[1], layer(k), core]
+            arrive(a, layers + k, spot)
+            start(a, 3 * layers + k, spot, spot, sides(a)[1])
+
+    def third(k):
+        for a in range(count):
+            for turn_of, side in enumerate(sides(a)[3]):
+                arrive(a, (2 + turn_of) * layers + k, outs[a].at[side[0], side[1], layer(k), core])
+            if k == 0:
+                own[a].wait()
+            spot = outs[a].at[:, :, layer(k), core]
+            start(a, 4 * layers + k, spot, spot, here.sibling)
+
+    def z_sends(k):
+        for a in range(count):
+            start(a, k, ins[a], outs[a].at[y, x, z, core], here.up[k])
+
+    for a in range(count):
+        for k in range(1, layers):
+            start(a, k, ins[a], outs[a].at[y, x, z, core], here.up[k])
+    for k in range(layers + 2):
+        if k < layers:
+            first(k)
+        if 1 <= k <= layers:
+            second(k - 1)
+        if k >= 2:
+            third(k - 2)
+    for k in range(layers):
+        for a in range(count):
+            arrive(a, 4 * layers + k, outs[a].at[:, :, layer(k), 1 - core])
+    for copy in sent:
+        copy.wait_send()
+
+
+def gather_all(parts, layers):
+    count = len(parts)
+    anywhere = pl.BlockSpec(memory_space=pl.ANY)
+    return pl.pallas_call(
+        functools.partial(gather_kernel, count, layers),
+        out_shape=tuple(shape((2, 2, layers, 2) + part.shape, part.dtype) for part in parts),
+        in_specs=[anywhere] * count,
+        out_specs=(anywhere,) * count,
+        scratch_shapes=[
+            pltpu.SemaphoreType.DMA((count, 5 * layers)),
+            pltpu.SemaphoreType.DMA((count, 5 * layers)),
+            pltpu.SemaphoreType.DMA((count,)),
+        ],
+        compiler_params=pltpu.CompilerParams(collective_id=0, has_side_effects=True),
+        name="gather_all",
+    )(*parts)
+
+
+def reduce_kernel(count, layers, *refs):
+    ins, outs = refs[:count], refs[count : 2 * count]
+    held, core_in, first_in, second_in, done, z_in = (
+        refs[(2 + i) * count : (3 + i) * count] for i in range(6)
+    )
+    send, recv, keep = refs[8 * count :]
+    here = Place(layers)
+    here.greet()
+    y, x, z, core = here.y, here.x, here.z, here.core
+    sent = []
+
+    def slot(a, index):
+        return send.at[a, index], recv.at[a, index]
+
+    def start(a, index, source, target, peer):
+        copy = remote(source, target, slot(a, index), peer)
+        copy.start()
+        sent.append(copy)
+
+    def arrive(a, index, landing):
+        remote(landing, landing, slot(a, index), here.sibling).wait_recv()
+
+    def layer(k):
+        return lax.rem(z + k + 1, layers)
+
+    def added(ref, one, two):
+        return (one.astype(F32) + two.astype(F32)).astype(ref.dtype)
+
+    loads = [[None] * layers for _ in range(count)]
+    for k in range(layers):
+        for a in range(count):
+            start(a, k, ins[a].at[:, :, layer(k), 1 - core], core_in[a].at[k], here.sibling)
+            loads[a][k] = pltpu.make_async_copy(
+                ins[a].at[:, :, layer(k), core], held[a].at[k], keep.at[a, k]
+            )
+            loads[a][k].start()
+
+    def first(k):
+        for a in range(count):
+            loads[a][k].wait()
+            arrive(a, k, core_in[a].at[k])
+            held[a][k] = added(held[a], held[a][k], core_in[a][k])
+            if a % 2 == 0:
+                start(a, layers + k, held[a].at[k, :, 1 - x], first_in[a].at[k], here.over_x)
+            else:
+                start(a, layers + k, held[a].at[k, 1 - y], first_in[a].at[k], here.over_y)
+
+    def second(k):
+        for a in range(count):
+            arrive(a, layers + k, first_in[a].at[k])
+            for i in range(2):
+                if a % 2 == 0:
+                    held[a][k, i, x] = added(held[a], held[a][k, i, x], first_in[a][k, i])
+                else:
+                    held[a][k, y, i] = added(held[a], held[a][k, y, i], first_in[a][k, i])
+            if a % 2 == 0:
+                start(a, 2 * layers + k, held[a].at[k, 1 - y, x], second_in[a].at[k], here.over_y)
+            else:
+                start(a, 2 * layers + k, held[a].at[k, y, 1 - x], second_in[a].at[k], here.over_x)
+
+    def third(k):
+        for a in range(count):
+            arrive(a, 2 * layers + k, second_in[a].at[k])
+            done[a][k] = added(held[a], held[a][k, y, x], second_in[a][k])
+            if k < layers - 1:
+                start(a, 3 * layers + k, done[a].at[k], z_in[a].at[k], here.up[k + 1])
+
+    for k in range(layers + 2):
+        if k < layers:
+            first(k)
+        if 1 <= k <= layers:
+            second(k - 1)
+        if k >= 2:
+            third(k - 2)
+    for a in range(count):
+        total = done[a][layers - 1].astype(F32)
+        for k in range(layers - 1):
+            arrive(a, 3 * layers + k, z_in[a].at[k])
+            total = total + z_in[a][k].astype(F32)
+        outs[a][...] = total
+    for copy in sent:
+        copy.wait_send()
+
+
+def reduce_all(parts):
+    count = len(parts)
+    layers = parts[0].shape[2]
+    anywhere = pl.BlockSpec(memory_space=pl.ANY)
+
+    def buffers(*lead):
+        return [pltpu.VMEM(lead + part.shape[4:], part.dtype) for part in parts]
+
+    return pl.pallas_call(
+        functools.partial(reduce_kernel, count, layers),
+        out_shape=tuple(shape(part.shape[4:], F32) for part in parts),
+        in_specs=[anywhere] * count,
+        out_specs=(vmem,) * count,
+        scratch_shapes=[
+            *buffers(layers, 2, 2),
+            *buffers(layers, 2, 2),
+            *buffers(layers, 2),
+            *buffers(layers),
+            *buffers(layers),
+            *buffers(layers - 1),
+            pltpu.SemaphoreType.DMA((count, 4 * layers)),
+            pltpu.SemaphoreType.DMA((count, 4 * layers)),
+            pltpu.SemaphoreType.DMA((count, layers)),
+        ],
+        compiler_params=pltpu.CompilerParams(
+            collective_id=1, has_side_effects=True, vmem_limit_bytes=56 * MIB
+        ),
+        name="reduce_all",
+    )(*parts)
+
+
 def rope_tables(tokens):
     half = HEAD_DIM // 2
     frequency = rope_base ** (-(jnp.arange(half, dtype=F32) * 2.0 / HEAD_DIM))
@@ -563,7 +805,7 @@
     gate_weight, up_weight, down_weight, attn_gain, ffn_gain, router_weight,
 ):
     micros, _, tokens, width = inputs.shape
-    seq = lax.axis_size("seq")
+    seq, ranks = lax.axis_size("seq"), lax.axis_size("dp")
     mine = lax.axis_index("seq")
     rows = query_weight.shape[0]
     qc, kc = query_weight.shape[1], key_weight.shape[1]
@@ -572,14 +814,29 @@
     attn_local = jnp.concatenate([query_weight, key_weight, value_weight, out_weight], axis=1)
     both = ("seq", "dp")
 
-    def gather(local_part):
-        full = lax.all_gather(local_part, both, axis=0, tiled=False)
-        return full.reshape(seq, -1, full.shape[-1])
-
-    attn_w = gather(attn_local)
-    gate_w, up_w, down_w = gather(gate_weight), gather(up_weight), gather(down_weight)
-    small = jnp.concatenate([attn_gain[:, None], ffn_gain[:, None], router_weight], axis=1)
-    small = lax.all_gather(small, "dp", axis=0, tiled=True).astype(F32).T
+    span = ceil_to(max(rows, tokens), LANE)
+    small = jnp.concatenate([attn_gain[None], ffn_gain[None], router_weight.T], axis=0).astype(F32)
+    marks = jnp.concatenate([segments[:, 0], depths[:, 0]], axis=0).astype(F32)
+    small = jnp.concatenate(
+        [
+            jnp.pad(small, ((0, 8 - small.shape[0]), (0, span - rows))),
+            jnp.pad(marks, ((0, ceil_to(2 * micros, 8) - 2 * micros), (0, span - tokens))),
+        ],
+        axis=0,
+    )
+    parts = (attn_local, gate_weight, up_weight, down_weight, small)
+    direct = seq == 4 and ranks % 2 == 0
+    if direct:
+        gathered = gather_all(parts, ranks // 2)
+    else:
+        gathered = [lax.all_gather(part, both, axis=0, tiled=False) for part in parts]
+    attn_w, gate_w, up_w, down_w = (
+        full.reshape(seq, -1, full.shape[-1]) for full in gathered[:4]
+    )
+    small = gathered[4].reshape(seq, ranks, *small.shape)
+    marks = lax.dynamic_index_in_dim(small, lax.axis_index("dp"), 1, keepdims=False)
+    marks = marks[:, 8 : 8 + 2 * micros, :tokens].reshape(seq, 2, micros, tokens)
+    small = small[0, :, : 2 + RECUR, :rows].transpose(1, 0, 2).reshape(2 + RECUR, width)
     attn_g, ffn_g = small[0:1], small[1:2]
     routers = [small[2 + r : 3 + r] for r in range(RECUR)]
     used = qc + 2 * kc
@@ -589,11 +846,9 @@
     shift = used - low_col
     qkv_w, out_w = attn_w[:, :, :high_col], attn_w[:, :, low_col:]
 
-    marks = jnp.stack([segments[:, 0], depths[:, 0]], axis=1)
-    marks = lax.all_gather(marks, "seq", axis=0, tiled=False).astype(F32)
     order = mine - jnp.arange(seq)
     marks = jnp.where((order >= 0)[:, None, None, None], marks[order % seq], -1.0)
-    marks = marks.transpose(1, 2, 0, 3).reshape(micros, 2, seq * tokens)
+    marks = marks.transpose(2, 1, 0, 3).reshape(micros, 2, seq * tokens)
     infos = [jnp.pad(marks[m], ((0, 6), (0, 0))) for m in range(micros)]
     cosine, sine = rope_tables(tokens)
 
@@ -667,17 +922,23 @@
         every("normed"), every("packed"), every("attended"), every("grad_branch"), low_col, total_cols
     )
 
-    def reduce(partial):
-        partial = partial.reshape(seq, lax.axis_size("dp"), -1, partial.shape[-1])
-        part = lax.psum_scatter(partial, "seq", scatter_dimension=0, tiled=False)
-        return lax.psum_scatter(part, "dp", scatter_dimension=0, tiled=False).astype(F32)
-
-    down_grad, gate_grad, up_grad, attn_grad = (
-        reduce(partial) for partial in (down_sum, gate_sum, up_sum, attn_sum)
+    small_sum = jnp.concatenate([attn_gain_sum, ffn_gain_sum, *router_sums], axis=0)
+    small_sum = small_sum.reshape(2 + RECUR, ranks, rows).transpose(1, 0, 2)
+    small_sum = jnp.pad(
+        small_sum, ((0, 0), (0, 8 - small_sum.shape[1]), (0, ceil_to(rows, LANE) - rows))
     )
-    small_sum = jnp.concatenate([attn_gain_sum, ffn_gain_sum, *router_sums], axis=0)
-    small_sum = lax.psum(small_sum, both)
-    small_own = lax.dynamic_slice_in_dim(small_sum, lax.axis_index("dp") * rows, rows, axis=1)
+    small_sum = jnp.broadcast_to(small_sum[None], (seq,) + small_sum.shape)
+    sums = [
+        part.reshape(seq, ranks, -1, part.shape[-1])
+        for part in (attn_sum, gate_sum, up_sum, down_sum, small_sum)
+    ]
+    if direct:
+        sums = reduce_all([part.reshape(2, 2, ranks // 2, 2, *part.shape[2:]) for part in sums])
+    else:
+        sums = [lax.psum_scatter(part, "seq", scatter_dimension=0) for part in sums]
+        sums = [lax.psum_scatter(part, "dp", scatter_dimension=0).astype(F32) for part in sums]
+    attn_grad, gate_grad, up_grad, down_grad, small_own = sums
+    small_own = small_own[: 2 + RECUR, :rows]
 
     outputs = jnp.stack(states, axis=0)[:, None]
     input_grad = jnp.stack(grads, axis=0)[:, None]

time: 1140 us -> 825 us (0.72)
  waiting for transfers between devices: 484 us -> 12.5 us
  Pallas kernels: 367 us -> 611 us
  blocking collectives: 62.3 us -> 0 us
  between operations: 16.7 us -> 2.92 us
    pallas_call x0 -> x2, Pallas kernels: none -> 235 us  [the longest x1 125 us: reduce_all(): pl.pallas_call(functools.partial(reduce_kernel, count, layers), out_shape...]
    unnamed x19 -> x0, waiting for transfers between devices: 220 us -> none
    all_gather x4 -> x0, waiting for transfers between devices: 202 us -> none  [gather(): full = lax.all_gather(local_part, both, axis=0, tiled=False)]
    psum x1 -> x0, blocking collectives: 39.8 us -> none  [local(): small_sum = lax.psum(small_sum, both)]
    reduce_scatter x1 -> x0, waiting for transfers between devices: 32.1 us -> none  [reduce(): lax.psum_scatter(part, 'dp', scatter_dimension=0, tiled=False).astype(F32)]
    ppermute x18, waiting for transfers between devices: 29.5 us -> 0.05 us  [pass_back(): lax.ppermute(array, 'seq', [(i + step, i) for i in range(count - step)])]
    all_gather x2 -> x0, blocking collectives: 22.5 us -> none  [the longest x1 12.9 us: local(): small = lax.all_gather(small, 'dp', axis=0, tiled=True).astype(F32).T]
    ppermute x18, waiting for transfers between devices: 0.05 us -> 12.5 us  [pass_on(): lax.ppermute(array, 'seq', [(i, i + step) for i in range(count - step)])]
  transfers between devices with their start and end apart: 48 -> 36, of which waited for: 13 -> 1; matrix products, arithmetic and copies ran while one was open for 3% -> 2% of each run, Pallas kernels for 29% -> 43%
where the time goes in v2:
time: 825 us; the launch traced here: 813 us
  Pallas kernels  611 us (74%)
  local copies, waits for them, and re-layouts  116 us (14%)
  starting transfers between devices  64.9 us (8%)
  waiting for transfers between devices  12.5 us (2%)
    pallas_call x1, Pallas kernels, reduce_all(): pl.pallas_call(functools.partial(reduce_kernel, count, layers), out_shape...  125 us
    pallas_call x1, Pallas kernels, gather_all(): pl.pallas_call(functools.partial(gather_kernel, count, layers), out_shape...  110 us
    unnamed x396, local copies, waits for them, and re-layouts  97 us
    pallas_call x6, Pallas kernels, post_back(): pl.pallas_call(functools.partial(post_back_kernel, shift), grid=(pieces,)...  93.1 us
    pallas_call x6, Pallas kernels, post_part(): pl.pallas_call(functools.partial(post_kernel, shift), grid=(pieces,), out...  74.7 us
    pallas_call x6, Pallas kernels, attend_back(): pl.pallas_call(functools.partial(attend_back_kernel, blocks, recursion),...  72.3 us
    pallas_call x6, Pallas kernels, attend(): pl.pallas_call(functools.partial(attend_kernel, blocks, recursion), out_s...  44.6 us
    ppermute x18, starting transfers between devices, pass_on(): lax.ppermute(array, 'seq', [(i, i + step) for i in range(count - step)])  40.3 us
  transfers between devices with their start and end apart: 36, of which 1 were waited for; matrix products, arithmetic and copies ran while one was open for 2% of the time, Pallas kernels for 43%

profile of v2, /device:TPU:0, one launch (start us, length us, event | category | flops | bytes accessed | tf_op | source)
XLA Modules:
  0.0 812.6 jit_solution(5809609297260513695)
XLA Ops:
  7.1 109.8 %gather_all.1 = (bf16[2,2,4,2,120,640]{5,4,3,2,1,0:T(8,128)(2,1)}, bf16[2,2,4,2,120,640]{5,4,3,2,1,0:T(8,128)(2,1)}, bf16[2,2,4,2,120,640]{5,4,3,2,1,0:T(8,128)(...) custom-call(bf16[120,640]{1,0:T(8,128)(2,1)} %pad_maximum_fusion.refs_0_, ...), custom_call_target="tpu_custom_call" | custom-call | tf_op jit(solution)/shard_map/gather_all/pallas_call | solution.py:652
  123.6 4.1 collective-permute-start.11
  149.8 12.4 %collective-permute-done.1.refs_3_ = bf16[256,640]{1,0:T(8,128)(2,1)} collective-permute-done((bf16[256,640]{1,0:T(8,128)(2,1)}, bf16[256,640]{1,0:T(8,128)(2,1)}, u32[]{:S(2)}, u32[]{:S(2)}) %collective-permute-start.1) | collective-permute-done | bytes 327712 | tf_op jit(solution)/shard_map/ppermute | solution.py:796
  162.2 7.5 attend.6
  169.8 12.6 %post.6 = (f32[256,960]{1,0:T(8,128)S(1)}, bf16[256,960]{1,0:T(8,128)(2,1)S(1)}, bf16[4,256,640]{2,1,0:T(8,128)(2,1)}, bf16[4,256,640]{2,1,0:T(8,128)(2,1)}, bf1...) custom-call(f32[256,960]{1,0:T(8,128)S(1)} %bitcast.68, ...), custom_call_target="tpu_custom_call" | custom-call | tf_op jit(solution)/shard_map/post/pallas_call | solution.py:266
  187.3 4.5 collective-permute-start.4
  194.3 7.5 attend.9
  201.9 12.4 %post.9 = (f32[256,960]{1,0:T(8,128)S(1)}, bf16[256,960]{1,0:T(8,128)(2,1)S(1)}, bf16[4,256,640]{2,1,0:T(8,128)(2,1)}, bf16[4,256,640]{2,1,0:T(8,128)(2,1)}, bf1...) custom-call(f32[256,960]{1,0:T(8,128)S(1)} %bitcast.64, ...), custom_call_target="tpu_custom_call" | custom-call | tf_op jit(solution)/shard_map/post/pallas_call | solution.py:266
  227.9 7.4 attend.7
  236.0 12.5 %post.7 = (f32[256,960]{1,0:T(8,128)S(1)}, bf16[256,960]{1,0:T(8,128)(2,1)S(1)}, bf16[4,256,640]{2,1,0:T(8,128)(2,1)}, bf16[4,256,640]{2,1,0:T(8,128)(2,1)}, bf1...) custom-call(f32[256,960]{1,0:T(8,128)S(1)} %copy-done.7, ...), custom_call_target="tpu_custom_call" | custom-call | tf_op jit(solution)/shard_map/post/pallas_call | solution.py:266
  257.8 7.5 attend.10
  265.4 12.4 %post.10 = (f32[256,960]{1,0:T(8,128)S(1)}, bf16[256,960]{1,0:T(8,128)(2,1)S(1)}, bf16[4,256,640]{2,1,0:T(8,128)(2,1)}, bf16[4,256,640]{2,1,0:T(8,128)(2,1)}, bf...) custom-call(f32[256,960]{1,0:T(8,128)S(1)} %get-tuple-element.218.state.re, ...), custom_call_target="tpu_custom_call" | custom-call | tf_op jit(solution)/shard_map/post/pallas_call | solution.py:266
  295.7 7.4 attend.8
  303.2 12.5 %post.8 = (f32[256,960]{1,0:T(8,128)S(1)}, bf16[256,960]{1,0:T(8,128)(2,1)S(1)}, bf16[4,256,640]{2,1,0:T(8,128)(2,1)}, bf16[4,256,640]{2,1,0:T(8,128)(2,1)}, bf1...) custom-call(f32[256,960]{1,0:T(8,128)S(1)} %copy-done.12, ...), custom_call_target="tpu_custom_call" | custom-call | tf_op jit(solution)/shard_map/post/pallas_call | solution.py:266
  317.7 15.6 %post_back.6 = (bf16[4,256,240]{2,1,0:T(8,128)(2,1)S(1)}, bf16[4,256,640]{2,1,0:T(8,128)(2,1)}, bf16[4,256,640]{2,1,0:T(8,128)(2,1)}, bf16[4,256,256]{2,1,0:T(8,...) custom-call(f32[256,960]{1,0:T(8,128)S(1)} %bitcast.72, ...), custom_call_target="tpu_custom_call" | custom-call | tf_op jit(solution)/shard_map/post_back/pallas_call | solution.py:358
  335.9 12.0 %attend_back.6 = (f32[256,960]{1,0:T(8,128)S(1)}, f32[256,640]{1,0:T(8,128)S(1)}, bf16[256,640]{1,0:T(8,128)(2,1)}, bf16[256,640]{1,0:T(8,128)(2,1)}, bf16[256,640]{1,0:T(8,128)(2,1)}) custom-call(bf16[256,960]{1,0:T(8,128)(2,1)S(1)} %copy-done.39, bf16[256,640]{1,0:T(8,128)(2,1)} %get-tuple-element.212.refs_1_, ...), custom_call_target="tpu_custom_call" | custom-call | tf_op jit(solution)/shard_map/attend_back/pallas_call | solution.py:201
  352.5 7.5 attend.11
  360.2 12.4 %post.11 = (f32[256,960]{1,0:T(8,128)S(1)}, bf16[256,960]{1,0:T(8,128)(2,1)S(1)}, bf16[4,256,640]{2,1,0:T(8,128)(2,1)}, bf16[4,256,640]{2,1,0:T(8,128)(2,1)}, bf...) custom-call(f32[256,960]{1,0:T(8,128)S(1)} %copy-done.10, ...), custom_call_target="tpu_custom_call" | custom-call | tf_op jit(solution)/shard_map/post/pallas_call | solution.py:266
  378.5 15.7 %post_back.9 = (bf16[4,256,240]{2,1,0:T(8,128)(2,1)S(1)}, bf16[4,256,640]{2,1,0:T(8,128)(2,1)}, bf16[4,256,640]{2,1,0:T(8,128)(2,1)}, bf16[4,256,256]{2,1,0:T(8,...) custom-call(f32[256,960]{1,0:T(8,128)S(1)} %bitcast.71, ...), custom_call_target="tpu_custom_call" | custom-call | tf_op jit(solution)/shard_map/post_back/pallas_call | solution.py:358
  398.7 12.1 %attend_back.9 = (f32[256,960]{1,0:T(8,128)S(1)}, f32[256,640]{1,0:T(8,128)S(1)}, bf16[256,640]{1,0:T(8,128)(2,1)}, bf16[256,640]{1,0:T(8,128)(2,1)}, bf16[256,640]{1,0:T(8,128)(2,1)}) custom-call(bf16[256,960]{1,0:T(8,128)(2,1)S(1)} %copy-done.36, bf16[256,640]{1,0:T(8,128)(2,1)} %get-tuple-element.224.refs_1_, ...), custom_call_target="tpu_custom_call" | custom-call | tf_op jit(solution)/shard_map/attend_back/pallas_call | solution.py:201
  429.6 15.8 %post_back.7 = (bf16[4,256,240]{2,1,0:T(8,128)(2,1)S(1)}, bf16[4,256,640]{2,1,0:T(8,128)(2,1)}, bf16[4,256,640]{2,1,0:T(8,128)(2,1)}, bf16[4,256,256]{2,1,0:T(8,...) custom-call(f32[256,960]{1,0:T(8,128)S(1)} %copy-done.79, ...), custom_call_target="tpu_custom_call" | custom-call | tf_op jit(solution)/shard_map/post_back/pallas_call | solution.py:358
  448.0 12.0 %attend_back.7 = (f32[256,960]{1,0:T(8,128)S(1)}, f32[256,640]{1,0:T(8,128)S(1)}, bf16[256,640]{1,0:T(8,128)(2,1)}, bf16[256,640]{1,0:T(8,128)(2,1)}, bf16[256,640]{1,0:T(8,128)(2,1)}) custom-call(bf16[256,960]{1,0:T(8,128)(2,1)S(1)} %copy-done.34, bf16[256,640]{1,0:T(8,128)(2,1)} %get-tuple-element.208.refs_1_, ...), custom_call_target="tpu_custom_call" | custom-call | tf_op jit(solution)/shard_map/attend_back/pallas_call | solution.py:201
  477.8 15.4 %post_back.10 = (bf16[4,256,240]{2,1,0:T(8,128)(2,1)S(1)}, bf16[4,256,640]{2,1,0:T(8,128)(2,1)}, bf16[4,256,640]{2,1,0:T(8,128)(2,1)}, bf16[4,256,256]{2,1,0:T(8...) custom-call(f32[256,960]{1,0:T(8,128)S(1)} %copy-done.77, ...), custom_call_target="tpu_custom_call" | custom-call | tf_op jit(solution)/shard_map/post_back/pallas_call | solution.py:358
  495.8 12.1 %attend_back.10 = (f32[256,960]{1,0:T(8,128)S(1)}, f32[256,640]{1,0:T(8,128)S(1)}, bf16[256,640]{1,0:T(8,128)(2,1)}, bf16[256,640]{1,0:T(8,128)(2,1)}, bf16[256,640]{1,0:T(8,128)(2,1)}) custom-call(bf16[256,960]{1,0:T(8,128)(2,1)S(1)} %copy-done.31, bf16[256,640]{1,0:T(8,128)(2,1)} %get-tuple-element.220.refs_1_, ...), custom_call_target="tpu_custom_call" | custom-call | tf_op jit(solution)/shard_map/attend_back/pallas_call | solution.py:201
  522.5 15.3 %post_back.8 = (bf16[4,256,240]{2,1,0:T(8,128)(2,1)S(1)}, bf16[4,256,640]{2,1,0:T(8,128)(2,1)}, bf16[4,256,640]{2,1,0:T(8,128)(2,1)}, bf16[4,256,256]{2,1,0:T(8,...) custom-call(f32[256,960]{1,0:T(8,128)S(1)} %copy-done.81, ...), custom_call_target="tpu_custom_call" | custom-call | tf_op jit(solution)/shard_map/post_back/pallas_call | solution.py:358
  542.3 12.1 %attend_back.8 = (f32[256,960]{1,0:T(8,128)S(1)}, f32[256,640]{1,0:T(8,128)S(1)}, bf16[256,640]{1,0:T(8,128)(2,1)}, bf16[256,640]{1,0:T(8,128)(2,1)}, bf16[256,640]{1,0:T(8,128)(2,1)}) custom-call(bf16[256,960]{1,0:T(8,128)(2,1)S(1)} %copy-done.28, bf16[256,640]{1,0:T(8,128)(2,1)} %get-tuple-element.201.refs_1_, ...), custom_call_target="tpu_custom_call" | custom-call | tf_op jit(solution)/shard_map/attend_back/pallas_call | solution.py:201
  566.2 15.4 %post_back.11 = (bf16[4,256,240]{2,1,0:T(8,128)(2,1)S(1)}, bf16[4,256,640]{2,1,0:T(8,128)(2,1)}, bf16[4,256,640]{2,1,0:T(8,128)(2,1)}, bf16[4,256,256]{2,1,0:T(8...) custom-call(f32[256,960]{1,0:T(8,128)S(1)} %get-tuple-element.297.gr, ...), custom_call_target="tpu_custom_call" | custom-call | tf_op jit(solution)/shard_map/post_back/pallas_call | solution.py:358
  584.2 12.1 %attend_back.11 = (f32[256,960]{1,0:T(8,128)S(1)}, f32[256,640]{1,0:T(8,128)S(1)}, bf16[256,640]{1,0:T(8,128)(2,1)}, bf16[256,640]{1,0:T(8,128)(2,1)}, bf16[256,640]{1,0:T(8,128)(2,1)}) custom-call(bf16[256,960]{1,0:T(8,128)(2,1)S(1)} %copy-done.26, bf16[256,640]{1,0:T(8,128)(2,1)} %get-tuple-element.216.refs_1_, bf16[256,640]{1,0:T(8,128)(2,1)S(1)} %copy-done.41, ...), custom_call_target="tpu_custom_call" | custom-call | tf_op jit(solution)/shard_map/attend_back/pallas_call | solution.py:201
  606.7 13.0 %down_sums.1 = bf16[4,2560,240]{2,1,0:T(8,128)(2,1)} custom-call(bf16[4,256,640]{2,1,0:T(8,128)(2,1)} %get-tuple-element.349.refs_0_, bf16[4,256,640]{2,1,0:T(8,128)(2,1)} %get-tuple-element.350.refs_1_, bf16[4,256,640]{2,1,0:T(8,128)(2,1)} %get-tuple-element.351.refs_2_, bf16[4,256,640]{2,1,0:T(8,128)(2,1)} %get-tuple-element.352.refs_3_, ...), custom_call_target="tpu_custom_call" | custom-call | tf_op jit(solution)/shard_map/down_sums/pallas_call | solution.py:527
  619.8 24.7 %pair_sums.1 = (bf16[4,960,640]{2,1,0:T(8,128)(2,1)}, bf16[4,960,640]{2,1,0:T(8,128)(2,1)}) custom-call(bf16[256,960]{1,0:T(8,128)(2,1)} %copy-done.138, bf16[256,960]{1,0:T(8,128)(2,1)} %copy-done.141, bf16[256,960]{1,0:T(8,128)(2,1)} %copy-done.135, bf16[256,960]{1,0:T(8,128)(2,1)} %copy-done.136, bf16[256,960]{1,0:T(8,128)(2,1)} %copy-done.131, ...), custom_call_target="tpu_custom_call" | custom-call | tf_op jit(solution)/shard_map/pair_sums/pallas_call | solution.py:498
  656.0 16.9 %attn_sums.1 = bf16[4,960,640]{2,1,0:T(8,128)(2,1)} custom-call(bf16[256,960]{1,0:T(8,128)(2,1)} %copy-done.130, bf16[256,960]{1,0:T(8,128)(2,1)} %copy-done.132, bf16[256,960]{1,0:T(8,128)(2,1)} %copy-done.128, bf16[256,960]{1,0:T(8,128)(2,1)} %copy-done.129, bf16[256,960]{1,0:T(8,128)(2,1)} %copy-done.127, bf16[256,960]{1,0:T(8,128)(2,1)} %copy-done.126, ...), custom_call_target="tpu_custom_call" | custom-call | tf_op jit(solution)/shard_map/attn_sums/pallas_call | solution.py:467
  673.5 125.3 %reduce_all.1 = (f32[120,640]{1,0:T(8,128)}, f32[120,640]{1,0:T(8,128)}, f32[120,640]{1,0:T(8,128)}, f32[320,240]{1,0:T(8,128)}, f32[8,128]{1,0:T(8,128)}) custom-call(bf16[2,2,4,2,120,640]{5,4,3,2,1,0:T(8,128)(2,1)} %bitcast.114, bf16[2,2,4,2,120,640]{5,4,3,2,1,0:T(8,128)(2,1)} %bitcast.117, bf16[2,2,4,2,120,640]{5,4,3,2,1,0:T(8,128)(2,1)} %bitcast.118, ...), custom_call_target="tpu_custom_call" | custom-call | tf_op jit(solution)/shard_map/reduce_all/pallas_call | solution.py:759
  (531 shorter events, 214.2 us)
Async XLA Ops:
  123.6 68.2 %collective-permute-start.11 = (bf16[256,640]{1,0:T(8,128)(2,1)}, bf16[256,640]{1,0:T(8,128)(2,1)}, u32[]{:S(2)}, u32[]{:S(2)}) collective-permute-start(bf16[256,640]{1,0:T(8,128)(2,1)} %get-tuple-element.216.refs_1_), channel_id=1, source_target_pairs={{0,3},{4,7},{8,11},{12,15},{16,19},{20,23},{24,27},{28,31}} | collective-permute-start | bytes 983048 | tf_op jit(solution)/shard_map/ppermute | solution.py:796
  127.7 66.5 %collective-permute-start.10 = (bf16[256,640]{1,0:T(8,128)(2,1)}, bf16[256,640]{1,0:T(8,128)(2,1)}, u32[]{:S(2)}, u32[]{:S(2)}) collective-permute-start(bf16[256,640]{1,0:T(8,128)(2,1)} %get-tuple-element.216.refs_1_), channel_id=1, source_target_pairs={{0,2},{1,3},{4,6},{5,7},{8,10},{9,11},{12,14},{13,15},{16,18},{17,... | collective-permute-start | bytes 983048 | tf_op jit(solution)/shard_map/ppermute | solution.py:796
  148.3 46.0 %collective-permute-start.9 = (bf16[256,640]{1,0:T(8,128)(2,1)}, bf16[256,640]{1,0:T(8,128)(2,1)S(1)}, u32[]{:S(2)}, u32[]{:S(2)}) collective-permute-start(bf16[256,640]{1,0:T(8,128)(2,1)} %get-tuple-element.216.refs_1_), channel_id=1, source_target_pairs={{0,1},{1,2},{2,3},{4,5},{5,6},{6,7},{8,9},{9,10},{10,11},{12,13},{... | collective-permute-start | bytes 983048 | tf_op jit(solution)/shard_map/ppermute | solution.py:796
  186.0 36.7 %collective-permute-start.5 = (bf16[256,640]{1,0:T(8,128)(2,1)}, bf16[256,640]{1,0:T(8,128)(2,1)S(1)}, u32[]{:S(2)}, u32[]{:S(2)}) collective-permute-start(bf16[256,640]{1,0:T(8,128)(2,1)} %get-tuple-element.208.refs_1_), channel_id=1, source_target_pairs={{0,3},{4,7},{8,11},{12,15},{16,19},{20,23},{24,27},{28,31}} | collective-permute-start | bytes 983048 | tf_op jit(solution)/shard_map/ppermute | solution.py:796
  187.3 38.5 %collective-permute-start.4 = (bf16[256,640]{1,0:T(8,128)(2,1)}, bf16[256,640]{1,0:T(8,128)(2,1)}, u32[]{:S(2)}, u32[]{:S(2)}) collective-permute-start(bf16[256,640]{1,0:T(8,128)(2,1)} %get-tuple-element.208.refs_1_), channel_id=1, source_target_pairs={{0,2},{1,3},{4,6},{5,7},{8,10},{9,11},{12,14},{13,15},{16,18},{17,... | collective-permute-start | bytes 983048 | tf_op jit(solution)/shard_map/ppermute | solution.py:796
  191.8 34.0 %collective-permute-start.3 = (bf16[256,640]{1,0:T(8,128)(2,1)}, bf16[256,640]{1,0:T(8,128)(2,1)}, u32[]{:S(2)}, u32[]{:S(2)}) collective-permute-start(bf16[256,640]{1,0:T(8,128)(2,1)} %get-tuple-element.208.refs_1_), channel_id=1, source_target_pairs={{0,1},{1,2},{2,3},{4,5},{5,6},{6,7},{8,9},{9,10},{10,11},{12,13},{... | collective-permute-start | bytes 983048 | tf_op jit(solution)/shard_map/ppermute | solution.py:796
  218.7 36.9 %collective-permute-start.14 = (bf16[256,640]{1,0:T(8,128)(2,1)}, bf16[256,640]{1,0:T(8,128)(2,1)}, u32[]{:S(2)}, u32[]{:S(2)}) collective-permute-start(bf16[256,640]{1,0:T(8,128)(2,1)} %get-tuple-element.220.refs_1_), channel_id=1, source_target_pairs={{0,3},{4,7},{8,11},{12,15},{16,19},{20,23},{24,27},{28,31}} | collective-permute-start | bytes 983048 | tf_op jit(solution)/shard_map/ppermute | solution.py:796
  220.7 37.1 %collective-permute-start.13 = (bf16[256,640]{1,0:T(8,128)(2,1)}, bf16[256,640]{1,0:T(8,128)(2,1)}, u32[]{:S(2)}, u32[]{:S(2)}) collective-permute-start(bf16[256,640]{1,0:T(8,128)(2,1)} %get-tuple-element.220.refs_1_), channel_id=1, source_target_pairs={{0,2},{1,3},{4,6},{5,7},{8,10},{9,11},{12,14},{13,15},{16,18},{17,... | collective-permute-start | bytes 983048 | tf_op jit(solution)/shard_map/ppermute | solution.py:796
  223.5 34.3 %collective-permute-start.12 = (bf16[256,640]{1,0:T(8,128)(2,1)}, bf16[256,640]{1,0:T(8,128)(2,1)}, u32[]{:S(2)}, u32[]{:S(2)}) collective-permute-start(bf16[256,640]{1,0:T(8,128)(2,1)} %get-tuple-element.220.refs_1_), channel_id=1, source_target_pairs={{0,1},{1,2},{2,3},{4,5},{5,6},{6,7},{8,9},{9,10},{10,11},{12,13},{... | collective-permute-start | bytes 983048 | tf_op jit(solution)/shard_map/ppermute | solution.py:796
  253.5 40.1 %collective-permute-start.7 = (bf16[256,640]{1,0:T(8,128)(2,1)}, bf16[256,640]{1,0:T(8,128)(2,1)}, u32[]{:S(2)}, u32[]{:S(2)}) collective-permute-start(bf16[256,640]{1,0:T(8,128)(2,1)} %get-tuple-element.212.refs_1_), channel_id=1, source_target_pairs={{0,2},{1,3},{4,6},{5,7},{8,10},{9,11},{12,14},{13,15},{16,18},{17,... | collective-permute-start | bytes 983048 | tf_op jit(solution)/shard_map/ppermute | solution.py:796
  255.5 38.1 %collective-permute-start.6 = (bf16[256,640]{1,0:T(8,128)(2,1)}, bf16[256,640]{1,0:T(8,128)(2,1)}, u32[]{:S(2)}, u32[]{:S(2)}) collective-permute-start(bf16[256,640]{1,0:T(8,128)(2,1)} %get-tuple-element.212.refs_1_), channel_id=1, source_target_pairs={{0,1},{1,2},{2,3},{4,5},{5,6},{6,7},{8,9},{9,10},{10,11},{12,13},{... | collective-permute-start | bytes 983048 | tf_op jit(solution)/shard_map/ppermute | solution.py:796
  280.6 70.2 %collective-permute-start.17 = (bf16[256,640]{1,0:T(8,128)(2,1)}, bf16[256,640]{1,0:T(8,128)(2,1)}, u32[]{:S(2)}, u32[]{:S(2)}) collective-permute-start(bf16[256,640]{1,0:T(8,128)(2,1)} %get-tuple-element.224.refs_1_), channel_id=1, source_target_pairs={{0,3},{4,7},{8,11},{12,15},{16,19},{20,23},{24,27},{28,31}} | collective-permute-start | bytes 983048 | tf_op jit(solution)/shard_map/ppermute | solution.py:796
  282.6 69.9 %collective-permute-start.16 = (bf16[256,640]{1,0:T(8,128)(2,1)}, bf16[256,640]{1,0:T(8,128)(2,1)}, u32[]{:S(2)}, u32[]{:S(2)}) collective-permute-start(bf16[256,640]{1,0:T(8,128)(2,1)} %get-tuple-element.224.refs_1_), channel_id=1, source_target_pairs={{0,2},{1,3},{4,6},{5,7},{8,10},{9,11},{12,14},{13,15},{16,18},{17,... | collective-permute-start | bytes 983048 | tf_op jit(solution)/shard_map/ppermute | solution.py:796
  284.6 67.9 %collective-permute-start.15 = (bf16[256,640]{1,0:T(8,128)(2,1)}, bf16[256,640]{1,0:T(8,128)(2,1)}, u32[]{:S(2)}, u32[]{:S(2)}) collective-permute-start(bf16[256,640]{1,0:T(8,128)(2,1)} %get-tuple-element.224.refs_1_), channel_id=1, source_target_pairs={{0,1},{1,2},{2,3},{4,5},{5,6},{6,7},{8,9},{9,10},{10,11},{12,13},{... | collective-permute-start | bytes 983048 | tf_op jit(solution)/shard_map/ppermute | solution.py:796
  347.9 67.3 %collective-permute-start.18 = (bf16[256,640]{1,0:T(8,128)(2,1)}, bf16[256,640]{1,0:T(8,128)(2,1)S(1)}, u32[]{:S(2)}, u32[]{:S(2)}) collective-permute-start(bf16[256,640]{1,0:T(8,128)(2,1)} %get-tuple-element.238), channel_id=1, source_target_pairs={{1,0},{2,1},{3,2},{5,4},{6,5},{7,6},{9,8},{10,9},{11,10},{13,12},{... | collective-permute-start | bytes 983048 | tf_op jit(solution)/shard_map/ppermute | solution.py:800
  349.5 67.0 %collective-permute-start.19 = (bf16[256,640]{1,0:T(8,128)(2,1)}, bf16[256,640]{1,0:T(8,128)(2,1)}, u32[]{:S(2)}, u32[]{:S(2)}) collective-permute-start(bf16[256,640]{1,0:T(8,128)(2,1)} %get-tuple-element.239), channel_id=1, source_target_pairs={{2,0},{3,1},{6,4},{7,5},{10,8},{11,9},{14,12},{15,13},{18,16},{19,... | collective-permute-start | bytes 983048 | tf_op jit(solution)/shard_map/ppermute | solution.py:800
  350.8 65.7 %collective-permute-start.20 = (bf16[256,640]{1,0:T(8,128)(2,1)}, bf16[256,640]{1,0:T(8,128)(2,1)}, u32[]{:S(2)}, u32[]{:S(2)}) collective-permute-start(bf16[256,640]{1,0:T(8,128)(2,1)} %get-tuple-element.240), channel_id=1, source_target_pairs={{3,0},{7,4},{11,8},{15,12},{19,16},{23,20},{27,24},{31,28}} | collective-permute-start | bytes 983048 | tf_op jit(solution)/shard_map/ppermute | solution.py:800
  412.6 51.8 %collective-permute-start.27 = (bf16[256,640]{1,0:T(8,128)(2,1)}, bf16[256,640]{1,0:T(8,128)(2,1)}, u32[]{:S(2)}, u32[]{:S(2)}) collective-permute-start(bf16[256,640]{1,0:T(8,128)(2,1)} %get-tuple-element.280), channel_id=1, source_target_pairs={{1,0},{2,1},{3,2},{5,4},{6,5},{7,6},{9,8},{10,9},{11,10},{13,12},{... | collective-permute-start | bytes 983048 | tf_op jit(solution)/shard_map/ppermute | solution.py:800
  413.9 52.0 %collective-permute-start.28 = (bf16[256,640]{1,0:T(8,128)(2,1)}, bf16[256,640]{1,0:T(8,128)(2,1)}, u32[]{:S(2)}, u32[]{:S(2)}) collective-permute-start(bf16[256,640]{1,0:T(8,128)(2,1)} %get-tuple-element.281), channel_id=1, source_target_pairs={{2,0},{3,1},{6,4},{7,5},{10,8},{11,9},{14,12},{15,13},{18,16},{19,... | collective-permute-start | bytes 983048 | tf_op jit(solution)/shard_map/ppermute | solution.py:800
  415.2 50.7 %collective-permute-start.29 = (bf16[256,640]{1,0:T(8,128)(2,1)}, bf16[256,640]{1,0:T(8,128)(2,1)}, u32[]{:S(2)}, u32[]{:S(2)}) collective-permute-start(bf16[256,640]{1,0:T(8,128)(2,1)} %get-tuple-element.282), channel_id=1, source_target_pairs={{3,0},{7,4},{11,8},{15,12},{19,16},{23,20},{27,24},{31,28}} | collective-permute-start | bytes 983048 | tf_op jit(solution)/shard_map/ppermute | solution.py:800
  461.8 50.5 %collective-permute-start.21 = (bf16[256,640]{1,0:T(8,128)(2,1)}, bf16[256,640]{1,0:T(8,128)(2,1)}, u32[]{:S(2)}, u32[]{:S(2)}) collective-permute-start(bf16[256,640]{1,0:T(8,128)(2,1)} %get-tuple-element.251), channel_id=1, source_target_pairs={{1,0},{2,1},{3,2},{5,4},{6,5},{7,6},{9,8},{10,9},{11,10},{13,12},{... | collective-permute-start | bytes 983048 | tf_op jit(solution)/shard_map/ppermute | solution.py:800
  463.1 50.9 %collective-permute-start.22 = (bf16[256,640]{1,0:T(8,128)(2,1)}, bf16[256,640]{1,0:T(8,128)(2,1)}, u32[]{:S(2)}, u32[]{:S(2)}) collective-permute-start(bf16[256,640]{1,0:T(8,128)(2,1)} %get-tuple-element.252), channel_id=1, source_target_pairs={{2,0},{3,1},{6,4},{7,5},{10,8},{11,9},{14,12},{15,13},{18,16},{19,... | collective-permute-start | bytes 983048 | tf_op jit(solution)/shard_map/ppermute | solution.py:800
  464.4 49.6 %collective-permute-start.23 = (bf16[256,640]{1,0:T(8,128)(2,1)}, bf16[256,640]{1,0:T(8,128)(2,1)}, u32[]{:S(2)}, u32[]{:S(2)}) collective-permute-start(bf16[256,640]{1,0:T(8,128)(2,1)} %get-tuple-element.253), channel_id=1, source_target_pairs={{3,0},{7,4},{11,8},{15,12},{19,16},{23,20},{27,24},{31,28}} | collective-permute-start | bytes 983048 | tf_op jit(solution)/shard_map/ppermute | solution.py:800
  509.7 48.1 %collective-permute-start.30 = (bf16[256,640]{1,0:T(8,128)(2,1)}, bf16[256,640]{1,0:T(8,128)(2,1)}, u32[]{:S(2)}, u32[]{:S(2)}) collective-permute-start(bf16[256,640]{1,0:T(8,128)(2,1)} %get-tuple-element.293), channel_id=1, source_target_pairs={{1,0},{2,1},{3,2},{5,4},{6,5},{7,6},{9,8},{10,9},{11,10},{13,12},{... | collective-permute-start | bytes 983048 | tf_op jit(solution)/shard_map/ppermute | solution.py:800
  511.0 48.3 %collective-permute-start.31 = (bf16[256,640]{1,0:T(8,128)(2,1)}, bf16[256,640]{1,0:T(8,128)(2,1)}, u32[]{:S(2)}, u32[]{:S(2)}) collective-permute-start(bf16[256,640]{1,0:T(8,128)(2,1)} %get-tuple-element.294), channel_id=1, source_target_pairs={{2,0},{3,1},{6,4},{7,5},{10,8},{11,9},{14,12},{15,13},{18,16},{19,... | collective-permute-start | bytes 983048 | tf_op jit(solution)/shard_map/ppermute | solution.py:800
  512.3 47.0 %collective-permute-start.32 = (bf16[256,640]{1,0:T(8,128)(2,1)}, bf16[256,640]{1,0:T(8,128)(2,1)}, u32[]{:S(2)}, u32[]{:S(2)}) collective-permute-start(bf16[256,640]{1,0:T(8,128)(2,1)} %get-tuple-element.295), channel_id=1, source_target_pairs={{3,0},{7,4},{11,8},{15,12},{19,16},{23,20},{27,24},{31,28}} | collective-permute-start | bytes 983048 | tf_op jit(solution)/shard_map/ppermute | solution.py:800
  555.2 45.5 %collective-permute-start.24 = (bf16[256,640]{1,0:T(8,128)(2,1)}, bf16[256,640]{1,0:T(8,128)(2,1)}, u32[]{:S(2)}, u32[]{:S(2)}) collective-permute-start(bf16[256,640]{1,0:T(8,128)(2,1)} %get-tuple-element.264), channel_id=1, source_target_pairs={{1,0},{2,1},{3,2},{5,4},{6,5},{7,6},{9,8},{10,9},{11,10},{13,12},{... | collective-permute-start | bytes 983048 | tf_op jit(solution)/shard_map/ppermute | solution.py:800
  556.5 88.0 %collective-permute-start.25 = (bf16[256,640]{1,0:T(8,128)(2,1)}, bf16[256,640]{1,0:T(8,128)(2,1)}, u32[]{:S(2)}, u32[]{:S(2)}) collective-permute-start(bf16[256,640]{1,0:T(8,128)(2,1)} %get-tuple-element.265), channel_id=1, source_target_pairs={{2,0},{3,1},{6,4},{7,5},{10,8},{11,9},{14,12},{15,13},{18,16},{19,... | collective-permute-start | bytes 983048 | tf_op jit(solution)/shard_map/ppermute | solution.py:800
  557.8 86.7 %collective-permute-start.26 = (bf16[256,640]{1,0:T(8,128)(2,1)}, bf16[256,640]{1,0:T(8,128)(2,1)}, u32[]{:S(2)}, u32[]{:S(2)}) collective-permute-start(bf16[256,640]{1,0:T(8,128)(2,1)} %get-tuple-element.266), channel_id=1, source_target_pairs={{3,0},{7,4},{11,8},{15,12},{19,16},{23,20},{27,24},{31,28}} | collective-permute-start | bytes 983048 | tf_op jit(solution)/shard_map/ppermute | solution.py:800
  598.1 53.4 %collective-permute-start.33 = (bf16[256,640]{1,0:T(8,128)(2,1)}, bf16[256,640]{1,0:T(8,128)(2,1)}, u32[]{:S(2)}, u32[]{:S(2)}) collective-permute-start(bf16[256,640]{1,0:T(8,128)(2,1)} %get-tuple-element.306), channel_id=1, source_target_pairs={{1,0},{2,1},{3,2},{5,4},{6,5},{7,6},{9,8},{10,9},{11,10},{13,12},{... | collective-permute-start | bytes 983048 | tf_op jit(solution)/shard_map/ppermute | solution.py:800
  599.4 52.1 %collective-permute-start.34 = (bf16[256,640]{1,0:T(8,128)(2,1)}, bf16[256,640]{1,0:T(8,128)(2,1)}, u32[]{:S(2)}, u32[]{:S(2)}) collective-permute-start(bf16[256,640]{1,0:T(8,128)(2,1)} %get-tuple-element.307), channel_id=1, source_target_pairs={{2,0},{3,1},{6,4},{7,5},{10,8},{11,9},{14,12},{15,13},{18,16},{19,... | collective-permute-start | bytes 983048 | tf_op jit(solution)/shard_map/ppermute | solution.py:800
  600.7 50.8 %collective-permute-start.35 = (bf16[256,640]{1,0:T(8,128)(2,1)}, bf16[256,640]{1,0:T(8,128)(2,1)}, u32[]{:S(2)}, u32[]{:S(2)}) collective-permute-start(bf16[256,640]{1,0:T(8,128)(2,1)} %get-tuple-element.308), channel_id=1, source_target_pairs={{3,0},{7,4},{11,8},{15,12},{19,16},{23,20},{27,24},{31,28}} | collective-permute-start | bytes 983048 | tf_op jit(solution)/shard_map/ppermute | solution.py:800
  (193 other events, 1413.2 us)

commit v3 on v2

--- a/solution.py
+++ b/solution.py
@@ -210,6 +210,267 @@
     )(queries, *pairs, info, attended, logs, grad)
 
 
+def is_outer():
+    place = lax.axis_index("seq")
+    return (place == 0) | (place == 3)
+
+
+def block_bias(info, bias, index, key_block, query_block, recursion, columns, diagonal):
+    block = bias.shape[1]
+
+    def span(which):
+        return pl.ds(pl.multiple_of(which * block, block), block)
+
+    same = columns[span(key_block), 0:1] == info[0:1, span(query_block)]
+    seen = columns[span(key_block), 1:2] > recursion
+    if diagonal:
+        key = lax.broadcasted_iota(jnp.int32, (block, block), 0)
+        query = lax.broadcasted_iota(jnp.int32, (block, block), 1)
+        seen = ((key < query) & seen) | (key == query)
+    bias[index] = jnp.where(same & seen, 0.0, -1e30)
+
+
+def tall_heads(ref, rows, group):
+    heads = range(group * GROUP, (group + 1) * GROUP)
+    return jnp.concatenate([ref[rows, head_cols(head)] for head in heads], axis=0)
+
+
+def thrice(bias):
+    return jnp.concatenate([bias] * GROUP, axis=1)
+
+
+def with_ones(value):
+    return jnp.concatenate([value.T, jnp.ones((16, value.shape[0]), BF)], axis=0)
+
+
+def own_kernel(recursion, queries, pair, info, part, columns, bias):
+    block = queries.shape[0] // 2
+    wide = GROUP * block
+    columns[...] = info[...].T
+    block_bias(info, bias, 0, 0, 0, recursion, columns, True)
+    block_bias(info, bias, 1, 0, 1, recursion, columns, False)
+    block_bias(info, bias, 2, 1, 1, recursion, columns, True)
+    low, high = slice(0, block), slice(block, 2 * block)
+    for group in range(KV_HEADS):
+        kc, vc = head_cols(group), head_cols(KV_HEADS + group)
+        query_low, query_high = tall_heads(queries, low, group), tall_heads(queries, high, group)
+        first = dot(pair[low, kc], query_low, NT) + thrice(bias[0])
+        second = dot(pair[low, kc], query_high, NT) + thrice(bias[1])
+        third = dot(pair[high, kc], query_high, NT) + thrice(bias[2])
+        value_low, value_high = with_ones(pair[low, vc]), with_ones(pair[high, vc])
+        top = jnp.max(first, axis=0, keepdims=True)
+        mixed = dot(value_low, jnp.exp(first - top).astype(BF))
+        part[group, : HEAD_DIM + 8, :wide] = mixed[: HEAD_DIM + 8]
+        part[group, HEAD_DIM + 8 :, :wide] = jnp.broadcast_to(top, (8, wide))
+        top = jnp.maximum(
+            jnp.max(second, axis=0, keepdims=True), jnp.max(third, axis=0, keepdims=True)
+        )
+        mixed = dot(value_low, jnp.exp(second - top).astype(BF))
+        mixed += dot(value_high, jnp.exp(third - top).astype(BF))
+        part[group, : HEAD_DIM + 8, wide:] = mixed[: HEAD_DIM + 8]
+        part[group, HEAD_DIM + 8 :, wide:] = jnp.broadcast_to(top, (8, wide))
+
+
+def attend_own(queries, pair, info, recursion):
+    tokens = queries.shape[0]
+    block = tokens // 2
+    return pl.pallas_call(
+        functools.partial(own_kernel, recursion),
+        out_shape=shape((KV_HEADS, HEAD_DIM + 16, GROUP * tokens), F32),
+        in_specs=[vmem] * 3,
+        out_specs=vmem,
+        scratch_shapes=[
+            pltpu.VMEM(info.shape[::-1], F32),
+            pltpu.VMEM((3, block, block), F32),
+        ],
+        compiler_params=params(40),
+        name="attend_own",
+    )(queries, pair, info)
+
+
+def rest_rows(block):
+    outer = is_outer()
+    shift = pl.multiple_of(jnp.where(outer, block, 0), block)
+    return outer, pl.ds(shift, block)
+
+
+def rest_kernel(recursion, queries, pair, info, part, attended, logs, columns, bias):
+    block = queries.shape[0] // 2
+    wide = GROUP * block
+    columns[...] = info[...].T
+    outer, rows = rest_rows(block)
+    fifth = jnp.where(outer, 1, 0)
+    block_bias(info, bias, 0, 2, 1, recursion, columns, False)
+    block_bias(info, bias, 1, 2 + fifth, fifth, recursion, columns, False)
+    low, high = slice(0, block), slice(block, 2 * block)
+    logs[...] = jnp.zeros(logs.shape, F32)
+    for group in range(KV_HEADS):
+        kc, vc = head_cols(group), head_cols(KV_HEADS + group)
+        fourth = dot(pair[low, kc], tall_heads(queries, high, group), NT) + thrice(bias[0])
+        fifth = dot(pair[rows, kc], tall_heads(queries, rows, group), NT) + thrice(bias[1])
+        own_low, own_high = part[group, :, :wide], part[group, :, wide:]
+        top_low, top_high = own_low[HEAD_DIM + 8 : HEAD_DIM + 9], own_high[HEAD_DIM + 8 : HEAD_DIM + 9]
+        fifth_top = jnp.max(fifth, axis=0, keepdims=True)
+        new_low = jnp.where(outer, top_low, jnp.maximum(top_low, fifth_top))
+        new_high = jnp.maximum(top_high, jnp.max(fourth, axis=0, keepdims=True))
+        new_high = jnp.where(outer, jnp.maximum(new_high, fifth_top), new_high)
+        fourth = jnp.exp(fourth - new_high).astype(BF)
+        fifth = jnp.exp(fifth - jnp.where(outer, new_high, new_low)).astype(BF)
+        added_high = dot(with_ones(pair[low, vc]), fourth)[: HEAD_DIM + 8]
+        added = dot(with_ones(pair[rows, vc]), fifth)[: HEAD_DIM + 8]
+        mixed_low = own_low[: HEAD_DIM + 8] * jnp.exp(top_low - new_low)
+        mixed_low += jnp.where(outer, 0.0, added)
+        mixed_high = own_high[: HEAD_DIM + 8] * jnp.exp(top_high - new_high)
+        mixed_high += added_high + jnp.where(outer, added, 0.0)
+        for start, mixed, top in ((0, mixed_low, new_low), (block, mixed_high, new_high)):
+            total = mixed[HEAD_DIM : HEAD_DIM + 1]
+            final = mixed[:HEAD_DIM] * (1.0 / total)
+            log_total = top + jnp.log(total)
+            for offset in range(GROUP):
+                head = group * GROUP + offset
+                span = slice(offset * block, (offset + 1) * block)
+                attended[start : start + block, head_cols(head)] = final[:, span].T.astype(BF)
+                logs[head : head + 1, start : start + block] = log_total[:, span]
+
+
+def attend_rest(queries, pair, info, part, recursion):
+    tokens = queries.shape[0]
+    block = tokens // 2
+    return pl.pallas_call(
+        functools.partial(rest_kernel, recursion),
+        out_shape=(shape((tokens, QW), BF), shape((ceil_to(HEADS, 8), tokens), F32)),
+        in_specs=[vmem] * 4,
+        out_specs=(vmem, vmem),
+        scratch_shapes=[
+            pltpu.VMEM(info.shape[::-1], F32),
+            pltpu.VMEM((2, block, block), F32),
+        ],
+        compiler_params=params(40),
+        name="attend_rest",
+    )(queries, pair, info, part)
+
+
+def flat_row(ref, cols, group):
+    heads = range(group * GROUP, (group + 1) * GROUP)
+    return jnp.concatenate([ref[head : head + 1, cols] for head in heads], axis=1)
+
+
+def block_back(key, value, query, grad_mixed, bias, log_total, delta):
+    probs = jnp.exp(dot(key, query, NT) + thrice(bias) - log_total)
+    grad_scores = (probs * (dot(value, grad_mixed, NT) - delta)).astype(BF)
+    grad_value = dot(probs.astype(BF), grad_mixed)
+    grad_key = dot(grad_scores, query)
+    return dot(key.T, grad_scores), grad_key, grad_value
+
+
+def rest_back_kernel(
+    recursion, queries, pair, info, attended, logs, grad, grad_pair, part, deltas, columns, bias
+):
+    block = queries.shape[0] // 2
+    wide = GROUP * block
+    columns[...] = info[...].T
+    outer, rows = rest_rows(block)
+    fifth = jnp.where(outer, 1, 0)
+    block_bias(info, bias, 0, 2, 1, recursion, columns, False)
+    block_bias(info, bias, 1, 2 + fifth, fifth, recursion, columns, False)
+    low, high = slice(0, block), slice(block, 2 * block)
+    product = (attended[...].astype(F32) * grad[...].astype(F32)).T
+    deltas[...] = jnp.zeros(deltas.shape, F32)
+    for head in range(HEADS):
+        deltas[head : head + 1, :] = jnp.sum(product[head_cols(head)], axis=0, keepdims=True)
+    for group in range(KV_HEADS):
+        kc, vc = head_cols(group), head_cols(KV_HEADS + group)
+        query_high, key_high, value_high = block_back(
+            pair[low, kc], pair[low, vc], tall_heads(queries, high, group),
+            tall_heads(grad, high, group), bias[0], flat_row(logs, high, group),
+            flat_row(deltas, high, group),
+        )
+        query, key, value = block_back(
+            pair[rows, kc], pair[rows, vc], tall_heads(queries, rows, group),
+            tall_heads(grad, rows, group), bias[1], flat_row(logs, rows, group),
+            flat_row(deltas, rows, group),
+        )
+        part[group, :, :wide] = jnp.where(outer, 0.0, query)
+        part[group, :, wide:] = query_high + jnp.where(outer, query, 0.0)
+        grad_pair[low, kc] = (key_high + jnp.where(outer, 0.0, key)).astype(BF)
+        grad_pair[low, vc] = (value_high + jnp.where(outer, 0.0, value)).astype(BF)
+        grad_pair[high, kc] = jnp.where(outer, key, 0.0).astype(BF)
+        grad_pair[high, vc] = jnp.where(outer, value, 0.0).astype(BF)
+
+
+def attend_rest_back(queries, pair, info, attended, logs, grad, recursion):
+    tokens = queries.shape[0]
+    block = tokens // 2
+    return pl.pallas_call(
+        functools.partial(rest_back_kernel, recursion),
+        out_shape=(
+            shape((tokens, 2 * KW), BF),
+            shape((KV_HEADS, HEAD_DIM, GROUP * tokens), F32),
+            shape(logs.shape, F32),
+        ),
+        in_specs=[vmem] * 6,
+        out_specs=(vmem,) * 3,
+        scratch_shapes=[
+            pltpu.VMEM(info.shape[::-1], F32),
+            pltpu.VMEM((2, block, block), F32),
+        ],
+        compiler_params=params(48),
+        name="attend_rest_back",
+    )(queries, pair, info, attended, logs, grad)
+
+
+def own_back_kernel(
+    recursion, queries, pair, info, logs, deltas, grad, part, grad_queries, grad_pair, columns, bias
+):
+    block = queries.shape[0] // 2
+    wide = GROUP * block
+    columns[...] = info[...].T
+    block_bias(info, bias, 0, 0, 0, recursion, columns, True)
+    block_bias(info, bias, 1, 0, 1, recursion, columns, False)
+    block_bias(info, bias, 2, 1, 1, recursion, columns, True)
+    low, high = slice(0, block), slice(block, 2 * block)
+    for group in range(KV_HEADS):
+        kc, vc = head_cols(group), head_cols(KV_HEADS + group)
+        made = []
+        for index, keys, side in ((0, low, low), (1, low, high), (2, high, high)):
+            made.append(
+                block_back(
+                    pair[keys, kc], pair[keys, vc], tall_heads(queries, side, group),
+                    tall_heads(grad, side, group), bias[index], flat_row(logs, side, group),
+                    flat_row(deltas, side, group),
+                )
+            )
+        first, second, third = made
+        grad_pair[low, kc] = first[1] + second[1]
+        grad_pair[low, vc] = first[2] + second[2]
+        grad_pair[high, kc] = third[1]
+        grad_pair[high, vc] = third[2]
+        query_low = (part[group, :, :wide] + first[0]) * HEAD_DIM**-0.5
+        query_high = (part[group, :, wide:] + second[0] + third[0]) * HEAD_DIM**-0.5
+        for start, made_query in ((0, query_low), (block, query_high)):
+            for offset in range(GROUP):
+                head = group * GROUP + offset
+                span = slice(offset * block, (offset + 1) * block)
+                grad_queries[start : start + block, head_cols(head)] = made_query[:, span].T
+
+
+def attend_own_back(queries, pair, info, logs, deltas, grad, part, recursion):
+    tokens = queries.shape[0]
+    block = tokens // 2
+    return pl.pallas_call(
+        functools.partial(own_back_kernel, recursion),
+        out_shape=(shape((tokens, QW), F32), shape((tokens, 2 * KW), F32)),
+        in_specs=[vmem] * 7,
+        out_specs=(vmem,) * 2,
+        scratch_shapes=[
+            pltpu.VMEM(info.shape[::-1], F32),
+            pltpu.VMEM((3, block, block), F32),
+        ],
+        compiler_params=params(48),
+        name="attend_own_back",
+    )(queries, pair, info, logs, deltas, grad, part)
+
+
 def post_kernel(
     shift, state, attended, out_w, gain, router, active, gate_w, up_w, down_w,
     state_out, normed, gate_out, up_out, hidden_out, midway_out, update_out, routed,
@@ -263,7 +524,7 @@
     chunk = pl.BlockSpec((1, tokens, part), lambda f: (f, 0, 0))
     weight = pl.BlockSpec((1, width, part), lambda f: (f, 0, 0))
     row = whole(tokens, width)
-    return pl.pallas_call(
+    made = pl.pallas_call(
         functools.partial(post_kernel, shift),
         grid=(pieces,),
         out_shape=(
@@ -286,6 +547,8 @@
         compiler_params=params(48),
         name="post",
     )(state, attended, out_w, gain, router, active, gate_w, up_w, down_w)
+    names = ("state_out", "ffn_in", "gate", "up", "hidden", "midway", "update", "routed")
+    return dict(zip(names, made))
 
 
 def post_back_kernel(
@@ -340,10 +603,8 @@
         grad_attended[...] = grad.astype(BF)
 
 
-def post_back(
-    grad_state, update, routed, active, state, midway, gain, router, out_w, gate_pre, up_pre,
-    gate_w, up_w, down_w, shift,
-):
+def post_back(grad_state, s, gain, router, out_w, gate_w, up_w, down_w, shift):
+    state = s["state"]
     tokens, width = state.shape
     pieces, _, part = gate_w.shape
     cols = down_w.shape[2]
@@ -355,7 +616,7 @@
     weight = pl.BlockSpec((1, width, part), lambda f: (f, 0, 0))
     row, thin, line = whole(tokens, width), whole(tokens, LANE), whole(1, width)
     branch_dims = (pieces, tokens, out_w.shape[2])
-    return pl.pallas_call(
+    made = pl.pallas_call(
         functools.partial(post_back_kernel, shift),
         grid=(pieces,),
         out_shape=(
@@ -383,8 +644,13 @@
         ],
         compiler_params=params(48),
         name="post_back",
-    )(grad_state, update, routed, active, state, midway, gain, router, out_w, gate_pre, up_pre,
-      gate_w, up_w, down_w)
+    )(grad_state, s["update"], s["routed"], s["active"], state, s["midway"], gain, router, out_w,
+      s["gate"], s["up"], gate_w, up_w, down_w)
+    names = (
+        "grad_ffn", "grad_gate", "grad_up", "grad_branch", "grad_attended", "partial",
+        "ffn_gain_grad", "router_grad",
+    )
+    return dict(zip(names, made))
 
 
 def pre_back_kernel(cols, blocks, *refs):
@@ -664,15 +930,26 @@
     )(*parts)
 
 
-def reduce_kernel(count, layers, *refs):
-    ins, outs = refs[:count], refs[count : 2 * count]
-    held, core_in, first_in, second_in, done, z_in = (
-        refs[(2 + i) * count : (3 + i) * count] for i in range(6)
+def finish_kernel(layers, count, low_col, *refs):
+    refs = list(refs)
+
+    def pop(size):
+        taken = refs[:size]
+        del refs[:size]
+        return taken
+
+    normed, packed, attended, branch, ffn_in, grad_gate, grad_up, hidden, grad_ffn = (
+        pop(count) for _ in range(9)
     )
-    send, recv, keep = refs[8 * count :]
+    (small,) = pop(1)
+    outs = pop(5)
+    held, core_in, first_in, second_in, done, z_in = (pop(5) for _ in range(6))
+    raw, left, right, ffn_right, stage, down_stage = pop(6)
+    send, recv, keep, load = refs
     here = Place(layers)
     here.greet()
     y, x, z, core = here.y, here.x, here.z, here.core
+    tokens = raw.shape[0] // count
     sent = []
 
     def slot(a, index):
@@ -692,75 +969,247 @@
     def added(ref, one, two):
         return (one.astype(F32) + two.astype(F32)).astype(ref.dtype)
 
-    loads = [[None] * layers for _ in range(count)]
-    for k in range(layers):
-        for a in range(count):
-            start(a, k, ins[a].at[:, :, layer(k), 1 - core], core_in[a].at[k], here.sibling)
-            loads[a][k] = pltpu.make_async_copy(
-                ins[a].at[:, :, layer(k), core], held[a].at[k], keep.at[a, k]
+    def load_left(index, sources):
+        return [
+            pltpu.make_async_copy(ref, raw.at[pl.ds(i * tokens, tokens)], load.at[index, i])
+            for i, ref in enumerate(sources)
+        ]
+
+    def load_right(index, spot, sources, piece, start_col):
+        width = sources[0].shape[2]
+        return [
+            pltpu.make_async_copy(
+                ref.at[piece],
+                right.at[spot, pl.ds(i * tokens, tokens), pl.ds(start_col, width)],
+                load.at[index + spot, i],
             )
-            loads[a][k].start()
-
-    def first(k):
-        for a in range(count):
-            loads[a][k].wait()
-            arrive(a, k, core_in[a].at[k])
+            for i, ref in enumerate(sources)
+        ]
+
+    def go(copies):
+        for copy in copies:
+            copy.start()
+
+    def hold(copies):
+        for copy in copies:
+            copy.wait()
+
+    def turn_left(spot):
+        for i in range(count):
+            rows = slice(i * tokens, (i + 1) * tokens)
+            left[spot, :, rows] = raw[rows].T
+
+    def sends(a, piece, source):
+        if a == 3:
+            theirs = source.at[:, :, 1 - core]
+            ours = source.at[:, :, core]
+            spot = (piece,)
+        else:
+            theirs = source.at[:, 1 - core]
+            ours = source.at[:, core]
+            spot = (slice(None), lax.div(piece, 2), lax.rem(piece, 2))
+        return (
+            remote(
+                theirs, core_in[a].at[spot], (send.at[a, piece], recv.at[a, piece]), here.sibling
+            ),
+            pltpu.make_async_copy(ours, held[a].at[spot], keep.at[a, piece]),
+        )
+
+    def products(a, fetch, multiply, stages):
+        go(fetch(0, 0))
+
+        def step(piece, carry):
+            spot = lax.rem(piece, 2)
+            hold(fetch(piece, spot))
+
+            @pl.when(piece < 3)
+            def _():
+                go(fetch(piece + 1, 1 - spot))
+
+            @pl.when(piece >= 2)
+            def _():
+                out, own = sends(a, piece - 2, stages.at[spot])
+                out.wait_send()
+                own.wait()
+
+            multiply(piece, spot)
+            for copy in sends(a, piece, stages.at[spot]):
+                copy.start()
+            return carry
+
+        lax.fori_loop(0, 4, step, 0)
+        for piece in (2, 3):
+            out, own = sends(a, piece, stages.at[piece % 2])
+            out.wait_send()
+            own.wait()
+
+    def store(spot, result):
+        rows = stage.shape[3]
+        for index in range(2 * layers):
+            stage[spot, index // 2, index % 2] = result[index * rows : (index + 1) * rows].astype(BF)
+
+    def ffn_product(which):
+        def multiply(piece, spot):
+            width = which[0].shape[2]
+            store(spot, dot(left[0], right[spot, :, :width]))
+
+        return multiply
+
+    high_col = packed[0].shape[2]
+    far_col = branch[0].shape[2]
+
+    def attn_product(piece, spot):
+        first = dot(left[1], right[spot, :, :high_col])
+        second = dot(left[0], right[spot, :, high_col : high_col + far_col])
+        cut = high_col - low_col
+        store(
+            spot,
+            jnp.concatenate(
+                [first[:, :low_col], first[:, low_col:] + second[:, :cut], second[:, cut:]], axis=1
+            ),
+        )
+
+    def down_product(piece, spot):
+        part = hidden[0].shape[2]
+        turned = jnp.concatenate(
+            [right[spot, i * tokens : (i + 1) * tokens, :part].T for i in range(count)], axis=1
+        )
+        rows = part // 2
+        for column in range(4):
+            result = dot(turned, ffn_right[column]).astype(BF)
+            for index in range(2):
+                down_stage[spot, column // 2, column % 2, index] = result[
+                    index * rows : (index + 1) * rows
+                ]
+
+    def first(a):
+        if a < 4:
+            for piece in range(4):
+                spot = (piece,) if a == 3 else (slice(None), piece // 2, piece % 2)
+                arrive(a, piece, core_in[a].at[spot])
+        else:
+            arrive(a, 0, core_in[a])
+        for k in range(layers):
             held[a][k] = added(held[a], held[a][k], core_in[a][k])
-            if a % 2 == 0:
-                start(a, layers + k, held[a].at[k, :, 1 - x], first_in[a].at[k], here.over_x)
+        for k in range(layers):
+            if k % 2 == 0:
+                start(a, 4 + k, held[a].at[layer(k), :, 1 - x], first_in[a].at[k], here.over_x)
             else:
-                start(a, layers + k, held[a].at[k, 1 - y], first_in[a].at[k], here.over_y)
-
-    def second(k):
-        for a in range(count):
-            arrive(a, layers + k, first_in[a].at[k])
+                start(a, 4 + k, held[a].at[layer(k), 1 - y], first_in[a].at[k], here.over_y)
+
+    def second(a):
+        for k in range(layers):
+            at = layer(k)
+            arrive(a, 4 + k, first_in[a].at[k])
             for i in range(2):
-                if a % 2 == 0:
-                    held[a][k, i, x] = added(held[a], held[a][k, i, x], first_in[a][k, i])
+                if k % 2 == 0:
+                    held[a][at, i, x] = added(held[a], held[a][at, i, x], first_in[a][k, i])
                 else:
-                    held[a][k, y, i] = added(held[a], held[a][k, y, i], first_in[a][k, i])
-            if a % 2 == 0:
-                start(a, 2 * layers + k, held[a].at[k, 1 - y, x], second_in[a].at[k], here.over_y)
+                    held[a][at, y, i] = added(held[a], held[a][at, y, i], first_in[a][k, i])
+            index = 4 + layers + k
+            if k % 2 == 0:
+                start(a, index, held[a].at[at, 1 - y, x], second_in[a].at[k], here.over_y)
             else:
-                start(a, 2 * layers + k, held[a].at[k, y, 1 - x], second_in[a].at[k], here.over_x)
-
-    def third(k):
-        for a in range(count):
-            arrive(a, 2 * layers + k, second_in[a].at[k])
-            done[a][k] = added(held[a], held[a][k, y, x], second_in[a][k])
+                start(a, index, held[a].at[at, y, 1 - x], second_in[a].at[k], here.over_x)
+
+    def third(a):
+        for k in range(layers):
+            arrive(a, 4 + layers + k, second_in[a].at[k])
+            done[a][k] = added(held[a], held[a][layer(k), y, x], second_in[a][k])
             if k < layers - 1:
-                start(a, 3 * layers + k, done[a].at[k], z_in[a].at[k], here.up[k + 1])
-
-    for k in range(layers + 2):
-        if k < layers:
-            first(k)
-        if 1 <= k <= layers:
-            second(k - 1)
-        if k >= 2:
-            third(k - 2)
-    for a in range(count):
+                index = 4 + 2 * layers + k
+                start(a, index, done[a].at[k], z_in[a].at[k], here.up[k + 1])
+
+    def fourth(a):
         total = done[a][layers - 1].astype(F32)
         for k in range(layers - 1):
-            arrive(a, 3 * layers + k, z_in[a].at[k])
+            arrive(a, 4 + 2 * layers + k, z_in[a].at[k])
             total = total + z_in[a][k].astype(F32)
         outs[a][...] = total
+
+    start(4, 0, small.at[:, 1 - core], core_in[4], here.sibling)
+    small_own = pltpu.make_async_copy(small.at[:, core], held[4], keep.at[4, 0])
+    small_own.start()
+    ffn_left = load_left(0, ffn_in)
+    go(ffn_left)
+    down_right = [
+        pltpu.make_async_copy(
+            ref.at[column],
+            ffn_right.at[column, pl.ds(i * tokens, tokens)],
+            load.at[6 + column, i],
+        )
+        for i, ref in enumerate(grad_ffn)
+        for column in range(4)
+    ]
+
+    def fetch_of(index, sources):
+        return lambda piece, spot: load_right(index, spot, sources, piece, 0)
+
+    def fetch_attn(piece, spot):
+        return load_right(2, spot, packed, piece, 0) + load_right(4, spot, branch, piece, high_col)
+
+    hold(ffn_left)
+    turn_left(0)
+    normed_left = load_left(1, normed)
+    go(normed_left)
+    go(down_right)
+    products(0, fetch_of(2, grad_gate), ffn_product(grad_gate), stage)
+    first(0)
+    hold(normed_left)
+    turn_left(1)
+    attended_left = load_left(0, attended)
+    go(attended_left)
+    products(1, fetch_of(2, grad_up), ffn_product(grad_up), stage)
+    first(1)
+    second(0)
+    hold(attended_left)
+    turn_left(0)
+    products(2, fetch_attn, attn_product, stage)
+    first(2)
+    second(1)
+    third(0)
+    hold(down_right)
+    products(3, fetch_of(2, hidden), down_product, down_stage)
+    first(3)
+    small_own.wait()
+    first(4)
+    second(2)
+    third(1)
+    second(3)
+    second(4)
+    third(2)
+    third(3)
+    third(4)
+    for a in range(5):
+        fourth(a)
     for copy in sent:
         copy.wait_send()
 
 
-def reduce_all(parts):
-    count = len(parts)
-    layers = parts[0].shape[2]
+def finish(normed, packed, attended, branch, ffn_in, grad_gate, grad_up, hidden, grad_ffn, small, low_col):
+    count = len(normed)
+    tokens, width = normed[0].shape
+    pieces, _, part = hidden[0].shape
+    cols = grad_ffn[0].shape[2]
+    layers = small.shape[0]
+    ranks = 2 * layers
     anywhere = pl.BlockSpec(memory_space=pl.ANY)
+    rows, down_rows = width // ranks, pieces * part // ranks
+    wide = packed[0].shape[2] + branch[0].shape[2]
+    ends = [(rows, part), (rows, part), (rows, part), (down_rows, cols), small.shape[4:]]
+    types = [BF] * 4 + [F32]
 
     def buffers(*lead):
-        return [pltpu.VMEM(lead + part.shape[4:], part.dtype) for part in parts]
-
+        return [pltpu.VMEM(lead + end, dtype) for end, dtype in zip(ends, types)]
+
+    operands = (
+        *normed, *packed, *attended, *branch, *ffn_in, *grad_gate, *grad_up, *hidden, *grad_ffn, small,
+    )
     return pl.pallas_call(
-        functools.partial(reduce_kernel, count, layers),
-        out_shape=tuple(shape(part.shape[4:], F32) for part in parts),
-        in_specs=[anywhere] * count,
-        out_specs=(vmem,) * count,
+        functools.partial(finish_kernel, layers, count, low_col),
+        out_shape=tuple(shape(end, F32) for end in ends),
+        in_specs=[anywhere] * len(operands),
+        out_specs=(vmem,) * 5,
         scratch_shapes=[
             *buffers(layers, 2, 2),
             *buffers(layers, 2, 2),
@@ -768,21 +1217,27 @@
             *buffers(layers),
             *buffers(layers),
             *buffers(layers - 1),
-            pltpu.SemaphoreType.DMA((count, 4 * layers)),
-            pltpu.SemaphoreType.DMA((count, 4 * layers)),
-            pltpu.SemaphoreType.DMA((count, layers)),
+            pltpu.VMEM((count * tokens, width), BF),
+            pltpu.VMEM((2, width, count * tokens), BF),
+            pltpu.VMEM((2, count * tokens, max(wide, part)), BF),
+            pltpu.VMEM((pieces, count * tokens, cols), BF),
+            pltpu.VMEM((2, layers, 2, rows, part), BF),
+            pltpu.VMEM((2, 2, 2, 2, down_rows, cols), BF),
+            pltpu.SemaphoreType.DMA((5, 4 + 3 * layers)),
+            pltpu.SemaphoreType.DMA((5, 4 + 3 * layers)),
+            pltpu.SemaphoreType.DMA((5, 4)),
+            pltpu.SemaphoreType.DMA((10, count)),
         ],
         compiler_params=pltpu.CompilerParams(
-            collective_id=1, has_side_effects=True, vmem_limit_bytes=56 * MIB
+            collective_id=1, has_side_effects=True, vmem_limit_bytes=61 * MIB
         ),
-        name="reduce_all",
-    )(*parts)
-
-
-def rope_tables(tokens):
+        name="finish",
+    )(*operands)
+
+
+def rope_tables(positions):
     half = HEAD_DIM // 2
     frequency = rope_base ** (-(jnp.arange(half, dtype=F32) * 2.0 / HEAD_DIM))
-    positions = lax.axis_index("seq") * tokens + jnp.arange(tokens, dtype=jnp.int32)
     angles = positions.astype(F32)[:, None] * frequency[None, :]
     cosine, sine = jnp.cos(angles), jnp.sin(angles)
     repeat = LANE // HEAD_DIM
@@ -800,20 +1255,149 @@
     return lax.ppermute(array, "seq", [(i + step, i) for i in range(count - step)])
 
 
+def row_plan(inputs, cotangent, depths, marks, block_params):
+    micros, _, tokens, _ = inputs.shape
+    seq, mine = lax.axis_size("seq"), lax.axis_index("seq")
+    attn_g, ffn_g, routers, qkv_w, out_w, gate_w, up_w, down_w, cols, shift = block_params
+    order = mine - jnp.arange(seq)
+    marks = jnp.where((order >= 0)[:, None, None, None], marks[order % seq], -1.0)
+    marks = marks.transpose(2, 1, 0, 3).reshape(micros, 2, seq * tokens)
+    infos = [jnp.pad(marks[m], ((0, 6), (0, 0))) for m in range(micros)]
+    cosine, sine = rope_tables(mine * tokens + jnp.arange(tokens, dtype=jnp.int32))
+    states = [inputs[m, 0] for m in range(micros)]
+    actives = [
+        [
+            jnp.broadcast_to((depths[m, 0] > r).astype(F32)[:, None], (tokens, LANE))
+            for r in range(RECUR)
+        ]
+        for m in range(micros)
+    ]
+    saved = [[None] * RECUR for _ in range(micros)]
+    for r in range(RECUR):
+        made = []
+        for m in range(micros):
+            normed, queries, pair = pre_part(states[m], attn_g, qkv_w, cosine, sine, cols)
+            pairs = [pair] + [pass_on(pair, step, seq) for step in range(1, seq)]
+            made.append((normed, queries, pairs))
+        for m in range(micros):
+            normed, queries, pairs = made[m]
+            attended, logs = attend(queries, pairs, infos[m], r)
+            after = post_part(
+                states[m], attended, out_w, ffn_g, routers[r], actives[m][r], gate_w, up_w, down_w, shift
+            )
+            saved[m][r] = dict(
+                after, state=states[m], normed=normed, queries=queries, pairs=pairs,
+                attended=attended, logs=logs, active=actives[m][r],
+            )
+            states[m] = after["state_out"]
+    grads = [cotangent[m, 0] for m in range(micros)]
+    for r in reversed(range(RECUR)):
+        partials = []
+        for m in range(micros):
+            s = saved[m][r]
+            s.update(post_back(grads[m], s, ffn_g, routers[r], out_w, gate_w, up_w, down_w, shift))
+            grad_queries, *grad_pairs = attend_back(
+                s["queries"], s["pairs"], infos[m], s["attended"], s["logs"], s["grad_attended"], r
+            )
+            grad_pairs = [grad_pairs[0]] + [
+                pass_back(grad_pairs[step], step, seq) for step in range(1, seq)
+            ]
+            partials.append((grad_queries, grad_pairs))
+        for m in range(micros):
+            s = saved[m][r]
+            s["packed"], grads[m], s["attn_gain_grad"] = pre_back(
+                *partials[m], s["partial"], s["state"], attn_g, qkv_w, cosine, sine, cols
+            )
+    outputs = jnp.stack(states, axis=0)[:, None]
+    input_grad = jnp.stack(grads, axis=0)[:, None]
+    return outputs, input_grad, saved
+
+
+def swap(array, pairs):
+    return lax.ppermute(array, "seq", [(a, b) for a, b in pairs] + [(b, a) for a, b in pairs])
+
+
+ACROSS = ((0, 3), (1, 2))
+PARTNERS = ((0, 1), (2, 3))
+
+
+def paired_plan(inputs, cotangent, marks, block_params):
+    tokens = inputs.shape[2]
+    mine = lax.axis_index("seq")
+    late = mine >= 2
+    outer = is_outer()
+    attn_g, ffn_g, routers, qkv_w, out_w, gate_w, up_w, down_w, cols, shift = block_params
+
+    def take(array):
+        own = jnp.where(late, array[1, 0], array[0, 0])
+        other = swap(jnp.where(late, array[0, 0], array[1, 0]).astype(BF), ACROSS).astype(F32)
+        return jnp.concatenate(
+            [jnp.where(late, other, own), jnp.where(late, own, other)], axis=0
+        )
+
+    def give(array):
+        low, high = array[:tokens], array[tokens:]
+        own = jnp.where(late, high, low)
+        other = swap(jnp.where(late, low, high).astype(BF), ACROSS).astype(F32)
+        return jnp.stack([jnp.where(late, other, own), jnp.where(late, own, other)], axis=0)[:, None]
+
+    blocks = jnp.where(outer, jnp.array([0, 3, 1, 2]), jnp.array([1, 2, 0, 3]))
+    info = jnp.where(late, marks[:, :, 1], marks[:, :, 0])[blocks]
+    info = jnp.pad(info.transpose(1, 0, 2).reshape(2, -1), ((0, 6), (0, 0)))
+    depth = info[1, : 2 * tokens]
+    places = jnp.arange(tokens, dtype=jnp.int32)
+    cosine, sine = rope_tables(
+        jnp.concatenate([blocks[0] * tokens + places, blocks[1] * tokens + places])
+    )
+    state = take(inputs)
+    cotangent, depth = lax.optimization_barrier((cotangent, depth))
+    grad = take(cotangent)
+    saved = []
+    for r in range(RECUR):
+        active = jnp.broadcast_to((depth > r).astype(F32)[:, None], (2 * tokens, LANE))
+        normed, queries, pair = pre_part(state, attn_g, qkv_w, cosine, sine, cols)
+        partner = swap(pair, PARTNERS)
+        part = attend_own(queries, pair, info, r)
+        attended, logs = attend_rest(queries, partner, info, part, r)
+        after = post_part(
+            state, attended, out_w, ffn_g, routers[r], active, gate_w, up_w, down_w, shift
+        )
+        saved.append(
+            dict(
+                after, state=state, normed=normed, queries=queries, pair=pair, partner=partner,
+                attended=attended, logs=logs, active=active,
+            )
+        )
+        state = after["state_out"]
+    outputs = give(state)
+    for r in reversed(range(RECUR)):
+        s = saved[r]
+        s.update(post_back(grad, s, ffn_g, routers[r], out_w, gate_w, up_w, down_w, shift))
+        grad_partner, part, deltas = attend_rest_back(
+            s["queries"], s["partner"], info, s["attended"], s["logs"], s["grad_attended"], r
+        )
+        grad_partner = swap(grad_partner, PARTNERS)
+        grad_queries, grad_pair = attend_own_back(
+            s["queries"], s["pair"], info, s["logs"], deltas, s["grad_attended"], part, r
+        )
+        s["packed"], grad, s["attn_gain_grad"] = pre_back(
+            grad_queries, [grad_pair, grad_partner], s["partial"], s["state"], attn_g, qkv_w,
+            cosine, sine, cols,
+        )
+    return outputs, give(grad), [saved]
+
+
 def local(
     inputs, cotangent, segments, depths, query_weight, key_weight, value_weight, out_weight,
     gate_weight, up_weight, down_weight, attn_gain, ffn_gain, router_weight,
 ):
     micros, _, tokens, width = inputs.shape
     seq, ranks = lax.axis_size("seq"), lax.axis_size("dp")
-    mine = lax.axis_index("seq")
     rows = query_weight.shape[0]
     qc, kc = query_weight.shape[1], key_weight.shape[1]
-    cols = (qc, kc)
+    both = ("seq", "dp")
 
     attn_local = jnp.concatenate([query_weight, key_weight, value_weight, out_weight], axis=1)
-    both = ("seq", "dp")
-
     span = ceil_to(max(rows, tokens), LANE)
     small = jnp.concatenate([attn_gain[None], ffn_gain[None], router_weight.T], axis=0).astype(F32)
     marks = jnp.concatenate([segments[:, 0], depths[:, 0]], axis=0).astype(F32)
@@ -825,7 +1409,7 @@
         axis=0,
     )
     parts = (attn_local, gate_weight, up_weight, down_weight, small)
-    direct = seq == 4 and ranks % 2 == 0
+    direct = micros == 2 and (seq, ranks) == (4, 8)
     if direct:
         gathered = gather_all(parts, ranks // 2)
     else:
@@ -846,102 +1430,50 @@
     shift = used - low_col
     qkv_w, out_w = attn_w[:, :, :high_col], attn_w[:, :, low_col:]
 
-    order = mine - jnp.arange(seq)
-    marks = jnp.where((order >= 0)[:, None, None, None], marks[order % seq], -1.0)
-    marks = marks.transpose(2, 1, 0, 3).reshape(micros, 2, seq * tokens)
-    infos = [jnp.pad(marks[m], ((0, 6), (0, 0))) for m in range(micros)]
-    cosine, sine = rope_tables(tokens)
-
-    states = [inputs[m, 0] for m in range(micros)]
-    actives = [
-        [
-            jnp.broadcast_to((depths[m, 0] > r).astype(F32)[:, None], (tokens, LANE))
-            for r in range(RECUR)
-        ]
-        for m in range(micros)
-    ]
-    saved = [[None] * RECUR for _ in range(micros)]
-    for r in range(RECUR):
-        made = []
-        for m in range(micros):
-            normed, queries, pair = pre_part(states[m], attn_g, qkv_w, cosine, sine, cols)
-            pairs = [pair] + [pass_on(pair, step, seq) for step in range(1, seq)]
-            made.append((normed, queries, pairs))
-        for m in range(micros):
-            normed, queries, pairs = made[m]
-            attended, logs = attend(queries, pairs, infos[m], r)
-            state_out, ffn_in, gate, up, hidden, midway, update, routed = post_part(
-                states[m], attended, out_w, ffn_g, routers[r], actives[m][r], gate_w, up_w, down_w, shift
-            )
-            saved[m][r] = dict(
-                state=states[m], normed=normed, queries=queries, pairs=pairs, attended=attended,
-                logs=logs, ffn_in=ffn_in, gate=gate, up=up, hidden=hidden, midway=midway,
-                update=update, routed=routed,
-            )
-            states[m] = state_out
-
-    grads = [cotangent[m, 0] for m in range(micros)]
-    attn_gain_sum, ffn_gain_sum, router_sums = 0.0, 0.0, [0.0] * RECUR
-    for r in reversed(range(RECUR)):
-        partials = []
-        for m in range(micros):
-            s = saved[m][r]
-            grad_ffn, grad_gate, grad_up, grad_branch, grad_attended, partial, gain_grad, router_grad = (
-                post_back(
-                    grads[m], s["update"], s["routed"], actives[m][r], s["state"], s["midway"], ffn_g,
-                    routers[r], out_w, s["gate"], s["up"], gate_w, up_w, down_w, shift,
-                )
-            )
-            ffn_gain_sum = ffn_gain_sum + gain_grad
-            router_sums[r] = router_sums[r] + router_grad
-            s.update(grad_ffn=grad_ffn, grad_gate=grad_gate, grad_up=grad_up, grad_branch=grad_branch)
-            grad_queries, *grad_pairs = attend_back(
-                s["queries"], s["pairs"], infos[m], s["attended"], s["logs"], grad_attended, r
-            )
-            grad_pairs = [grad_pairs[0]] + [
-                pass_back(grad_pairs[step], step, seq) for step in range(1, seq)
-            ]
-            partials.append((partial, grad_queries, grad_pairs))
-        for m in range(micros):
-            s = saved[m][r]
-            partial, grad_queries, grad_pairs = partials[m]
-            packed, grads[m], gain_grad = pre_back(
-                grad_queries, grad_pairs, partial, s["state"], attn_g, qkv_w, cosine, sine, cols
-            )
-            attn_gain_sum = attn_gain_sum + gain_grad
-            s.update(packed=packed)
-
-    flat = [saved[m][r] for r in reversed(range(RECUR)) for m in range(micros)]
+    block_params = (
+        attn_g, ffn_g, routers, qkv_w, out_w, gate_w, up_w, down_w, (qc, kc), shift
+    )
+    if direct:
+        outputs, input_grad, saved = paired_plan(inputs, cotangent, marks, block_params)
+    else:
+        outputs, input_grad, saved = row_plan(inputs, cotangent, depths, marks, block_params)
+    flat = [steps[r] for r in reversed(range(RECUR)) for steps in saved]
 
     def every(name):
         return [s[name] for s in flat]
 
-    down_sum = down_sums(every("hidden"), every("grad_ffn"))
-    gate_sum, up_sum = pair_sums(every("ffn_in"), every("grad_gate"), every("grad_up"))
-    attn_sum = attn_sums(
-        every("normed"), every("packed"), every("attended"), every("grad_branch"), low_col, total_cols
-    )
-
+    attn_gain_sum, ffn_gain_sum = sum(every("attn_gain_grad")), sum(every("ffn_gain_grad"))
+    router_sums = [sum(steps[r]["router_grad"] for steps in saved) for r in range(RECUR)]
     small_sum = jnp.concatenate([attn_gain_sum, ffn_gain_sum, *router_sums], axis=0)
     small_sum = small_sum.reshape(2 + RECUR, ranks, rows).transpose(1, 0, 2)
     small_sum = jnp.pad(
         small_sum, ((0, 0), (0, 8 - small_sum.shape[1]), (0, ceil_to(rows, LANE) - rows))
     )
-    small_sum = jnp.broadcast_to(small_sum[None], (seq,) + small_sum.shape)
-    sums = [
-        part.reshape(seq, ranks, -1, part.shape[-1])
-        for part in (attn_sum, gate_sum, up_sum, down_sum, small_sum)
-    ]
     if direct:
-        sums = reduce_all([part.reshape(2, 2, ranks // 2, 2, *part.shape[2:]) for part in sums])
+        small_sum = small_sum.reshape(ranks // 2, 2, 1, 1, *small_sum.shape[1:])
+        small_sum = jnp.broadcast_to(small_sum, small_sum.shape[:2] + (2, 2) + small_sum.shape[4:])
+        gate_grad, up_grad, attn_grad, down_grad, small_own = finish(
+            every("normed"), every("packed"), every("attended"), every("grad_branch"),
+            every("ffn_in"), every("grad_gate"), every("grad_up"), every("hidden"),
+            every("grad_ffn"), small_sum, low_col,
+        )
     else:
+        down_sum = down_sums(every("hidden"), every("grad_ffn"))
+        gate_sum, up_sum = pair_sums(every("ffn_in"), every("grad_gate"), every("grad_up"))
+        attn_sum = attn_sums(
+            every("normed"), every("packed"), every("attended"), every("grad_branch"),
+            low_col, total_cols,
+        )
+        small_sum = jnp.broadcast_to(small_sum[None], (seq,) + small_sum.shape)
+        sums = [
+            part.reshape(seq, ranks, -1, part.shape[-1])
+            for part in (gate_sum, up_sum, attn_sum, down_sum, small_sum)
+        ]
         sums = [lax.psum_scatter(part, "seq", scatter_dimension=0) for part in sums]
         sums = [lax.psum_scatter(part, "dp", scatter_dimension=0).astype(F32) for part in sums]
-    attn_grad, gate_grad, up_grad, down_grad, small_own = sums
+        gate_grad, up_grad, attn_grad, down_grad, small_own = sums
     small_own = small_own[: 2 + RECUR, :rows]
 
-    outputs = jnp.stack(states, axis=0)[:, None]
-    input_grad = jnp.stack(grads, axis=0)[:, None]
     return (
         outputs,
         input_grad,

time: 825 us -> 670 us (0.81)
  Pallas kernels: 611 us -> 520 us
  starting transfers between devices: 64.9 us -> 12.1 us
  local copies, waits for them, and re-layouts: 116 us -> 91.6 us
  other arithmetic: 6.13 us -> 19.1 us
    pallas_call x16 -> x13, Pallas kernels: 297 us -> 236 us  [the longest x1 141 us: finish(): pl.pallas_call(functools.partial(finish_kernel, layers, count, low_col),...]
    ppermute x36 -> x10, starting transfers between devices: 64.9 us -> 12.1 us  [swap(): lax.ppermute(array, 'seq', [(a, b) for a, b in pairs] + [(b, a) for a, b...]
    unnamed x396 -> x232, local copies, waits for them, and re-layouts: 97 us -> 56.3 us
    pallas_call x6 -> x3, Pallas kernels: 74.7 us -> 61.5 us  [post_part(): pl.pallas_call(functools.partial(post_kernel, shift), grid=(pieces,), out...]
    optimization_barrier x0 -> x1, local copies, waits for them, and re-layouts: none -> 12.1 us  [paired_plan(): cotangent, depth = lax.optimization_barrier((cotangent, depth))]
    pallas_call x6 -> x3, Pallas kernels: 93.1 us -> 83.3 us  [post_back(): pl.pallas_call(functools.partial(post_back_kernel, shift), grid=(pieces,)...]
    pallas_call x6 -> x3, Pallas kernels: 20 us -> 19.3 us  [pre_back(): pl.pallas_call(functools.partial(pre_back_kernel, cols, len(grad_pairs)),...]
  transfers between devices with their start and end apart: 36 -> 10, of which waited for: 1 -> 4; matrix products, arithmetic and copies ran while one was open for 2% -> 8% of each run, Pallas kernels for 43% -> 57%
where the time goes in v3:
time: 670 us; the launch traced here: 660 us
  Pallas kernels  520 us (78%)
  local copies, waits for them, and re-layouts  91.6 us (14%)
  other arithmetic  19.1 us (3%)
  waiting for transfers between devices  13.4 us (2%)
  starting transfers between devices  12.1 us (2%)
    pallas_call x1, Pallas kernels, finish(): pl.pallas_call(functools.partial(finish_kernel, layers, count, low_col),...  141 us
    pallas_call x1, Pallas kernels, gather_all(): pl.pallas_call(functools.partial(gather_kernel, count, layers), out_shape...  107 us
    pallas_call x3, Pallas kernels, post_back(): pl.pallas_call(functools.partial(post_back_kernel, shift), grid=(pieces,)...  83.3 us
    pallas_call x3, Pallas kernels, post_part(): pl.pallas_call(functools.partial(post_kernel, shift), grid=(pieces,), out...  61.5 us
    unnamed x232, local copies, waits for them, and re-layouts  56.3 us
    pallas_call x3, Pallas kernels, attend_own_back(): pl.pallas_call(functools.partial(own_back_kernel, recursion), out_shape=(...  34.2 us
    pallas_call x3, Pallas kernels, attend_rest_back(): pl.pallas_call(functools.partial(rest_back_kernel, recursion), out_shape=...  25.9 us
    pallas_call x3, Pallas kernels, pre_back(): pl.pallas_call(functools.partial(pre_back_kernel, cols, len(grad_pairs)),...  19.3 us
  transfers between devices with their start and end apart: 10, of which 4 were waited for; matrix products, arithmetic and copies ran while one was open for 8% of the time, Pallas kernels for 57%

profile of v3, /device:TPU:0, one launch (start us, length us, event | category | flops | bytes accessed | tf_op | source)
XLA Modules:
  0.0 659.8 jit_solution(7385464383295803949)
XLA Ops:
  4.2 3.9 collective-permute-start
  9.8 106.8 %gather_all.1 = (bf16[2,2,4,2,120,640]{5,4,3,2,1,0:T(8,128)(2,1)}, bf16[2,2,4,2,120,640]{5,4,3,2,1,0:T(8,128)(2,1)}, bf16[2,2,4,2,120,640]{5,4,3,2,1,0:T(8,128)(...) custom-call(bf16[120,640]{1,0:T(8,128)(2,1)} %pad_maximum_fusion.4.refs_0_, ...), custom_call_target="tpu_custom_call" | custom-call | tf_op jit(solution)/shard_map/gather_all/pallas_call | solution.py:918
  122.5 4.3 slice.149.weight.refs_6_
  133.9 4.6 pre.3
  146.2 5.7 attend_own.3.part
  151.9 5.1 collective-permute-done.1.pair
  157.0 6.1 attend_rest.3
  163.8 20.5 %post.3 = (f32[512,960]{1,0:T(8,128)}, bf16[512,960]{1,0:T(8,128)(2,1)S(1)}, bf16[4,512,640]{2,1,0:T(8,128)(2,1)}, bf16[4,512,640]{2,1,0:T(8,128)(2,1)}, bf16[4,...) custom-call(f32[512,960]{1,0:T(8,128)} %copy-done.3, ...), custom_call_target="tpu_custom_call" | custom-call | tf_op jit(solution)/shard_map/post/pallas_call | solution.py:527
  186.4 4.5 pre.4
  193.5 12.1 %copy.76 = f32[2,1,256,960]{3,2,1,0:T(8,128)} copy(f32[2,1,256,960]{2,3,1,0:T(8,128)} %param.17) | data formatting | bytes 3932160 | tf_op jit(solution)/shard_map/optimization_barrier | solution.py:1353
  213.7 5.4 attend_own.4.part
  219.1 6.1 attend_rest.4
  226.0 20.8 %post.4 = (f32[512,960]{1,0:T(8,128)}, bf16[512,960]{1,0:T(8,128)(2,1)S(1)}, bf16[4,512,640]{2,1,0:T(8,128)(2,1)}, bf16[4,512,640]{2,1,0:T(8,128)(2,1)}, bf16[4,...) custom-call(f32[512,960]{1,0:T(8,128)} %get-tuple-element.120.state.refs_4_, ...), custom_call_target="tpu_custom_call" | custom-call | tf_op jit(solution)/shard_map/post/pallas_call | solution.py:527
  248.9 4.5 pre.5
  260.8 5.4 attend_own.5.part
  266.3 5.2 collective-permute-done.3.pair
  271.5 6.2 attend_rest.5
  277.9 20.2 %post.5 = (f32[512,960]{1,0:T(8,128)}, bf16[512,960]{1,0:T(8,128)(2,1)S(1)}, bf16[4,512,640]{2,1,0:T(8,128)(2,1)}, bf16[4,512,640]{2,1,0:T(8,128)(2,1)}, bf16[4,...) custom-call(f32[512,960]{1,0:T(8,128)} %get-tuple-element.124.state.refs_4_, ...), custom_call_target="tpu_custom_call" | custom-call | tf_op jit(solution)/shard_map/post/pallas_call | solution.py:527
  299.1 27.5 %post_back.3 = (bf16[4,512,240]{2,1,0:T(8,128)(2,1)S(1)}, bf16[4,512,640]{2,1,0:T(8,128)(2,1)}, bf16[4,512,640]{2,1,0:T(8,128)(2,1)}, bf16[4,512,256]{2,1,0:T(8,...) custom-call(f32[512,960]{1,0:T(8,128)} %pad_maximum_fusion.1.grad_st, ...), custom_call_target="tpu_custom_call" | custom-call | tf_op jit(solution)/shard_map/post_back/pallas_call | solution.py:619
  328.6 8.4 %attend_rest_back.3 = (bf16[512,640]{1,0:T(8,128)(2,1)}, f32[5,64,1536]{2,1,0:T(8,128)}, f32[16,512]{1,0:T(8,128)S(1)}) custom-call(bf16[512,960]{1,0:T(8,128)(2,1)S(1)} %copy-done.13, bf16[512,640]{1,0:T(8,128)(2,1)} %collective-permute-done.3.pair, f32[8,1024]{1,0:T(8,128)S(1)} %copy-done.21, bf16[512,960]{1,0:T(8,128)(2,1)S(1)} %get-tuple-element.127.attended.refs_6_, ...), custom_call_target="tpu_custom_call" | custom-call | tf_op jit(solution)/shard_map/attend_rest_back/pallas_call | solution.py:404
  339.0 11.6 %attend_own_back.3 = (f32[512,960]{1,0:T(8,128)}, f32[512,640]{1,0:T(8,128)S(1)}) custom-call(bf16[512,960]{1,0:T(8,128)(2,1)S(1)} %copy-done.13, bf16[512,640]{1,0:T(8,128)(2,1)} %get-tuple-element.126.pair, f32[8,1024]{1,0:T(8,128)S(1)} %copy-done.21, f32[16,512]{1,0:T(8,128)S(1)} %get-tuple-element.131.logs, f32[16,512]{1,0:T(8,128)S(1)} %get-tuple-element.139.deltas, ...), custom_call_target="tpu_custom_call" | custom-call | tf_op jit(solution)/shard_map/attend_own_back/pallas_call | solution.py:460
  355.6 6.3 pre_back.3
  365.3 27.7 %post_back.4 = (bf16[4,512,240]{2,1,0:T(8,128)(2,1)S(1)}, bf16[4,512,640]{2,1,0:T(8,128)(2,1)}, bf16[4,512,640]{2,1,0:T(8,128)(2,1)}, bf16[4,512,256]{2,1,0:T(8,...) custom-call(f32[512,960]{1,0:T(8,128)} %copy-done.33, ...), custom_call_target="tpu_custom_call" | custom-call | tf_op jit(solution)/shard_map/post_back/pallas_call | solution.py:619
  395.0 8.6 %attend_rest_back.4 = (bf16[512,640]{1,0:T(8,128)(2,1)}, f32[5,64,1536]{2,1,0:T(8,128)}, f32[16,512]{1,0:T(8,128)S(1)}) custom-call(bf16[512,960]{1,0:T(8,128)(2,1)S(1)} %copy-done.11, bf16[512,640]{1,0:T(8,128)(2,1)} %collective-permute-done.2.pair, f32[8,1024]{1,0:T(8,128)S(1)} %copy-done.21, bf16[512,960]{1,0:T(8,128)(2,1)S(1)} %copy-done.17, ...), custom_call_target="tpu_custom_call" | custom-call | tf_op jit(solution)/shard_map/attend_rest_back/pallas_call | solution.py:404
  407.6 11.4 %attend_own_back.4 = (f32[512,960]{1,0:T(8,128)}, f32[512,640]{1,0:T(8,128)S(1)}) custom-call(bf16[512,960]{1,0:T(8,128)(2,1)S(1)} %copy-done.11, bf16[512,640]{1,0:T(8,128)(2,1)} %get-tuple-element.122.pair, f32[8,1024]{1,0:T(8,128)S(1)} %copy-done.21, f32[16,512]{1,0:T(8,128)S(1)} %copy-done.71, f32[16,512]{1,0:T(8,128)S(1)} %get-tuple-element.152.deltas, ...), custom_call_target="tpu_custom_call" | custom-call | tf_op jit(solution)/shard_map/attend_own_back/pallas_call | solution.py:460
  426.3 6.4 pre_back.4
  435.5 28.1 %post_back.5 = (bf16[4,512,240]{2,1,0:T(8,128)(2,1)S(1)}, bf16[4,512,640]{2,1,0:T(8,128)(2,1)}, bf16[4,512,640]{2,1,0:T(8,128)(2,1)}, bf16[4,512,256]{2,1,0:T(8,...) custom-call(f32[512,960]{1,0:T(8,128)} %copy-done.32, ...), custom_call_target="tpu_custom_call" | custom-call | tf_op jit(solution)/shard_map/post_back/pallas_call | solution.py:619
  465.6 8.9 %attend_rest_back.5 = (bf16[512,640]{1,0:T(8,128)(2,1)}, f32[5,64,1536]{2,1,0:T(8,128)}, f32[16,512]{1,0:T(8,128)S(1)}) custom-call(bf16[512,960]{1,0:T(8,128)(2,1)S(1)} %get-tuple-element.113.queries, bf16[512,640]{1,0:T(8,128)(2,1)} %collective-permute-done.1.pair, f32[8,1024]{1,0:T(8,128)S(1)} %copy-done.21, bf16[512,960]{1,0:T(8,128)(2,1)S(1)} %copy-done.15, ...), custom_call_target="tpu_custom_call" | custom-call | tf_op jit(solution)/shard_map/attend_rest_back/pallas_call | solution.py:404
  477.0 3.1 copy.79
  481.6 11.2 %attend_own_back.5 = (f32[512,960]{1,0:T(8,128)}, f32[512,640]{1,0:T(8,128)S(1)}) custom-call(bf16[512,960]{1,0:T(8,128)(2,1)S(1)} %get-tuple-element.113.queries, bf16[512,640]{1,0:T(8,128)(2,1)} %get-tuple-element.114.pair, f32[8,1024]{1,0:T(8,128)S(1)} %copy-done.22, f32[16,512]{1,0:T(8,128)S(1)} %copy-done.69, f32[16,512]{1,0:T(8,128)S(1)} %get-tuple-element.165.deltas, ...), custom_call_target="tpu_custom_call" | custom-call | tf_op jit(solution)/shard_map/attend_own_back/pallas_call | solution.py:460
  496.4 6.6 pre_back.5
  507.5 140.6 %finish.1 = (f32[120,640]{1,0:T(8,128)}, f32[120,640]{1,0:T(8,128)}, f32[120,640]{1,0:T(8,128)}, f32[320,240]{1,0:T(8,128)}, f32[8,128]{1,0:T(8,128)}) custom-call(bf16[512,960]{1,0:T(8,128)(2,1)} %copy-done.49, bf16[512,960]{1,0:T(8,128)(2,1)} %copy-done.47, bf16[512,960]{1,0:T(8,128)(2,1)} %copy-done.45, bf16[4,512,512]{2,1,0:T(8,128)(2,1)} %copy-done.29, ...), custom_call_target="tpu_custom_call" | custom-call | tf_op jit(solution)/shard_map/finish/pallas_call | solution.py:1208
  (304 shorter events, 102.5 us)
Async XLA Ops:
  3.1 119.4 %copy-start.87 = (f32[1,1,256,960]{3,2,1,0:T(8,128)}, f32[1,1,256,960]{3,2,1,0:T(8,128)S(1)}, u32[]{:S(2)}) copy-start(f32[1,1,256,960]{3,2,1,0:T(8,128)S(1)} %copy.86) | copy-start | bytes 2949124
  3.1 114.9 %copy-start.106 = (s32[4]{0:T(128)S(1)}, s32[4]{0:T(128)}, u32[]{:S(2)}) copy-start(s32[4]{0:T(128)} %constant.47.clone) | copy-start | bytes 52
  3.1 114.9 %copy-start.107 = (s32[4]{0:T(128)S(1)}, s32[4]{0:T(128)}, u32[]{:S(2)}) copy-start(s32[4]{0:T(128)} %constant.48.clone) | copy-start | bytes 52
  4.2 126.1 %collective-permute-start = (bf16[256,960]{1,0:T(8,128)(2,1)}, bf16[256,960]{1,0:T(8,128)(2,1)}, u32[]{:S(2)}, u32[]{:S(2)}) collective-permute-start(bf16[256,960]{1,0:T(8,128)(2,1)} %fusion.4), channel_id=1, source_target_pairs={{0,3},{1,2},{3,0},{2,1},{4,7},{5,6},{7,4},{6,5},{8,11},{9,10},{11,... | collective-permute-start | bytes 1474568 | tf_op jit(solution)/shard_map/ppermute | solution.py:1317
  139.5 17.5 %collective-permute-start.1 = (bf16[512,640]{1,0:T(8,128)(2,1)}, bf16[512,640]{1,0:T(8,128)(2,1)}, u32[]{:S(2)}, u32[]{:S(2)}) collective-permute-start(bf16[512,640]{1,0:T(8,128)(2,1)} %get-tuple-element.114.pair), channel_id=1, source_target_pairs={{0,1},{2,3},{1,0},{3,2},{4,5},{6,7},{5,4},{7,6},{8,9},{10,11},{9,8... | collective-permute-start | bytes 1966088 | tf_op jit(solution)/shard_map/ppermute | solution.py:1317
  163.7 20.6 %copy-start.14 = (bf16[512,960]{1,0:T(8,128)(2,1)}, bf16[512,960]{1,0:T(8,128)(2,1)S(1)}, u32[]{:S(2)}) copy-start(bf16[512,960]{1,0:T(8,128)(2,1)S(1)} %get-tuple-element.115.attended.refs_8_) | copy-start | bytes 2949124
  163.8 20.5 %copy-start.25 = (f32[512,128]{1,0:T(8,128)}, f32[512,128]{1,0:T(8,128)S(1)}, u32[]{:S(2)}) copy-start(f32[512,128]{1,0:T(8,128)S(1)} %broadcast_in_dim.45.active) | copy-start | bytes 786436
  163.8 20.5 %copy-start.1 = (bf16[4,960,512]{2,1,0:T(8,128)(2,1)S(1)}, bf16[4,960,512]{2,1,0:T(8,128)(2,1)}, u32[]{:S(2)}) copy-start(bf16[4,960,512]{2,1,0:T(8,128)(2,1)} %slice.149.weight.refs_6_) | copy-start | bytes 11796484
  192.9 26.2 %collective-permute-start.2 = (bf16[512,640]{1,0:T(8,128)(2,1)}, bf16[512,640]{1,0:T(8,128)(2,1)}, u32[]{:S(2)}, u32[]{:S(2)}) collective-permute-start(bf16[512,640]{1,0:T(8,128)(2,1)} %get-tuple-element.122.pair), channel_id=1, source_target_pairs={{0,1},{2,3},{1,0},{3,2},{4,5},{6,7},{5,4},{7,6},{8,9},{10,11},{9,8... | collective-permute-start | bytes 1966088 | tf_op jit(solution)/shard_map/ppermute | solution.py:1317
  208.1 49.0 %collective-permute-start.5 = (bf16[256,960]{1,0:T(8,128)(2,1)}, bf16[256,960]{1,0:T(8,128)(2,1)}, u32[]{:S(2)}, u32[]{:S(2)}) collective-permute-start(bf16[256,960]{1,0:T(8,128)(2,1)} %fusion.5), channel_id=1, source_target_pairs={{0,3},{1,2},{3,0},{2,1},{4,7},{5,6},{7,4},{6,5},{8,11},{9,10},{11,... | collective-permute-start | bytes 1474568 | tf_op jit(solution)/shard_map/ppermute | solution.py:1317
  225.8 21.0 %copy-start.16 = (bf16[512,960]{1,0:T(8,128)(2,1)}, bf16[512,960]{1,0:T(8,128)(2,1)S(1)}, u32[]{:S(2)}) copy-start(bf16[512,960]{1,0:T(8,128)(2,1)S(1)} %get-tuple-element.123.attended.refs_7_) | copy-start | bytes 2949124
  226.0 20.8 %copy-start.27 = (f32[512,128]{1,0:T(8,128)}, f32[512,128]{1,0:T(8,128)S(1)}, u32[]{:S(2)}) copy-start(f32[512,128]{1,0:T(8,128)S(1)} %broadcast_in_dim.46.active) | copy-start | bytes 786436
  226.0 20.9 %copy-start.2 = (bf16[4,960,512]{2,1,0:T(8,128)(2,1)S(1)}, bf16[4,960,512]{2,1,0:T(8,128)(2,1)}, u32[]{:S(2)}) copy-start(bf16[4,960,512]{2,1,0:T(8,128)(2,1)} %slice.149.weight.refs_6_) | copy-start | bytes 11796484
  255.4 16.1 %collective-permute-start.3 = (bf16[512,640]{1,0:T(8,128)(2,1)}, bf16[512,640]{1,0:T(8,128)(2,1)}, u32[]{:S(2)}, u32[]{:S(2)}) collective-permute-start(bf16[512,640]{1,0:T(8,128)(2,1)} %get-tuple-element.126.pair), channel_id=1, source_target_pairs={{0,1},{2,3},{1,0},{3,2},{4,5},{6,7},{5,4},{7,6},{8,9},{10,11},{9,8... | collective-permute-start | bytes 1966088 | tf_op jit(solution)/shard_map/ppermute | solution.py:1317
  277.8 50.8 %copy-start.18 = (bf16[512,960]{1,0:T(8,128)(2,1)}, bf16[512,960]{1,0:T(8,128)(2,1)S(1)}, u32[]{:S(2)}) copy-start(bf16[512,960]{1,0:T(8,128)(2,1)S(1)} %get-tuple-element.127.attended.refs_6_) | copy-start | bytes 2949124
  328.6 21.9 %copy-start.73 = (f32[1,960]{1,0:T(1,128)}, f32[1,960]{1,0:T(1,128)S(1)}, u32[]{:S(2)}) copy-start(f32[1,960]{1,0:T(1,128)S(1)} %get-tuple-element.199) | copy-start | bytes 11524
  328.6 21.9 %copy-start.81 = (f32[1,960]{1,0:T(1,128)}, f32[1,960]{1,0:T(1,128)S(1)}, u32[]{:S(2)}) copy-start(f32[1,960]{1,0:T(1,128)S(1)} %get-tuple-element.204) | copy-start | bytes 11524
  337.0 15.1 %collective-permute-start.6 = (bf16[512,640]{1,0:T(8,128)(2,1)}, bf16[512,640]{1,0:T(8,128)(2,1)S(1)}, u32[]{:S(2)}, u32[]{:S(2)}) collective-permute-start(bf16[512,640]{1,0:T(8,128)(2,1)} %get-tuple-element.143), channel_id=1, source_target_pairs={{0,1},{2,3},{1,0},{3,2},{4,5},{6,7},{5,4},{7,6},{8,9},{10,11},{9,8... | collective-permute-start | bytes 1966088 | tf_op jit(solution)/shard_map/ppermute | solution.py:1317
  339.0 14.0 %copy-start.8 = (f32[512,960]{1,0:T(8,128)S(1)}, f32[512,960]{1,0:T(8,128)}, u32[]{:S(2)}) copy-start(f32[512,960]{1,0:T(8,128)} %get-tuple-element.124.state.refs_4_) | copy-start | bytes 5898244
  339.0 14.0 %copy-start.36 = (f32[512,960]{1,0:T(8,128)S(1)}, f32[512,960]{1,0:T(8,128)}, u32[]{:S(2)}) copy-start(f32[512,960]{1,0:T(8,128)} %get-tuple-element.144.refs_3_) | copy-start | bytes 5898244
  365.3 29.7 %copy-start.11 = (bf16[512,960]{1,0:T(8,128)(2,1)S(1)}, bf16[512,960]{1,0:T(8,128)(2,1)}, u32[]{:S(2)}) copy-start(bf16[512,960]{1,0:T(8,128)(2,1)} %copy-done.9) | copy-start | bytes 2949124
  365.3 29.7 %copy-start.17 = (bf16[512,960]{1,0:T(8,128)(2,1)S(1)}, bf16[512,960]{1,0:T(8,128)(2,1)}, u32[]{:S(2)}) copy-start(bf16[512,960]{1,0:T(8,128)(2,1)} %copy-done.16) | copy-start | bytes 2949124
  365.3 29.7 %copy-start.71 = (f32[16,512]{1,0:T(8,128)S(1)}, f32[16,512]{1,0:T(8,128)}, u32[]{:S(2)}) copy-start(f32[16,512]{1,0:T(8,128)} %copy-done.70) | copy-start | bytes 98308
  403.6 17.9 %collective-permute-start.7 = (bf16[512,640]{1,0:T(8,128)(2,1)}, bf16[512,640]{1,0:T(8,128)(2,1)S(1)}, u32[]{:S(2)}, u32[]{:S(2)}) collective-permute-start(bf16[512,640]{1,0:T(8,128)(2,1)} %get-tuple-element.156), channel_id=1, source_target_pairs={{0,1},{2,3},{1,0},{3,2},{4,5},{6,7},{5,4},{7,6},{8,9},{10,11},{9,8... | collective-permute-start | bytes 1966088 | tf_op jit(solution)/shard_map/ppermute | solution.py:1317
  405.1 70.0 %collective-permute-start.4 = (bf16[256,960]{1,0:T(8,128)(2,1)}, bf16[256,960]{1,0:T(8,128)(2,1)S(1)}, u32[]{:S(2)}, u32[]{:S(2)}) collective-permute-start(bf16[256,960]{1,0:T(8,128)(2,1)} %select_convert_fusion.2), channel_id=1, source_target_pairs={{0,3},{1,2},{3,0},{2,1},{4,7},{5,6},{7,4},{6,5},{8,11},{9,10},{11,... | collective-permute-start | bytes 1474568 | tf_op jit(solution)/shard_map/ppermute | solution.py:1317
  407.6 14.8 %copy-start.6 = (f32[512,960]{1,0:T(8,128)S(1)}, f32[512,960]{1,0:T(8,128)}, u32[]{:S(2)}) copy-start(f32[512,960]{1,0:T(8,128)} %get-tuple-element.120.state.refs_4_) | copy-start | bytes 5898244
  407.6 14.8 %copy-start.35 = (f32[512,960]{1,0:T(8,128)S(1)}, f32[512,960]{1,0:T(8,128)}, u32[]{:S(2)}) copy-start(f32[512,960]{1,0:T(8,128)} %get-tuple-element.157.refs_3_) | copy-start | bytes 5898244
  435.5 30.1 %copy-start.15 = (bf16[512,960]{1,0:T(8,128)(2,1)S(1)}, bf16[512,960]{1,0:T(8,128)(2,1)}, u32[]{:S(2)}) copy-start(bf16[512,960]{1,0:T(8,128)(2,1)} %copy-done.14) | copy-start | bytes 2949124
  435.5 30.1 %copy-start.68 = (f32[16,512]{1,0:T(8,128)S(1)}, f32[16,512]{1,0:T(8,128)}, u32[]{:S(2)}) copy-start(f32[16,512]{1,0:T(8,128)} %copy-done.67) | copy-start | bytes 98308
  474.5 18.3 %collective-permute-start.8 = (bf16[512,640]{1,0:T(8,128)(2,1)}, bf16[512,640]{1,0:T(8,128)(2,1)S(1)}, u32[]{:S(2)}, u32[]{:S(2)}) collective-permute-start(bf16[512,640]{1,0:T(8,128)(2,1)} %get-tuple-element.169), channel_id=1, source_target_pairs={{0,1},{2,3},{1,0},{3,2},{4,5},{6,7},{5,4},{7,6},{8,9},{10,11},{9,8... | collective-permute-start | bytes 1966088 | tf_op jit(solution)/shard_map/ppermute | solution.py:1317
  481.6 12.1 %copy-start.4 = (f32[512,960]{1,0:T(8,128)S(1)}, f32[512,960]{1,0:T(8,128)}, u32[]{:S(2)}) copy-start(f32[512,960]{1,0:T(8,128)} %copy-done.3) | copy-start | bytes 5898244
  505.2 149.7 %collective-permute-start.9 = (bf16[256,960]{1,0:T(8,128)(2,1)}, bf16[256,960]{1,0:T(8,128)(2,1)S(1)}, u32[]{:S(2)}, u32[]{:S(2)}) collective-permute-start(bf16[256,960]{1,0:T(8,128)(2,1)} %select_convert_fusion), channel_id=1, source_target_pairs={{0,3},{1,2},{3,0},{2,1},{4,7},{5,6},{7,4},{6,5},{8,11},{9,10},{11,... | collective-permute-start | bytes 1474568 | tf_op jit(solution)/shard_map/ppermute | solution.py:1317
  (87 other events, 379.0 us)

commit v4 on v3

--- a/solution.py
+++ b/solution.py
@@ -16,6 +16,7 @@
 QW = HEADS * HEAD_DIM
 LANE = 128
 MIB = 2**20
+BESIDE = 16
 
 epsilon = 1e-05
 rope_base = 10000.0
@@ -42,6 +43,26 @@
 
 def params(limit):
     return pltpu.CompilerParams(vmem_limit_bytes=limit * MIB)
+
+
+def pin(array):
+    return pltpu.with_memory_space_constraint(array, pltpu.VMEM)
+
+
+def wide_limit(weight, limit):
+    return limit if whole_lanes(weight) else 62
+
+
+def whole_lanes(weight):
+    return weight.shape[-1] % LANE == 0
+
+
+def placed(weight):
+    return pin(weight) if whole_lanes(weight) else weight
+
+
+def side_by_side(ref, rows=slice(None)):
+    return jnp.concatenate([ref[piece, rows] for piece in range(ref.shape[0])], axis=1)
 
 
 def turn(block, cosine, sine):
@@ -68,8 +89,9 @@
     inverse = lax.rsqrt(jnp.mean(values_in * values_in, axis=-1, keepdims=True) + epsilon)
     low = (values_in * inverse * gain[...]).astype(BF)
     normed[...] = low
+    used = min(ceil_to(qc + 2 * kc, LANE), weight.shape[2])
     for piece in range(weight.shape[0]):
-        made = dot(low, weight[piece])
+        made = dot(low, weight[piece, :, :used])
         qbuf[:, piece * qc : (piece + 1) * qc] = made[:, :qc]
         kbuf[:, piece * kc : (piece + 1) * kc] = made[:, qc : qc + kc]
         pair[:, KW + piece * kc : KW + (piece + 1) * kc] = made[:, qc + kc : qc + 2 * kc].astype(BF)
@@ -95,9 +117,9 @@
             pltpu.VMEM((tokens, ceil_to(QW, LANE)), F32),
             pltpu.VMEM((tokens, ceil_to(KW, LANE)), F32),
         ],
-        compiler_params=params(40),
+        compiler_params=params(wide_limit(weight, 20)),
         name="pre",
-    )(state, gain, weight, cosine, sine)
+    )(state, gain, placed(weight), cosine, sine)
 
 
 def fill_bias(info, bias, recursion):
@@ -283,7 +305,7 @@
             pltpu.VMEM(info.shape[::-1], F32),
             pltpu.VMEM((3, block, block), F32),
         ],
-        compiler_params=params(40),
+        compiler_params=params(16),
         name="attend_own",
     )(queries, pair, info)
 
@@ -345,7 +367,7 @@
             pltpu.VMEM(info.shape[::-1], F32),
             pltpu.VMEM((2, block, block), F32),
         ],
-        compiler_params=params(40),
+        compiler_params=params(16),
         name="attend_rest",
     )(queries, pair, info, part)
 
@@ -414,7 +436,7 @@
             pltpu.VMEM(info.shape[::-1], F32),
             pltpu.VMEM((2, block, block), F32),
         ],
-        compiler_params=params(48),
+        compiler_params=params(20),
         name="attend_rest_back",
     )(queries, pair, info, attended, logs, grad)
 
@@ -466,67 +488,89 @@
             pltpu.VMEM(info.shape[::-1], F32),
             pltpu.VMEM((3, block, block), F32),
         ],
-        compiler_params=params(48),
+        compiler_params=params(20),
         name="attend_own_back",
     )(queries, pair, info, logs, deltas, grad, part)
 
 
 def post_kernel(
-    shift, state, attended, out_w, gain, router, active, gate_w, up_w, down_w,
-    state_out, normed, gate_out, up_out, hidden_out, midway_out, update_out, routed,
-    branch, total,
+    used, cols, state, attended, attn_w, gain, router, active, gate_w, up_w, down_w,
+    state_out, normed_out, gate_out, up_out, hidden_out, midway_out, update_out, routed,
+    normed, midway, update, branch, total, stage, sems,
 ):
-    pieces, cols = down_w.shape[0], down_w.shape[2]
-    step = pl.program_id(0)
-
-    @pl.when(step == 0)
-    def _():
-        for piece in range(pieces):
-            made = dot(attended[...], out_w[piece])
-            branch[:, piece * cols : (piece + 1) * cols] = made[:, shift : shift + cols]
-        midway = state[...] + branch[...]
-        midway_out[...] = midway
-        inverse = lax.rsqrt(jnp.mean(midway * midway, axis=-1, keepdims=True) + epsilon)
-        normed[...] = (midway * inverse * gain[...]).astype(BF)
-        total[...] = jnp.zeros(total.shape, F32)
-
-    low = normed[...]
-    gate = dot(low, gate_w[0])
-    up = dot(low, up_w[0])
-    gate_out[0] = gate.astype(BF)
-    up_out[0] = up.astype(BF)
-    hidden = (gate / (1.0 + jnp.exp(-gate)) * up).astype(BF)
-    hidden_out[0] = hidden
+    pieces, _, part = gate_w.shape
+    wide = down_w.shape[2]
+    low_col = used // LANE * LANE
+
+    def ship(index, source, target):
+        return pltpu.make_async_copy(source, target, sems.at[index])
+
+    def ship_piece(piece):
+        spot = lax.rem(piece, 2)
+        return [
+            ship(3 + 3 * spot + index, stage.at[spot, index], out.at[piece])
+            for index, out in enumerate((gate_out, up_out, hidden_out))
+        ]
+
     for piece in range(pieces):
-        total[piece] += dot(hidden, down_w[piece])
-
-    @pl.when(step == pl.num_programs(0) - 1)
-    def _():
-        for piece in range(pieces):
-            span = slice(piece * cols, (piece + 1) * cols)
-            branch[:, span] = branch[:, span] + total[piece]
-        update = branch[...]
-        update_out[...] = update
-        before = state[...]
-        chance = 1.0 / (1.0 + jnp.exp(-jnp.sum(before * router[...], axis=-1, keepdims=True)))
-        routed[...] = jnp.broadcast_to(chance, routed.shape)
-        state_out[...] = before + (active[:, 0:1] * chance) * update
-
-
-def post_part(state, attended, out_w, gain, router, active, gate_w, up_w, down_w, shift):
+        made = dot(attended[...], attn_w[piece, :, low_col:])
+        branch[:, piece * cols : (piece + 1) * cols] = made[:, used - low_col :]
+    between = state[...] + branch[...]
+    midway[...] = between
+    ship(0, midway, midway_out).start()
+    inverse = lax.rsqrt(jnp.mean(between * between, axis=-1, keepdims=True) + epsilon)
+    normed[...] = (between * inverse * gain[...]).astype(BF)
+    ship(1, normed, normed_out).start()
+    chance = 1.0 / (1.0 + jnp.exp(-jnp.sum(state[...] * router[...], axis=-1, keepdims=True)))
+    routed[...] = jnp.broadcast_to(chance, routed.shape)
+    total[...] = jnp.zeros(total.shape, F32)
+
+    def step(piece, carry):
+        spot = lax.rem(piece, 2)
+
+        @pl.when(piece >= 2)
+        def _():
+            for copy in ship_piece(piece - 2):
+                copy.wait()
+
+        rows = pl.ds(pl.multiple_of(piece * part, part), part)
+        half = normed.shape[0] // 2
+        for span in (slice(0, half), slice(half, 2 * half)):
+            pre = dot(normed[span], jnp.concatenate([gate_w[piece], up_w[piece]], axis=1))
+            gate, up = pre[:, :part], pre[:, part:]
+            hidden = (gate / (1.0 + jnp.exp(-gate)) * up).astype(BF)
+            for index, made in enumerate((gate.astype(BF), up.astype(BF), hidden)):
+                stage[spot, index, span] = made
+            total[span] += dot(hidden, side_by_side(down_w, rows))
+        for copy in ship_piece(piece):
+            copy.start()
+        return carry
+
+    lax.fori_loop(0, pieces, step, 0)
+    for piece in range(pieces):
+        span = slice(piece * cols, (piece + 1) * cols)
+        branch[:, span] = branch[:, span] + total[:, piece * wide : piece * wide + cols]
+    changed = branch[...]
+    update[...] = changed.astype(BF)
+    ship(2, update, update_out).start()
+    state_out[...] = state[...] + (active[:, 0:1] * routed[:, 0:1]) * changed
+    for index, (source, target) in enumerate(
+        ((midway, midway_out), (normed, normed_out), (update, update_out))
+    ):
+        ship(index, source, target).wait()
+    for piece in range(max(0, pieces - 2), pieces):
+        for copy in ship_piece(piece):
+            copy.wait()
+
+
+anywhere = pl.BlockSpec(memory_space=pl.ANY)
+
+
+def post_part(state, attended, attn_w, gain, router, active, gate_w, up_w, down_w, used):
     tokens, width = state.shape
     pieces, _, part = gate_w.shape
-    cols = down_w.shape[2]
-
-    def whole(*dims):
-        return pl.BlockSpec(dims, lambda f: (0,) * len(dims))
-
-    chunk = pl.BlockSpec((1, tokens, part), lambda f: (f, 0, 0))
-    weight = pl.BlockSpec((1, width, part), lambda f: (f, 0, 0))
-    row = whole(tokens, width)
     made = pl.pallas_call(
-        functools.partial(post_kernel, shift),
-        grid=(pieces,),
+        functools.partial(post_kernel, used, width // pieces),
         out_shape=(
             shape((tokens, width), F32),
             shape((tokens, width), BF),
@@ -534,121 +578,165 @@
             shape((pieces, tokens, part), BF),
             shape((pieces, tokens, part), BF),
             shape((tokens, width), F32),
-            shape((tokens, width), F32),
+            shape((tokens, width), BF),
             shape((tokens, LANE), F32),
         ),
-        in_specs=[
-            row, whole(tokens, QW), whole(*out_w.shape), whole(1, width), whole(1, width),
-            whole(tokens, LANE), weight, weight,
-            pl.BlockSpec((pieces, part, cols), lambda f: (0, f, 0)),
+        in_specs=[vmem] * 9,
+        out_specs=(vmem,) + (anywhere,) * 6 + (vmem,),
+        scratch_shapes=[
+            pltpu.VMEM((tokens, width), BF),
+            pltpu.VMEM((tokens, width), F32),
+            pltpu.VMEM((tokens, width), BF),
+            pltpu.VMEM((tokens, width), F32),
+            pltpu.VMEM((tokens, pieces * down_w.shape[2]), F32),
+            pltpu.VMEM((2, 3, tokens, part), BF),
+            pltpu.SemaphoreType.DMA((9,)),
         ],
-        out_specs=(row, row, chunk, chunk, chunk, row, row, whole(tokens, LANE)),
-        scratch_shapes=[pltpu.VMEM((tokens, width), F32), pltpu.VMEM((pieces, tokens, cols), F32)],
-        compiler_params=params(48),
+        compiler_params=params(wide_limit(gate_w, 30)),
         name="post",
-    )(state, attended, out_w, gain, router, active, gate_w, up_w, down_w)
+    )(state, attended, placed(attn_w), gain, router, active, placed(gate_w), placed(up_w),
+      placed(down_w))
     names = ("state_out", "ffn_in", "gate", "up", "hidden", "midway", "update", "routed")
     return dict(zip(names, made))
 
 
 def post_back_kernel(
-    shift, grad_state, update, routed, active, state, midway, gain, router, out_w, gate_pre, up_pre,
-    gate_w, up_w, down_w,
-    grad_ffn, grad_gate_out, grad_up_out, grad_branch, grad_attended, partial, gain_grad, router_grad,
-    total, scaled, logit,
+    used, cols, grad_state, update, routed, active, state, midway, gain, router, attn_w,
+    gate_w, up_w, down_w, gate_pre, up_pre,
+    grad_attended, partial, gain_grad, router_grad, ffn_out, gate_out, up_out, branch_out,
+    scaled, total, grad_ffn, grad_branch, fetched, stage, load, sems,
 ):
-    pieces, cols = down_w.shape[0], down_w.shape[2]
-    step = pl.program_id(0)
-
-    @pl.when(step == 0)
-    def _():
-        chance = routed[:, 0:1]
-        weight = active[:, 0:1] * chance
-        grad = grad_state[...]
-        change = grad * weight
-        scaled[...] = change
-        slope = jnp.sum(grad * update[...], axis=-1, keepdims=True) * weight * (1.0 - chance)
-        logit[...] = jnp.broadcast_to(slope, logit.shape)
-        router_grad[...] = jnp.sum(state[...] * slope, axis=0, keepdims=True)
-        low = change.astype(BF)
-        for piece in range(pieces):
-            grad_ffn[piece] = low[:, piece * cols : (piece + 1) * cols]
-        total[...] = jnp.zeros(total.shape, F32)
-
-    grad_hidden = dot(grad_ffn[0], down_w[0], NT)
-    for piece in range(1, pieces):
-        grad_hidden += dot(grad_ffn[piece], down_w[piece], NT)
-    gate = gate_pre[0].astype(F32)
-    chance = 1.0 / (1.0 + jnp.exp(-gate))
-    smooth = gate * chance
-    grad_gate = (grad_hidden * up_pre[0].astype(F32) * (chance + smooth * (1.0 - chance))).astype(BF)
-    grad_up = (grad_hidden * smooth).astype(BF)
-    grad_gate_out[0] = grad_gate
-    grad_up_out[0] = grad_up
-    total[...] += dot(grad_gate, gate_w[0], NT) + dot(grad_up, up_w[0], NT)
-
-    @pl.when(step == pl.num_programs(0) - 1)
-    def _():
-        grad_midway, grad_gain = norm_back(total[...], midway[...], gain[...])
-        gain_grad[...] = grad_gain
-        partial[...] = grad_state[...] + logit[:, 0:1] * router[...] + grad_midway
-        low = (scaled[...] + grad_midway).astype(BF)
-        grad = None
-        for piece in range(pieces):
-            if grad_branch.shape[2] > cols:
-                grad_branch[piece] = jnp.zeros(grad_branch.shape[1:], BF)
-            grad_branch[piece, :, shift : shift + cols] = low[:, piece * cols : (piece + 1) * cols]
-            made = dot(grad_branch[piece], out_w[piece], NT)
-            grad = made if grad is None else grad + made
-        grad_attended[...] = grad.astype(BF)
-
-
-def post_back(grad_state, s, gain, router, out_w, gate_w, up_w, down_w, shift):
+    pieces, _, part = gate_w.shape
+    low_col = used // LANE * LANE
+
+    def ship(index, source, target):
+        return pltpu.make_async_copy(source, target, sems.at[index])
+
+    def ship_piece(piece):
+        spot = lax.rem(piece, 2)
+        return [
+            ship(2 + 2 * spot + index, stage.at[spot, index], out.at[piece])
+            for index, out in enumerate((gate_out, up_out))
+        ]
+
+    def fetch(piece):
+        spot = lax.rem(piece, 2)
+        return [
+            pltpu.make_async_copy(ref.at[piece], fetched.at[spot, index], load.at[spot, index])
+            for index, ref in enumerate((gate_pre, up_pre))
+        ]
+
+    for copy in fetch(0):
+        copy.start()
+    chance = routed[:, 0:1]
+    weight = active[:, 0:1] * chance
+    grad = grad_state[...]
+    change = grad * weight
+    scaled[...] = change
+    slope = jnp.sum(grad * update[...].astype(F32), axis=-1, keepdims=True) * weight * (1.0 - chance)
+    router_grad[...] = jnp.sum(state[...] * slope, axis=0, keepdims=True)
+    partial[...] = grad + slope * router[...]
+    low = change.astype(BF)
+    for piece in range(pieces):
+        grad_ffn[piece] = jnp.zeros(grad_ffn.shape[1:], BF)
+        grad_ffn[piece, :, :cols] = low[:, piece * cols : (piece + 1) * cols]
+    ship(0, grad_ffn, ffn_out).start()
+    total[...] = jnp.zeros(total.shape, F32)
+
+    def step(piece, carry):
+        spot = lax.rem(piece, 2)
+
+        @pl.when(piece + 1 < pieces)
+        def _():
+            for copy in fetch(piece + 1):
+                copy.start()
+
+        @pl.when(piece >= 2)
+        def _():
+            for copy in ship_piece(piece - 2):
+                copy.wait()
+
+        for copy in fetch(piece):
+            copy.wait()
+        rows = pl.ds(pl.multiple_of(piece * part, part), part)
+        grad_hidden = dot(side_by_side(grad_ffn), side_by_side(down_w, rows), NT)
+        gate = fetched[spot, 0].astype(F32)
+        chance = 1.0 / (1.0 + jnp.exp(-gate))
+        smooth = gate * chance
+        slope = chance + smooth * (1.0 - chance)
+        grad_gate = (grad_hidden * fetched[spot, 1].astype(F32) * slope).astype(BF)
+        grad_up = (grad_hidden * smooth).astype(BF)
+        stage[spot, 0] = grad_gate
+        stage[spot, 1] = grad_up
+        total[...] += dot(
+            jnp.concatenate([grad_gate, grad_up], axis=1),
+            jnp.concatenate([gate_w[piece], up_w[piece]], axis=1),
+            NT,
+        )
+        for copy in ship_piece(piece):
+            copy.start()
+        return carry
+
+    lax.fori_loop(0, pieces, step, 0)
+    grad_midway, grad_gain = norm_back(total[...], midway[...], gain[...])
+    gain_grad[...] = grad_gain
+    partial[...] = partial[...] + grad_midway
+    low = (scaled[...] + grad_midway).astype(BF)
+    shift = used - low_col
+    for piece in range(pieces):
+        if grad_branch.shape[2] > cols:
+            grad_branch[piece] = jnp.zeros(grad_branch.shape[1:], BF)
+        grad_branch[piece, :, shift : shift + cols] = low[:, piece * cols : (piece + 1) * cols]
+    ship(1, grad_branch, branch_out).start()
+    grad = None
+    for piece in range(pieces):
+        made = dot(grad_branch[piece], attn_w[piece, :, low_col:], NT)
+        grad = made if grad is None else grad + made
+    grad_attended[...] = grad.astype(BF)
+    ship(0, grad_ffn, ffn_out).wait()
+    ship(1, grad_branch, branch_out).wait()
+    for piece in range(max(0, pieces - 2), pieces):
+        for copy in ship_piece(piece):
+            copy.wait()
+
+
+def post_back(grad_state, s, gain, router, attn_w, gate_w, up_w, down_w, used):
     state = s["state"]
     tokens, width = state.shape
     pieces, _, part = gate_w.shape
-    cols = down_w.shape[2]
-
-    def whole(*dims):
-        return pl.BlockSpec(dims, lambda f: (0,) * len(dims))
-
-    chunk = pl.BlockSpec((1, tokens, part), lambda f: (f, 0, 0))
-    weight = pl.BlockSpec((1, width, part), lambda f: (f, 0, 0))
-    row, thin, line = whole(tokens, width), whole(tokens, LANE), whole(1, width)
-    branch_dims = (pieces, tokens, out_w.shape[2])
+    branch_dims = (pieces, tokens, attn_w.shape[2] - used // LANE * LANE)
+    ffn_dims = (pieces, tokens, down_w.shape[2])
     made = pl.pallas_call(
-        functools.partial(post_back_kernel, shift),
-        grid=(pieces,),
+        functools.partial(post_back_kernel, used, width // pieces),
         out_shape=(
-            shape((pieces, tokens, cols), BF),
-            shape((pieces, tokens, part), BF),
-            shape((pieces, tokens, part), BF),
-            shape(branch_dims, BF),
             shape((tokens, QW), BF),
             shape((tokens, width), F32),
             shape((1, width), F32),
             shape((1, width), F32),
+            shape(ffn_dims, BF),
+            shape((pieces, tokens, part), BF),
+            shape((pieces, tokens, part), BF),
+            shape(branch_dims, BF),
         ),
-        in_specs=[
-            row, row, thin, thin, row, row, line, line, whole(*out_w.shape), chunk, chunk,
-            weight, weight, pl.BlockSpec((pieces, part, cols), lambda f: (0, f, 0)),
-        ],
-        out_specs=(
-            whole(pieces, tokens, cols), chunk, chunk, whole(*branch_dims), whole(tokens, QW),
-            row, line, line,
-        ),
+        in_specs=[vmem] * 12 + [anywhere] * 2,
+        out_specs=(vmem,) * 4 + (anywhere,) * 4,
         scratch_shapes=[
             pltpu.VMEM((tokens, width), F32),
             pltpu.VMEM((tokens, width), F32),
-            pltpu.VMEM((tokens, LANE), F32),
+            pltpu.VMEM(ffn_dims, BF),
+            pltpu.VMEM(branch_dims, BF),
+            pltpu.VMEM((2, 2, tokens, part), BF),
+            pltpu.VMEM((2, 2, tokens, part), BF),
+            pltpu.SemaphoreType.DMA((2, 2)),
+            pltpu.SemaphoreType.DMA((6,)),
         ],
-        compiler_params=params(48),
+        compiler_params=params(wide_limit(gate_w, 34)),
         name="post_back",
-    )(grad_state, s["update"], s["routed"], s["active"], state, s["midway"], gain, router, out_w,
-      s["gate"], s["up"], gate_w, up_w, down_w)
+    )(grad_state, s["update"], s["routed"], s["active"], state, s["midway"], gain, router,
+      placed(attn_w), placed(gate_w), placed(up_w), placed(down_w), s["gate"], s["up"])
     names = (
-        "grad_ffn", "grad_gate", "grad_up", "grad_branch", "grad_attended", "partial",
-        "ffn_gain_grad", "router_grad",
+        "grad_attended", "partial", "ffn_gain_grad", "router_grad", "grad_ffn", "grad_gate", "grad_up",
+        "grad_branch",
     )
     return dict(zip(names, made))
 
@@ -671,12 +759,13 @@
     low_k = kbuf[...].astype(BF)
     low_v = summed[:, KW:].astype(BF)
     total = None
+    used = packed.shape[2]
     for piece in range(weight.shape[0]):
         packed[piece] = jnp.zeros(packed.shape[1:], BF)
         packed[piece, :, :qc] = low_q[:, piece * qc : (piece + 1) * qc]
         packed[piece, :, qc : qc + kc] = low_k[:, piece * kc : (piece + 1) * kc]
         packed[piece, :, qc + kc : qc + 2 * kc] = low_v[:, piece * kc : (piece + 1) * kc]
-        made = dot(packed[piece], weight[piece], NT)
+        made = dot(packed[piece], weight[piece, :, :used], NT)
         total = made if total is None else total + made
     grad_in, grad_gain = norm_back(total, state[...], gain[...])
     gain_grad[...] = grad_gain
@@ -685,10 +774,11 @@
 
 def pre_back(grad_queries, grad_pairs, partial, state, gain, weight, cosine, sine, cols):
     tokens, width = state.shape
+    used = min(ceil_to(cols[0] + 2 * cols[1], LANE), weight.shape[2])
     return pl.pallas_call(
         functools.partial(pre_back_kernel, cols, len(grad_pairs)),
         out_shape=(
-            shape((weight.shape[0], tokens, weight.shape[2]), BF),
+            shape((weight.shape[0], tokens, used), BF),
             shape((tokens, width), F32),
             shape((1, width), F32),
         ),
@@ -698,9 +788,9 @@
             pltpu.VMEM((tokens, ceil_to(QW, LANE)), F32),
             pltpu.VMEM((tokens, ceil_to(KW, LANE)), F32),
         ],
-        compiler_params=params(40),
+        compiler_params=params(wide_limit(weight, 24)),
         name="pre_back",
-    )(grad_queries, *grad_pairs, partial, state, gain, weight, cosine, sine)
+    )(grad_queries, *grad_pairs, partial, state, gain, placed(weight), cosine, sine)
 
 
 def attn_sums_kernel(count, low_col, *refs):
@@ -914,10 +1004,9 @@
 
 def gather_all(parts, layers):
     count = len(parts)
-    anywhere = pl.BlockSpec(memory_space=pl.ANY)
     return pl.pallas_call(
         functools.partial(gather_kernel, count, layers),
-        out_shape=tuple(shape((2, 2, layers, 2) + part.shape, part.dtype) for part in parts),
+        out_shape=tuple(pltpu.VMEM((2, 2, layers, 2) + part.shape, part.dtype) for part in parts),
         in_specs=[anywhere] * count,
         out_specs=(anywhere,) * count,
         scratch_shapes=[
@@ -925,9 +1014,53 @@
             pltpu.SemaphoreType.DMA((count, 5 * layers)),
             pltpu.SemaphoreType.DMA((count,)),
         ],
-        compiler_params=pltpu.CompilerParams(collective_id=0, has_side_effects=True),
+        compiler_params=pltpu.CompilerParams(
+            collective_id=0, has_side_effects=True, vmem_limit_bytes=4 * MIB
+        ),
         name="gather_all",
     )(*parts)
+
+
+def unpack_kernel(rows, down_rows, micros, down, gains, info, active):
+    spot = down.shape[2] - LANE
+    first = LANE - BESIDE
+    late = second_micro()
+    outer = is_outer()
+    here = pl.ds(pl.multiple_of(lax.axis_index("dp") * down_rows, BESIDE), active.shape[1] // 2)
+    block = active.shape[1] // 2
+    for rank in range(down.shape[1] // down_rows):
+        tile = down[0, rank * down_rows : rank * down_rows + LANE, spot:].astype(F32).T
+        gains[:, rank * rows : (rank + 1) * rows] = tile[first : first + gains.shape[0], :rows]
+    info[...] = jnp.zeros(info.shape, F32)
+    for index, (one, two) in enumerate(zip((0, 3, 1, 2), (1, 2, 0, 3))):
+        tile = down[jnp.where(outer, one, two), here, spot:].astype(F32)
+        turned = tile.T
+        span = slice(index * block, (index + 1) * block)
+        for row in range(2):
+            start = first + 2 + RECUR + row * micros
+            info[row : row + 1, span] = jnp.where(
+                late, turned[start + 1 : start + 2], turned[start : start + 1]
+            )
+        if index < 2:
+            depth = jnp.where(late, tile[:, start + 1 : start + 2], tile[:, start : start + 1])
+            for r in range(RECUR):
+                active[r, span] = jnp.broadcast_to(jnp.where(depth > r, 1.0, 0.0), (block, LANE))
+
+
+def unpack(down, rows, tokens, ranks, micros):
+    down_rows = down.shape[1] // ranks
+    return pl.pallas_call(
+        functools.partial(unpack_kernel, rows, down_rows, micros),
+        out_shape=(
+            shape((8, rows * ranks), F32),
+            shape((8, 4 * tokens), F32),
+            shape((RECUR, 2 * tokens, LANE), F32),
+        ),
+        in_specs=[vmem],
+        out_specs=(vmem,) * 3,
+        compiler_params=params(8),
+        name="unpack",
+    )(pin(down))
 
 
 def finish_kernel(layers, count, low_col, *refs):
@@ -942,8 +1075,8 @@
         pop(count) for _ in range(9)
     )
     (small,) = pop(1)
-    outs = pop(5)
-    held, core_in, first_in, second_in, done, z_in = (pop(5) for _ in range(6))
+    outs = pop(4)
+    held, core_in, first_in, second_in, done, z_in = (pop(4) for _ in range(6))
     raw, left, right, ffn_right, stage, down_stage = pop(6)
     send, recv, keep, load = refs
     here = Place(layers)
@@ -1075,20 +1208,18 @@
             [right[spot, i * tokens : (i + 1) * tokens, :part].T for i in range(count)], axis=1
         )
         rows = part // 2
+        cols = ffn_right.shape[2] - small.shape[3]
         for column in range(4):
             result = dot(turned, ffn_right[column]).astype(BF)
             for index in range(2):
-                down_stage[spot, column // 2, column % 2, index] = result[
-                    index * rows : (index + 1) * rows
-                ]
+                place = (spot, column // 2, column % 2, index)
+                down_stage[place] = result[index * rows : (index + 1) * rows]
+                down_stage[place + (slice(None), slice(cols, None))] = small[piece, index]
 
     def first(a):
-        if a < 4:
-            for piece in range(4):
-                spot = (piece,) if a == 3 else (slice(None), piece // 2, piece % 2)
-                arrive(a, piece, core_in[a].at[spot])
-        else:
-            arrive(a, 0, core_in[a])
+        for piece in range(4):
+            spot = (piece,) if a == 3 else (slice(None), piece // 2, piece % 2)
+            arrive(a, piece, core_in[a].at[spot])
         for k in range(layers):
             held[a][k] = added(held[a], held[a][k], core_in[a][k])
         for k in range(layers):
@@ -1127,9 +1258,6 @@
             total = total + z_in[a][k].astype(F32)
         outs[a][...] = total
 
-    start(4, 0, small.at[:, 1 - core], core_in[4], here.sibling)
-    small_own = pltpu.make_async_copy(small.at[:, core], held[4], keep.at[4, 0])
-    small_own.start()
     ffn_left = load_left(0, ffn_in)
     go(ffn_left)
     down_right = [
@@ -1171,16 +1299,12 @@
     hold(down_right)
     products(3, fetch_of(2, hidden), down_product, down_stage)
     first(3)
-    small_own.wait()
-    first(4)
     second(2)
     third(1)
     second(3)
-    second(4)
     third(2)
     third(3)
-    third(4)
-    for a in range(5):
+    for a in range(4):
         fourth(a)
     for copy in sent:
         copy.wait_send()
@@ -1193,14 +1317,12 @@
     cols = grad_ffn[0].shape[2]
     layers = small.shape[0]
     ranks = 2 * layers
-    anywhere = pl.BlockSpec(memory_space=pl.ANY)
     rows, down_rows = width // ranks, pieces * part // ranks
     wide = packed[0].shape[2] + branch[0].shape[2]
-    ends = [(rows, part), (rows, part), (rows, part), (down_rows, cols), small.shape[4:]]
-    types = [BF] * 4 + [F32]
+    ends = [(rows, part), (rows, part), (rows, part), (down_rows, cols)]
 
     def buffers(*lead):
-        return [pltpu.VMEM(lead + end, dtype) for end, dtype in zip(ends, types)]
+        return [pltpu.VMEM(lead + end, BF) for end in ends]
 
     operands = (
         *normed, *packed, *attended, *branch, *ffn_in, *grad_gate, *grad_up, *hidden, *grad_ffn, small,
@@ -1208,8 +1330,8 @@
     return pl.pallas_call(
         functools.partial(finish_kernel, layers, count, low_col),
         out_shape=tuple(shape(end, F32) for end in ends),
-        in_specs=[anywhere] * len(operands),
-        out_specs=(vmem,) * 5,
+        in_specs=[anywhere] * (len(operands) - 1) + [vmem],
+        out_specs=(vmem,) * 4,
         scratch_shapes=[
             *buffers(layers, 2, 2),
             *buffers(layers, 2, 2),
@@ -1223,9 +1345,9 @@
             pltpu.VMEM((pieces, count * tokens, cols), BF),
             pltpu.VMEM((2, layers, 2, rows, part), BF),
             pltpu.VMEM((2, 2, 2, 2, down_rows, cols), BF),
-            pltpu.SemaphoreType.DMA((5, 4 + 3 * layers)),
-            pltpu.SemaphoreType.DMA((5, 4 + 3 * layers)),
-            pltpu.SemaphoreType.DMA((5, 4)),
+            pltpu.SemaphoreType.DMA((4, 4 + 3 * layers)),
+            pltpu.SemaphoreType.DMA((4, 4 + 3 * layers)),
+            pltpu.SemaphoreType.DMA((4, 4)),
             pltpu.SemaphoreType.DMA((10, count)),
         ],
         compiler_params=pltpu.CompilerParams(
@@ -1258,7 +1380,7 @@
 def row_plan(inputs, cotangent, depths, marks, block_params):
     micros, _, tokens, _ = inputs.shape
     seq, mine = lax.axis_size("seq"), lax.axis_index("seq")
-    attn_g, ffn_g, routers, qkv_w, out_w, gate_w, up_w, down_w, cols, shift = block_params
+    attn_g, ffn_g, routers, attn_w, gate_w, up_w, down_w, cols, used = block_params
     order = mine - jnp.arange(seq)
     marks = jnp.where((order >= 0)[:, None, None, None], marks[order % seq], -1.0)
     marks = marks.transpose(2, 1, 0, 3).reshape(micros, 2, seq * tokens)
@@ -1276,14 +1398,14 @@
     for r in range(RECUR):
         made = []
         for m in range(micros):
-            normed, queries, pair = pre_part(states[m], attn_g, qkv_w, cosine, sine, cols)
+            normed, queries, pair = pre_part(states[m], attn_g, attn_w, cosine, sine, cols)
             pairs = [pair] + [pass_on(pair, step, seq) for step in range(1, seq)]
             made.append((normed, queries, pairs))
         for m in range(micros):
             normed, queries, pairs = made[m]
             attended, logs = attend(queries, pairs, infos[m], r)
             after = post_part(
-                states[m], attended, out_w, ffn_g, routers[r], actives[m][r], gate_w, up_w, down_w, shift
+                states[m], attended, attn_w, ffn_g, routers[r], actives[m][r], gate_w, up_w, down_w, used
             )
             saved[m][r] = dict(
                 after, state=states[m], normed=normed, queries=queries, pairs=pairs,
@@ -1295,7 +1417,7 @@
         partials = []
         for m in range(micros):
             s = saved[m][r]
-            s.update(post_back(grads[m], s, ffn_g, routers[r], out_w, gate_w, up_w, down_w, shift))
+            s.update(post_back(grads[m], s, ffn_g, routers[r], attn_w, gate_w, up_w, down_w, used))
             grad_queries, *grad_pairs = attend_back(
                 s["queries"], s["pairs"], infos[m], s["attended"], s["logs"], s["grad_attended"], r
             )
@@ -1306,7 +1428,7 @@
         for m in range(micros):
             s = saved[m][r]
             s["packed"], grads[m], s["attn_gain_grad"] = pre_back(
-                *partials[m], s["partial"], s["state"], attn_g, qkv_w, cosine, sine, cols
+                *partials[m], s["partial"], s["state"], attn_g, attn_w, cosine, sine, cols
             )
     outputs = jnp.stack(states, axis=0)[:, None]
     input_grad = jnp.stack(grads, axis=0)[:, None]
@@ -1314,53 +1436,68 @@
 
 
 def swap(array, pairs):
-    return lax.ppermute(array, "seq", [(a, b) for a, b in pairs] + [(b, a) for a, b in pairs])
-
-
-ACROSS = ((0, 3), (1, 2))
-PARTNERS = ((0, 1), (2, 3))
-
-
-def paired_plan(inputs, cotangent, marks, block_params):
+    seq, ranks = lax.axis_size("seq"), lax.axis_size("dp")
+    moves = []
+    for rank in range(ranks):
+        for one, two in pairs[rank % 2]:
+            moves += [(rank * seq + one, rank * seq + two), (rank * seq + two, rank * seq + one)]
+    return lax.ppermute(array, ("dp", "seq"), moves)
+
+
+ACROSS = (((0, 3), (1, 2)),) * 2
+PARTNERS = (((0, 1), (2, 3)), ((0, 2), (1, 3)))
+
+
+def second_micro():
+    place = lax.axis_index("seq")
+    return jnp.where(lax.axis_index("dp") % 2 == 0, place >= 2, place % 2 == 1)
+
+
+def paired_start(inputs, cotangent):
     tokens = inputs.shape[2]
-    mine = lax.axis_index("seq")
-    late = mine >= 2
+    second = second_micro()
     outer = is_outer()
-    attn_g, ffn_g, routers, qkv_w, out_w, gate_w, up_w, down_w, cols, shift = block_params
-
-    def take(array):
-        own = jnp.where(late, array[1, 0], array[0, 0])
-        other = swap(jnp.where(late, array[0, 0], array[1, 0]).astype(BF), ACROSS).astype(F32)
-        return jnp.concatenate(
-            [jnp.where(late, other, own), jnp.where(late, own, other)], axis=0
-        )
+
+    def split(array):
+        own = jnp.where(second, array[1, 0], array[0, 0])
+        return own, jnp.where(second, array[0, 0], array[1, 0]).astype(BF)
+
+    places = jnp.arange(tokens, dtype=jnp.int32)
+    low, high = jnp.where(outer, 0, 1), jnp.where(outer, 3, 2)
+    tables = rope_tables(jnp.concatenate([low * tokens + places, high * tokens + places]))
+    return split(inputs), split(cotangent), tables
+
+
+def paired_plan(prepared, info, actives, block_params):
+    (own_state, other_state), (own_grad, other_grad), (cosine, sine) = prepared
+    tokens = own_state.shape[0]
+    late = lax.axis_index("seq") >= 2
+    attn_g, ffn_g, routers, attn_w, gate_w, up_w, down_w, cols, used = block_params
+
+    def join(own, other):
+        other = other.astype(F32)
+        return jnp.concatenate([jnp.where(late, other, own), jnp.where(late, own, other)], axis=0)
 
     def give(array):
         low, high = array[:tokens], array[tokens:]
         own = jnp.where(late, high, low)
         other = swap(jnp.where(late, low, high).astype(BF), ACROSS).astype(F32)
-        return jnp.stack([jnp.where(late, other, own), jnp.where(late, own, other)], axis=0)[:, None]
-
-    blocks = jnp.where(outer, jnp.array([0, 3, 1, 2]), jnp.array([1, 2, 0, 3]))
-    info = jnp.where(late, marks[:, :, 1], marks[:, :, 0])[blocks]
-    info = jnp.pad(info.transpose(1, 0, 2).reshape(2, -1), ((0, 6), (0, 0)))
-    depth = info[1, : 2 * tokens]
-    places = jnp.arange(tokens, dtype=jnp.int32)
-    cosine, sine = rope_tables(
-        jnp.concatenate([blocks[0] * tokens + places, blocks[1] * tokens + places])
-    )
-    state = take(inputs)
-    cotangent, depth = lax.optimization_barrier((cotangent, depth))
-    grad = take(cotangent)
+        second = second_micro()
+        return jnp.stack([jnp.where(second, other, own), jnp.where(second, own, other)], axis=0)[:, None]
+
+    state = join(own_state, other_state)
     saved = []
     for r in range(RECUR):
-        active = jnp.broadcast_to((depth > r).astype(F32)[:, None], (2 * tokens, LANE))
-        normed, queries, pair = pre_part(state, attn_g, qkv_w, cosine, sine, cols)
+        active = actives[r]
+        normed, queries, pair = pre_part(state, attn_g, attn_w, cosine, sine, cols)
         partner = swap(pair, PARTNERS)
+        if r == 0:
+            other_grad, partner = lax.optimization_barrier((other_grad, partner))
+            other_grad = swap(other_grad, ACROSS)
         part = attend_own(queries, pair, info, r)
         attended, logs = attend_rest(queries, partner, info, part, r)
         after = post_part(
-            state, attended, out_w, ffn_g, routers[r], active, gate_w, up_w, down_w, shift
+            state, attended, attn_w, ffn_g, routers[r], active, gate_w, up_w, down_w, used
         )
         saved.append(
             dict(
@@ -1370,9 +1507,10 @@
         )
         state = after["state_out"]
     outputs = give(state)
+    grad = join(own_grad, other_grad)
     for r in reversed(range(RECUR)):
         s = saved[r]
-        s.update(post_back(grad, s, ffn_g, routers[r], out_w, gate_w, up_w, down_w, shift))
+        s.update(post_back(grad, s, ffn_g, routers[r], attn_w, gate_w, up_w, down_w, used))
         grad_partner, part, deltas = attend_rest_back(
             s["queries"], s["partner"], info, s["attended"], s["logs"], s["grad_attended"], r
         )
@@ -1381,7 +1519,7 @@
             s["queries"], s["pair"], info, s["logs"], deltas, s["grad_attended"], part, r
         )
         s["packed"], grad, s["attn_gain_grad"] = pre_back(
-            grad_queries, [grad_pair, grad_partner], s["partial"], s["state"], attn_g, qkv_w,
+            grad_queries, [grad_pair, grad_partner], s["partial"], s["state"], attn_g, attn_w,
             cosine, sine, cols,
         )
     return outputs, give(grad), [saved]
@@ -1398,43 +1536,45 @@
     both = ("seq", "dp")
 
     attn_local = jnp.concatenate([query_weight, key_weight, value_weight, out_weight], axis=1)
-    span = ceil_to(max(rows, tokens), LANE)
-    small = jnp.concatenate([attn_gain[None], ffn_gain[None], router_weight.T], axis=0).astype(F32)
-    marks = jnp.concatenate([segments[:, 0], depths[:, 0]], axis=0).astype(F32)
+    down_rows, down_cols = down_weight.shape
+    marks = jnp.concatenate([segments[:, 0], depths[:, 0]], axis=0).T.astype(BF)
+    small = jnp.concatenate([attn_gain[:, None], ffn_gain[:, None], router_weight], axis=1)
     small = jnp.concatenate(
         [
-            jnp.pad(small, ((0, 8 - small.shape[0]), (0, span - rows))),
-            jnp.pad(marks, ((0, ceil_to(2 * micros, 8) - 2 * micros), (0, span - tokens))),
+            jnp.pad(small, ((0, down_rows - rows), (0, 0))),
+            jnp.pad(marks, ((0, down_rows - tokens), (0, BESIDE - 2 - RECUR - 2 * micros))),
         ],
-        axis=0,
+        axis=1,
     )
-    parts = (attn_local, gate_weight, up_weight, down_weight, small)
+    parts = (
+        attn_local, gate_weight, up_weight, jnp.concatenate([down_weight, small], axis=1)
+    )
     direct = micros == 2 and (seq, ranks) == (4, 8)
     if direct:
+        states, grads, tables = paired_start(inputs, cotangent)
+        states = (states[0], swap(states[1], ACROSS))
+        parts, own, grads, tables = lax.optimization_barrier((parts, states[0], grads, tables))
         gathered = gather_all(parts, ranks // 2)
+        prepared = ((own, states[1]), grads, tables)
     else:
         gathered = [lax.all_gather(part, both, axis=0, tiled=False) for part in parts]
-    attn_w, gate_w, up_w, down_w = (
-        full.reshape(seq, -1, full.shape[-1]) for full in gathered[:4]
-    )
-    small = gathered[4].reshape(seq, ranks, *small.shape)
-    marks = lax.dynamic_index_in_dim(small, lax.axis_index("dp"), 1, keepdims=False)
-    marks = marks[:, 8 : 8 + 2 * micros, :tokens].reshape(seq, 2, micros, tokens)
-    small = small[0, :, : 2 + RECUR, :rows].transpose(1, 0, 2).reshape(2 + RECUR, width)
+    attn_w, gate_w, up_w, down_w = (full.reshape(seq, -1, full.shape[-1]) for full in gathered)
+    if direct:
+        small, info, actives = unpack(down_w, rows, tokens, ranks, micros)
+    else:
+        small = down_w[:, :, down_cols:].reshape(seq, ranks, down_rows, BESIDE).astype(F32)
+        marks = lax.dynamic_index_in_dim(small, lax.axis_index("dp"), 1, keepdims=False)
+        marks = marks[:, :tokens, 2 + RECUR : 2 + RECUR + 2 * micros].transpose(0, 2, 1)
+        marks = marks.reshape(seq, 2, micros, tokens)
+        small = small[0, :, :rows, : 2 + RECUR].reshape(width, 2 + RECUR).T
     attn_g, ffn_g = small[0:1], small[1:2]
     routers = [small[2 + r : 3 + r] for r in range(RECUR)]
     used = qc + 2 * kc
     total_cols = attn_w.shape[2]
-    high_col = min(ceil_to(used, LANE), total_cols)
     low_col = used // LANE * LANE
-    shift = used - low_col
-    qkv_w, out_w = attn_w[:, :, :high_col], attn_w[:, :, low_col:]
-
-    block_params = (
-        attn_g, ffn_g, routers, qkv_w, out_w, gate_w, up_w, down_w, (qc, kc), shift
-    )
+    block_params = (attn_g, ffn_g, routers, attn_w, gate_w, up_w, down_w, (qc, kc), used)
     if direct:
-        outputs, input_grad, saved = paired_plan(inputs, cotangent, marks, block_params)
+        outputs, input_grad, saved = paired_plan(prepared, info, actives, block_params)
     else:
         outputs, input_grad, saved = row_plan(inputs, cotangent, depths, marks, block_params)
     flat = [steps[r] for r in reversed(range(RECUR)) for steps in saved]
@@ -1445,18 +1585,17 @@
     attn_gain_sum, ffn_gain_sum = sum(every("attn_gain_grad")), sum(every("ffn_gain_grad"))
     router_sums = [sum(steps[r]["router_grad"] for steps in saved) for r in range(RECUR)]
     small_sum = jnp.concatenate([attn_gain_sum, ffn_gain_sum, *router_sums], axis=0)
-    small_sum = small_sum.reshape(2 + RECUR, ranks, rows).transpose(1, 0, 2)
-    small_sum = jnp.pad(
-        small_sum, ((0, 0), (0, 8 - small_sum.shape[1]), (0, ceil_to(rows, LANE) - rows))
-    )
+    small_sum = small_sum.T.reshape(ranks, rows, 2 + RECUR)
     if direct:
-        small_sum = small_sum.reshape(ranks // 2, 2, 1, 1, *small_sum.shape[1:])
-        small_sum = jnp.broadcast_to(small_sum, small_sum.shape[:2] + (2, 2) + small_sum.shape[4:])
-        gate_grad, up_grad, attn_grad, down_grad, small_own = finish(
+        small_sum = jnp.pad(
+            small_sum, ((0, 0), (0, down_rows - rows), (0, BESIDE - 2 - RECUR))
+        ).astype(BF)
+        gate_grad, up_grad, attn_grad, down_grad = finish(
             every("normed"), every("packed"), every("attended"), every("grad_branch"),
             every("ffn_in"), every("grad_gate"), every("grad_up"), every("hidden"),
-            every("grad_ffn"), small_sum, low_col,
+            every("grad_ffn"), small_sum.reshape(ranks // 2, 2, down_rows, BESIDE), low_col,
         )
+        small_own = down_grad[:rows, down_cols : down_cols + 2 + RECUR].T
     else:
         down_sum = down_sums(every("hidden"), every("grad_ffn"))
         gate_sum, up_sum = pair_sums(every("ffn_in"), every("grad_gate"), every("grad_up"))
@@ -1472,7 +1611,8 @@
         sums = [lax.psum_scatter(part, "seq", scatter_dimension=0) for part in sums]
         sums = [lax.psum_scatter(part, "dp", scatter_dimension=0).astype(F32) for part in sums]
         gate_grad, up_grad, attn_grad, down_grad, small_own = sums
-    small_own = small_own[: 2 + RECUR, :rows]
+        small_own = small_own.T
+    down_grad = down_grad[:, :down_cols]
 
     return (
         outputs,

time: 670 us -> 554 us (0.83)
  Pallas kernels: 520 us -> 451 us
  local copies, waits for them, and re-layouts: 91.6 us -> 46.6 us
  other arithmetic: 19.1 us -> 12.4 us
    pallas_call x6 -> x7, Pallas kernels: 145 us -> 113 us  [the longest x3 60.3 us: post_back(): pl.pallas_call(functools.partial(post_back_kernel, used, width // pieces)...]
    unnamed x232 -> x176, local copies, waits for them, and re-layouts: 56.3 us -> 36.4 us
    optimization_barrier x1 -> x0, local copies, waits for them, and re-layouts: 12.1 us -> none  [paired_plan(): cotangent, depth = lax.optimization_barrier((cotangent, depth))]
    pallas_call x3, Pallas kernels: 34.2 us -> 25.9 us  [attend_own_back(): pl.pallas_call(functools.partial(own_back_kernel, recursion), out_shape=(...]
    pallas_call x3, Pallas kernels: 25.9 us -> 18.8 us  [attend_rest_back(): pl.pallas_call(functools.partial(rest_back_kernel, recursion), out_shape=...]
  transfers between devices with their start and end apart: 10 -> 10, of which waited for: 4 -> 5; matrix products, arithmetic and copies ran while one was open for 8% -> 5% of each run, Pallas kernels for 57% -> 61%
where the time goes in v4:
time: 554 us; the launch traced here: 549 us
  Pallas kernels  451 us (81%)
  local copies, waits for them, and re-layouts  46.6 us (8%)
  waiting for transfers between devices  18.4 us (3%)
  starting transfers between devices  18.1 us (3%)
  other arithmetic  12.4 us (2%)
    pallas_call x1, Pallas kernels, finish(): pl.pallas_call(functools.partial(finish_kernel, layers, count, low_col),...  139 us
    pallas_call x1, Pallas kernels, gather_all(): pl.pallas_call(functools.partial(gather_kernel, count, layers), out_shape...  101 us
    pallas_call x3, Pallas kernels, post_back(): pl.pallas_call(functools.partial(post_back_kernel, used, width // pieces)...  60.3 us
    pallas_call x3, Pallas kernels, post_part(): pl.pallas_call(functools.partial(post_kernel, used, width // pieces), out...  52 us
    unnamed x176, local copies, waits for them, and re-layouts  36.4 us
    pallas_call x3, Pallas kernels, attend_own_back(): pl.pallas_call(functools.partial(own_back_kernel, recursion), out_shape=(...  25.9 us
    pallas_call x3, Pallas kernels, attend_rest_back(): pl.pallas_call(functools.partial(rest_back_kernel, recursion), out_shape=...  18.8 us
    ppermute x10, waiting for transfers between devices, swap(): return lax.ppermute(array, ('dp', 'seq'), moves)  18.4 us
  transfers between devices with their start and end apart: 10, of which 5 were waited for; matrix products, arithmetic and copies ran while one was open for 5% of the time, Pallas kernels for 61%

profile of v4, /device:TPU:0, one launch (start us, length us, event | category | flops | bytes accessed | tf_op | source)
XLA Modules:
  0.0 549.0 jit_solution(17349229693890724308)
XLA Ops:
  4.0 3.9 collective-permute-start
  8.5 2.6 fusion.14
  19.4 100.8 %gather_all.1 = (bf16[2,2,4,2,120,640]{5,4,3,2,1,0:T(8,128)(2,1)S(1)}, bf16[2,2,4,2,120,640]{5,4,3,2,1,0:T(8,128)(2,1)S(1)}, bf16[2,2,4,2,120,640]{5,4,3,2,1,0:T...) custom-call(bf16[120,640]{1,0:T(8,128)(2,1)S(1)} %pad_maximum_fusion.4.refs_0_, bf16[120,640]{1,0:T(8,128)(2,1)S(1)} %copy-done.60, ...), custom_call_target="tpu_custom_call" | custom-call | tf_op jit(solution)/shard_map/gather_all/pallas_call | solution.py:1007
  122.7 3.7 pre.3
  128.2 4.4 attend_own.3.part
  132.6 4.4 collective-permute-done.1.pair
  137.0 5.3 attend_rest.3
  142.4 17.3 %post.3 = (f32[512,960]{1,0:T(8,128)}, bf16[512,960]{1,0:T(8,128)(2,1)S(1)}, bf16[4,512,640]{2,1,0:T(8,128)(2,1)}, bf16[4,512,640]{2,1,0:T(8,128)(2,1)}, bf16[4,...) custom-call(f32[512,960]{1,0:T(8,128)} %copy-done.5, ...), custom_call_target="tpu_custom_call" | custom-call | tf_op jit(solution)/shard_map/post/pallas_call | solution.py:572
  162.2 3.7 pre.4
  169.2 4.4 attend_own.4.part
  173.6 8.5 %collective-permute-done.2.pair = bf16[512,640]{1,0:T(8,128)(2,1)S(1)} collective-permute-done((bf16[512,640]{1,0:T(8,128)(2,1)S(1)}, bf16[512,640]{1,0:T(8,128)(2,1)S(1)}, u32[]{:S(2)}, u32[]{:S(2)}) %collective-permute-start.2) | collective-permute-done | bytes 655392 | tf_op jit(solution)/shard_map/ppermute | solution.py:1444
  182.1 5.0 attend_rest.4
  187.2 17.4 %post.4 = (f32[512,960]{1,0:T(8,128)}, bf16[512,960]{1,0:T(8,128)(2,1)S(1)}, bf16[4,512,640]{2,1,0:T(8,128)(2,1)}, bf16[4,512,640]{2,1,0:T(8,128)(2,1)}, bf16[4,...) custom-call(f32[512,960]{1,0:T(8,128)} %get-tuple-element.140.state.refs_4_, ...), custom_call_target="tpu_custom_call" | custom-call | tf_op jit(solution)/shard_map/post/pallas_call | solution.py:572
  207.7 3.7 pre.5
  214.9 4.4 attend_own.5.part
  219.3 2.7 collective-permute-done.3.pair
  222.0 5.3 attend_rest.5
  227.4 17.3 %post.5 = (f32[512,960]{1,0:T(8,128)}, bf16[512,960]{1,0:T(8,128)(2,1)S(1)}, bf16[4,512,640]{2,1,0:T(8,128)(2,1)}, bf16[4,512,640]{2,1,0:T(8,128)(2,1)}, bf16[4,...) custom-call(f32[512,960]{1,0:T(8,128)} %get-tuple-element.144.state.refs_4_, ...), custom_call_target="tpu_custom_call" | custom-call | tf_op jit(solution)/shard_map/post/pallas_call | solution.py:572
  249.0 19.3 %post_back.3 = (bf16[512,960]{1,0:T(8,128)(2,1)}, f32[512,960]{1,0:T(8,128)}, f32[1,960]{1,0:T(1,128)S(1)}, f32[1,960]{1,0:T(1,128)S(1)}, bf16[4,512,256]{2,1,0:...) custom-call(f32[512,960]{1,0:T(8,128)} %pad_maximum_fusion.1.grad_state, ...), custom_call_target="tpu_custom_call" | custom-call | tf_op jit(solution)/shard_map/post_back/pallas_call | solution.py:709
  269.6 6.0 %attend_rest_back.3 = (bf16[512,640]{1,0:T(8,128)(2,1)S(1)}, f32[5,64,1536]{2,1,0:T(8,128)S(1)}, f32[16,512]{1,0:T(8,128)S(1)}) custom-call(bf16[512,960]{1,0:T(8,128)(2,1)S(1)} %get-tuple-element.145.queries, bf16[512,640]{1,0:T(8,128)(2,1)S(1)} %collective-permute-done.3.pair, f32[8,1024]{1,0:T(8,128)S(1)} %get-tuple-element.135.info, ...), custom_call_target="tpu_custom_call" | custom-call | tf_op jit(solution)/shard_map/attend_rest_back/pallas_call | solution.py:426
  277.2 8.7 %attend_own_back.3 = (f32[512,960]{1,0:T(8,128)S(1)}, f32[512,640]{1,0:T(8,128)S(1)}) custom-call(bf16[512,960]{1,0:T(8,128)(2,1)S(1)} %get-tuple-element.145.queries, bf16[512,640]{1,0:T(8,128)(2,1)S(1)} %get-tuple-element.146.pair, f32[8,1024]{1,0:T(8,128)S(1)} %get-tuple-element.135.info, f32[16,512]{1,0:T(8,128)S(1)} %get-tuple-element.151.logs, ...), custom_call_target="tpu_custom_call" | custom-call | tf_op jit(solution)/shard_map/attend_own_back/pallas_call | solution.py:482
  286.3 4.2 pre_back.3
  291.9 20.4 %post_back.4 = (bf16[512,960]{1,0:T(8,128)(2,1)}, f32[512,960]{1,0:T(8,128)}, f32[1,960]{1,0:T(1,128)S(1)}, f32[1,960]{1,0:T(1,128)S(1)}, bf16[4,512,256]{2,1,0:...) custom-call(f32[512,960]{1,0:T(8,128)} %copy-done.44, ...), custom_call_target="tpu_custom_call" | custom-call | tf_op jit(solution)/shard_map/post_back/pallas_call | solution.py:709
  313.6 6.0 %attend_rest_back.4 = (bf16[512,640]{1,0:T(8,128)(2,1)S(1)}, f32[5,64,1536]{2,1,0:T(8,128)S(1)}, f32[16,512]{1,0:T(8,128)S(1)}) custom-call(bf16[512,960]{1,0:T(8,128)(2,1)S(1)} %get-tuple-element.141.queries, bf16[512,640]{1,0:T(8,128)(2,1)S(1)} %copy-done.32, f32[8,1024]{1,0:T(8,128)S(1)} %get-tuple-element.135.info, bf16[512,960]{1,0:T(8,128)(2,1)S(1)} %copy-done.17, ...), custom_call_target="tpu_custom_call" | custom-call | tf_op jit(solution)/shard_map/attend_rest_back/pallas_call | solution.py:426
  323.7 8.7 %attend_own_back.4 = (f32[512,960]{1,0:T(8,128)S(1)}, f32[512,640]{1,0:T(8,128)S(1)}) custom-call(bf16[512,960]{1,0:T(8,128)(2,1)S(1)} %get-tuple-element.141.queries, bf16[512,640]{1,0:T(8,128)(2,1)S(1)} %copy-done.28, f32[8,1024]{1,0:T(8,128)S(1)} %get-tuple-element.135.info, f32[16,512]{1,0:T(8,128)S(1)} %get-tuple-element.150.logs, ...), custom_call_target="tpu_custom_call" | custom-call | tf_op jit(solution)/shard_map/attend_own_back/pallas_call | solution.py:482
  334.9 4.2 pre_back.4
  340.5 20.5 %post_back.5 = (bf16[512,960]{1,0:T(8,128)(2,1)}, f32[512,960]{1,0:T(8,128)}, f32[1,960]{1,0:T(1,128)S(1)}, f32[1,960]{1,0:T(1,128)S(1)}, bf16[4,512,256]{2,1,0:...) custom-call(f32[512,960]{1,0:T(8,128)} %copy-done.43, ...), custom_call_target="tpu_custom_call" | custom-call | tf_op jit(solution)/shard_map/post_back/pallas_call | solution.py:709
  362.3 6.8 %attend_rest_back.5 = (bf16[512,640]{1,0:T(8,128)(2,1)}, f32[5,64,1536]{2,1,0:T(8,128)S(1)}, f32[16,512]{1,0:T(8,128)S(1)}) custom-call(bf16[512,960]{1,0:T(8,128)(2,1)S(1)} %copy-done.12, bf16[512,640]{1,0:T(8,128)(2,1)S(1)} %copy-done.30, f32[8,1024]{1,0:T(8,128)S(1)} %get-tuple-element.135.info, bf16[512,960]{1,0:T(8,128)(2,1)S(1)} %copy-done.15, ...), custom_call_target="tpu_custom_call" | custom-call | tf_op jit(solution)/shard_map/attend_rest_back/pallas_call | solution.py:426
  372.1 3.4 copy.88
  377.1 8.5 %attend_own_back.5 = (f32[512,960]{1,0:T(8,128)S(1)}, f32[512,640]{1,0:T(8,128)S(1)}) custom-call(bf16[512,960]{1,0:T(8,128)(2,1)S(1)} %copy-done.13, bf16[512,640]{1,0:T(8,128)(2,1)S(1)} %copy-done.26, f32[8,1024]{1,0:T(8,128)S(1)} %get-tuple-element.135.info, f32[16,512]{1,0:T(8,128)S(1)} %get-tuple-element.149.logs, ...), custom_call_target="tpu_custom_call" | custom-call | tf_op jit(solution)/shard_map/attend_own_back/pallas_call | solution.py:482
  388.0 5.5 %pre_back.5 = (bf16[4,512,512]{2,1,0:T(8,128)(2,1)S(1)}, f32[512,960]{1,0:T(8,128)S(1)}, f32[1,960]{1,0:T(1,128)S(1)}) custom-call(f32[512,960]{1,0:T(8,128)S(1)} %get-tuple-element.188.refs_0_, f32[512,640]{1,0:T(8,128)S(1)} %get-tuple-element.189.refs_1_, bf16[512,640]{1,0:T(8,128)(2,1)} %collective-permute-done.8.refs_2_, f32[512,960]{1,0:T(8,128)S(1)} %copy-done.39, ...), custom_call_target="tpu_custom_call" | custom-call | tf_op jit(solution)/shard_map/pre_back/pallas_call | solution.py:778
  398.5 139.2 %finish.1 = (f32[120,640]{1,0:T(8,128)}, f32[120,640]{1,0:T(8,128)}, f32[120,640]{1,0:T(8,128)}, f32[320,256]{1,0:T(8,128)}) custom-call(bf16[512,960]{1,0:T(8,128)(2,1)} %copy-done.51, bf16[512,960]{1,0:T(8,128)(2,1)} %copy-done.49, bf16[512,960]{1,0:T(8,128)(2,1)} %copy-done.47, bf16[4,512,512]{2,1,0:T(8,128)(2,1)} %copy-done.37, ...), custom_call_target="tpu_custom_call" | custom-call | tf_op jit(solution)/shard_map/finish/pallas_call | solution.py:1330
  (235 shorter events, 70.7 us)
Async XLA Ops:
  4.0 116.8 %collective-permute-start = (bf16[256,960]{1,0:T(8,128)(2,1)}, bf16[256,960]{1,0:T(8,128)(2,1)}, u32[]{:S(2)}, u32[]{:S(2)}) collective-permute-start(bf16[256,960]{1,0:T(8,128)(2,1)} %fusion.4), channel_id=1, source_target_pairs={{0,3},{3,0},{1,2},{2,1},{4,7},{7,4},{5,6},{6,5},{8,11},{11,8},{9,1... | collective-permute-start | bytes 1474568 | tf_op jit(solution)/shard_map/ppermute | solution.py:1444
  120.2 107.2 %copy-start.2 = (bf16[2,2,4,2,120,640]{5,4,3,2,1,0:T(8,128)(2,1)}, bf16[2,2,4,2,120,640]{5,4,3,2,1,0:T(8,128)(2,1)S(1)}, u32[]{:S(2)}) copy-start(bf16[2,2,4,2,120,640]{5,4,3,2,1,0:T(8,128)(2,1)S(1)} %get-tuple-element.138) | copy-start | bytes 14745604
  120.2 126.4 %copy-start.4 = (bf16[2,2,4,2,120,640]{5,4,3,2,1,0:T(8,128)(2,1)}, bf16[2,2,4,2,120,640]{5,4,3,2,1,0:T(8,128)(2,1)S(1)}, u32[]{:S(2)}) copy-start(bf16[2,2,4,2,120,640]{5,4,3,2,1,0:T(8,128)(2,1)S(1)} %get-tuple-element.139) | copy-start | bytes 14745604
  120.2 220.3 %copy-start = (bf16[2,2,4,2,120,640]{5,4,3,2,1,0:T(8,128)(2,1)}, bf16[2,2,4,2,120,640]{5,4,3,2,1,0:T(8,128)(2,1)S(1)}, u32[]{:S(2)}) copy-start(bf16[2,2,4,2,120,640]{5,4,3,2,1,0:T(8,128)(2,1)S(1)} %get-tuple-element.128) | copy-start | bytes 14745604
  126.4 10.7 %copy-start.11 = (bf16[512,960]{1,0:T(8,128)(2,1)}, bf16[512,960]{1,0:T(8,128)(2,1)S(1)}, u32[]{:S(2)}) copy-start(bf16[512,960]{1,0:T(8,128)(2,1)S(1)} %get-tuple-element.131.queries) | copy-start | bytes 2949124
  126.4 10.7 %collective-permute-start.1 = (bf16[512,640]{1,0:T(8,128)(2,1)S(1)}, bf16[512,640]{1,0:T(8,128)(2,1)S(1)}, u32[]{:S(2)}, u32[]{:S(2)}) collective-permute-start(bf16[512,640]{1,0:T(8,128)(2,1)S(1)} %get-tuple-element.133.pair), channel_id=1, source_target_pairs={{0,1},{1,0},{2,3},{3,2},{4,6},{6,4},{5,7},{7,5},{8,9},{9,8},{10,11... | collective-permute-start | bytes 1966088 | tf_op jit(solution)/shard_map/ppermute | solution.py:1444
  128.2 14.2 %copy-start.33 = (f32[512,128]{1,0:T(8,128)}, f32[512,128]{1,0:T(8,128)S(1)}, u32[]{:S(2)}) copy-start(f32[512,128]{1,0:T(8,128)S(1)} %get-tuple-element.294.active) | copy-start | bytes 786436
  128.2 59.0 %copy-start.35 = (f32[512,128]{1,0:T(8,128)}, f32[512,128]{1,0:T(8,128)S(1)}, u32[]{:S(2)}) copy-start(f32[512,128]{1,0:T(8,128)S(1)} %get-tuple-element.293.active) | copy-start | bytes 786436
  142.3 17.4 %copy-start.14 = (bf16[512,960]{1,0:T(8,128)(2,1)}, bf16[512,960]{1,0:T(8,128)(2,1)S(1)}, u32[]{:S(2)}) copy-start(bf16[512,960]{1,0:T(8,128)(2,1)S(1)} %get-tuple-element.136.attended.refs_8_) | copy-start | bytes 2949124
  165.9 16.2 %collective-permute-start.2 = (bf16[512,640]{1,0:T(8,128)(2,1)S(1)}, bf16[512,640]{1,0:T(8,128)(2,1)S(1)}, u32[]{:S(2)}, u32[]{:S(2)}) collective-permute-start(bf16[512,640]{1,0:T(8,128)(2,1)S(1)} %get-tuple-element.142.pair), channel_id=1, source_target_pairs={{0,1},{1,0},{2,3},{3,2},{4,6},{6,4},{5,7},{7,5},{8,9},{9,8},{10,11... | collective-permute-start | bytes 1966088 | tf_op jit(solution)/shard_map/ppermute | solution.py:1444
  167.6 45.4 %collective-permute-start.5 = (bf16[256,960]{1,0:T(8,128)(2,1)S(1)}, bf16[256,960]{1,0:T(8,128)(2,1)S(1)}, u32[]{:S(2)}, u32[]{:S(2)}) collective-permute-start(bf16[256,960]{1,0:T(8,128)(2,1)S(1)} %fusion.5), channel_id=1, source_target_pairs={{0,3},{3,0},{1,2},{2,1},{4,7},{7,4},{5,6},{6,5},{8,11},{11,8},{9,1... | collective-permute-start | bytes 1474568 | tf_op jit(solution)/shard_map/ppermute | solution.py:1444
  187.2 17.4 %copy-start.16 = (bf16[512,960]{1,0:T(8,128)(2,1)}, bf16[512,960]{1,0:T(8,128)(2,1)S(1)}, u32[]{:S(2)}) copy-start(bf16[512,960]{1,0:T(8,128)(2,1)S(1)} %get-tuple-element.143.attended.refs_7_) | copy-start | bytes 2949124
  211.4 10.7 %collective-permute-start.3 = (bf16[512,640]{1,0:T(8,128)(2,1)S(1)}, bf16[512,640]{1,0:T(8,128)(2,1)S(1)}, u32[]{:S(2)}, u32[]{:S(2)}) collective-permute-start(bf16[512,640]{1,0:T(8,128)(2,1)S(1)} %get-tuple-element.146.pair), channel_id=1, source_target_pairs={{0,1},{1,0},{2,3},{3,2},{4,6},{6,4},{5,7},{7,5},{8,9},{9,8},{10,11... | collective-permute-start | bytes 1966088 | tf_op jit(solution)/shard_map/ppermute | solution.py:1444
  227.3 41.0 %copy-start.18 = (bf16[512,960]{1,0:T(8,128)(2,1)}, bf16[512,960]{1,0:T(8,128)(2,1)S(1)}, u32[]{:S(2)}) copy-start(bf16[512,960]{1,0:T(8,128)(2,1)S(1)} %get-tuple-element.147.attended.refs_6_) | copy-start | bytes 2949124
  275.6 10.7 %collective-permute-start.6 = (bf16[512,640]{1,0:T(8,128)(2,1)S(1)}, bf16[512,640]{1,0:T(8,128)(2,1)S(1)}, u32[]{:S(2)}, u32[]{:S(2)}) collective-permute-start(bf16[512,640]{1,0:T(8,128)(2,1)S(1)} %get-tuple-element.164), channel_id=1, source_target_pairs={{0,1},{1,0},{2,3},{3,2},{4,6},{6,4},{5,7},{7,5},{8,9},{9,8},{10,11... | collective-permute-start | bytes 1966088 | tf_op jit(solution)/shard_map/ppermute | solution.py:1444
  291.8 20.5 %copy-start.37 = (bf16[4,512,512]{2,1,0:T(8,128)(2,1)}, bf16[4,512,512]{2,1,0:T(8,128)(2,1)S(1)}, u32[]{:S(2)}) copy-start(bf16[4,512,512]{2,1,0:T(8,128)(2,1)S(1)} %get-tuple-element.196.refs_3_) | copy-start | bytes 6291460
  291.9 20.4 %copy-start.17 = (bf16[512,960]{1,0:T(8,128)(2,1)S(1)}, bf16[512,960]{1,0:T(8,128)(2,1)}, u32[]{:S(2)}) copy-start(bf16[512,960]{1,0:T(8,128)(2,1)} %copy-done.16) | copy-start | bytes 2949124
  291.9 20.4 %copy-start.32 = (bf16[512,640]{1,0:T(8,128)(2,1)S(1)}, bf16[512,640]{1,0:T(8,128)(2,1)}, u32[]{:S(2)}) copy-start(bf16[512,640]{1,0:T(8,128)(2,1)} %copy-done.31) | copy-start | bytes 1966084
  291.9 29.3 %copy-start.64 = (f32[512,960]{1,0:T(8,128)S(1)}, f32[512,960]{1,0:T(8,128)}, u32[]{:S(2)}) copy-start(f32[512,960]{1,0:T(8,128)} %get-tuple-element.148) | copy-start | bytes 5898244
  313.6 10.1 %copy-start.22 = (bf16[512,960]{1,0:T(8,128)(2,1)S(1)}, bf16[512,960]{1,0:T(8,128)(2,1)}, u32[]{:S(2)}) copy-start(bf16[512,960]{1,0:T(8,128)(2,1)} %get-tuple-element.172.grad) | copy-start | bytes 2949124
  313.6 10.1 %copy-start.28 = (bf16[512,640]{1,0:T(8,128)(2,1)S(1)}, bf16[512,640]{1,0:T(8,128)(2,1)}, u32[]{:S(2)}) copy-start(bf16[512,640]{1,0:T(8,128)(2,1)} %copy-done.27) | copy-start | bytes 1966084
  319.6 15.3 %collective-permute-start.7 = (bf16[512,640]{1,0:T(8,128)(2,1)S(1)}, bf16[512,640]{1,0:T(8,128)(2,1)S(1)}, u32[]{:S(2)}, u32[]{:S(2)}) collective-permute-start(bf16[512,640]{1,0:T(8,128)(2,1)S(1)} %get-tuple-element.177), channel_id=1, source_target_pairs={{0,1},{1,0},{2,3},{3,2},{4,6},{6,4},{5,7},{7,5},{8,9},{9,8},{10,11... | collective-permute-start | bytes 1966088 | tf_op jit(solution)/shard_map/ppermute | solution.py:1444
  322.1 48.2 %collective-permute-start.4 = (bf16[256,960]{1,0:T(8,128)(2,1)}, bf16[256,960]{1,0:T(8,128)(2,1)S(1)}, u32[]{:S(2)}, u32[]{:S(2)}) collective-permute-start(bf16[256,960]{1,0:T(8,128)(2,1)} %select_convert_fusion.1), channel_id=1, source_target_pairs={{0,3},{3,0},{1,2},{2,1},{4,7},{7,4},{5,6},{6,5},{8,11},{11,8},{9,1... | collective-permute-start | bytes 1474568 | tf_op jit(solution)/shard_map/ppermute | solution.py:1444
  323.7 11.2 %copy-start.8 = (f32[512,960]{1,0:T(8,128)S(1)}, f32[512,960]{1,0:T(8,128)}, u32[]{:S(2)}) copy-start(f32[512,960]{1,0:T(8,128)} %get-tuple-element.140.state.refs_4_) | copy-start | bytes 5898244
  323.7 11.2 %copy-start.41 = (f32[512,960]{1,0:T(8,128)S(1)}, f32[512,960]{1,0:T(8,128)}, u32[]{:S(2)}) copy-start(f32[512,960]{1,0:T(8,128)} %get-tuple-element.178.refs_3_) | copy-start | bytes 5898244
  340.5 20.6 %copy-start.38 = (bf16[4,512,512]{2,1,0:T(8,128)(2,1)}, bf16[4,512,512]{2,1,0:T(8,128)(2,1)S(1)}, u32[]{:S(2)}) copy-start(bf16[4,512,512]{2,1,0:T(8,128)(2,1)S(1)} %get-tuple-element.197.refs_4_) | copy-start | bytes 6291460
  340.5 20.6 %copy-start.12 = (bf16[512,960]{1,0:T(8,128)(2,1)S(1)}, bf16[512,960]{1,0:T(8,128)(2,1)}, u32[]{:S(2)}) copy-start(bf16[512,960]{1,0:T(8,128)(2,1)} %copy-done.11) | copy-start | bytes 2949124
  340.5 20.6 %copy-start.15 = (bf16[512,960]{1,0:T(8,128)(2,1)S(1)}, bf16[512,960]{1,0:T(8,128)(2,1)}, u32[]{:S(2)}) copy-start(bf16[512,960]{1,0:T(8,128)(2,1)} %copy-done.14) | copy-start | bytes 2949124
  340.5 20.6 %copy-start.30 = (bf16[512,640]{1,0:T(8,128)(2,1)S(1)}, bf16[512,640]{1,0:T(8,128)(2,1)}, u32[]{:S(2)}) copy-start(bf16[512,640]{1,0:T(8,128)(2,1)} %copy-done.29) | copy-start | bytes 1966084
  340.5 29.8 %copy-start.65 = (f32[512,960]{1,0:T(8,128)S(1)}, f32[512,960]{1,0:T(8,128)}, u32[]{:S(2)}) copy-start(f32[512,960]{1,0:T(8,128)} %get-tuple-element.148) | copy-start | bytes 5898244
  369.1 16.4 %collective-permute-start.8 = (bf16[512,640]{1,0:T(8,128)(2,1)}, bf16[512,640]{1,0:T(8,128)(2,1)}, u32[]{:S(2)}, u32[]{:S(2)}) collective-permute-start(bf16[512,640]{1,0:T(8,128)(2,1)} %get-tuple-element.190), channel_id=1, source_target_pairs={{0,1},{1,0},{2,3},{3,2},{4,6},{6,4},{5,7},{7,5},{8,9},{9,8},{10,11... | collective-permute-start | bytes 1966088 | tf_op jit(solution)/shard_map/ppermute | solution.py:1444
  395.7 148.6 %collective-permute-start.9 = (bf16[256,960]{1,0:T(8,128)(2,1)}, bf16[256,960]{1,0:T(8,128)(2,1)S(1)}, u32[]{:S(2)}, u32[]{:S(2)}) collective-permute-start(bf16[256,960]{1,0:T(8,128)(2,1)} %select_convert_fusion), channel_id=1, source_target_pairs={{0,3},{3,0},{1,2},{2,1},{4,7},{7,4},{5,6},{6,5},{8,11},{11,8},{9,1... | collective-permute-start | bytes 1474568 | tf_op jit(solution)/shard_map/ppermute | solution.py:1444
  (59 other events, 244.0 us)

commit v5 on v4

--- a/solution.py
+++ b/solution.py
@@ -117,7 +117,7 @@
             pltpu.VMEM((tokens, ceil_to(QW, LANE)), F32),
             pltpu.VMEM((tokens, ceil_to(KW, LANE)), F32),
         ],
-        compiler_params=params(wide_limit(weight, 20)),
+        compiler_params=params(wide_limit(weight, 14)),
         name="pre",
     )(state, gain, placed(weight), cosine, sine)
 
@@ -305,7 +305,7 @@
             pltpu.VMEM(info.shape[::-1], F32),
             pltpu.VMEM((3, block, block), F32),
         ],
-        compiler_params=params(16),
+        compiler_params=params(14),
         name="attend_own",
     )(queries, pair, info)
 
@@ -367,7 +367,7 @@
             pltpu.VMEM(info.shape[::-1], F32),
             pltpu.VMEM((2, block, block), F32),
         ],
-        compiler_params=params(16),
+        compiler_params=params(14),
         name="attend_rest",
     )(queries, pair, info, part)
 
@@ -436,7 +436,7 @@
             pltpu.VMEM(info.shape[::-1], F32),
             pltpu.VMEM((2, block, block), F32),
         ],
-        compiler_params=params(20),
+        compiler_params=params(18),
         name="attend_rest_back",
     )(queries, pair, info, attended, logs, grad)
 
@@ -488,7 +488,7 @@
             pltpu.VMEM(info.shape[::-1], F32),
             pltpu.VMEM((3, block, block), F32),
         ],
-        compiler_params=params(20),
+        compiler_params=params(18),
         name="attend_own_back",
     )(queries, pair, info, logs, deltas, grad, part)
 
@@ -592,7 +592,7 @@
             pltpu.VMEM((2, 3, tokens, part), BF),
             pltpu.SemaphoreType.DMA((9,)),
         ],
-        compiler_params=params(wide_limit(gate_w, 30)),
+        compiler_params=params(wide_limit(gate_w, 22)),
         name="post",
     )(state, attended, placed(attn_w), gain, router, active, placed(gate_w), placed(up_w),
       placed(down_w))
@@ -730,7 +730,7 @@
             pltpu.SemaphoreType.DMA((2, 2)),
             pltpu.SemaphoreType.DMA((6,)),
         ],
-        compiler_params=params(wide_limit(gate_w, 34)),
+        compiler_params=params(wide_limit(gate_w, 26)),
         name="post_back",
     )(grad_state, s["update"], s["routed"], s["active"], state, s["midway"], gain, router,
       placed(attn_w), placed(gate_w), placed(up_w), placed(down_w), s["gate"], s["up"])
@@ -788,7 +788,7 @@
             pltpu.VMEM((tokens, ceil_to(QW, LANE)), F32),
             pltpu.VMEM((tokens, ceil_to(KW, LANE)), F32),
         ],
-        compiler_params=params(wide_limit(weight, 24)),
+        compiler_params=params(wide_limit(weight, 16)),
         name="pre_back",
     )(grad_queries, *grad_pairs, partial, state, gain, placed(weight), cosine, sine)
 
@@ -909,7 +909,13 @@
         self.down = [
             (lax.rem(self.z + layers - k, layers) * 2 + self.core, seq) for k in range(layers)
         ]
-        self.peers = [self.sibling, self.over_x, self.over_y] + self.up[1:]
+        self.across = (dp, 3 - seq)
+        self.partner = (dp, jnp.where(self.core == 0, self.over_x[1], self.over_y[1]))
+        self.place_peers = [self.over_x, self.over_y, self.across]
+        self.rank_peers = self.up[1:] + [
+            (lax.rem(self.z + k, layers) * 2 + 1 - self.core, seq) for k in range(layers)
+        ]
+        self.peers = self.place_peers + self.rank_peers
 
     def greet(self):
         barrier = pltpu.get_barrier_semaphore()
@@ -925,12 +931,37 @@
     )
 
 
-def gather_kernel(count, layers, *refs):
-    ins, outs = refs[:count], refs[count : 2 * count]
-    send, recv, keep = refs[2 * count :]
+class Pieces:
+    def __init__(self, ref):
+        self.ref = ref
+        self.shape = (4, ref.shape[2] * ref.shape[3] * ref.shape[4], ref.shape[5])
+
+    def __getitem__(self, index):
+        piece, _, lanes = index
+        whole = self.ref[piece // 2, piece % 2, :, :, :, lanes]
+        return whole.reshape(self.shape[1], whole.shape[-1])
+
+
+def open_kernel(layers, micros, cols, *refs):
+    refs = list(refs)
+
+    def pop(size):
+        taken = refs[:size]
+        del refs[:size]
+        return taken
+
+    count = 4
+    ins = pop(count)
+    small, own_state, other_state, cosine, sine = pop(5)
+    outs = pop(count)
+    gains, active = pop(2 + RECUR), pop(RECUR)
+    info, state, normed, queries, pair, partner, attended, logs = pop(8)
+    ranks_in, places_in, state_in, part, qbuf, kbuf, columns, own_bias, rest_bias = pop(9)
+    send, recv, keep, side_send, side_recv = refs
     here = Place(layers)
     here.greet()
     y, x, z, core = here.y, here.x, here.z, here.core
+    rank, place = z * 2 + core, y * 2 + x
     sent = []
 
     def slot(a, index):
@@ -944,6 +975,16 @@
     def arrive(a, index, landing):
         remote(landing, landing, slot(a, index), here.sibling).wait_recv()
 
+    def aside(index, source, target, peer):
+        copy = remote(source, target, (side_send.at[index], side_recv.at[index]), peer)
+        copy.start()
+        sent.append(copy)
+
+    def arrive_aside(index, landing):
+        remote(
+            landing, landing, (side_send.at[index], side_recv.at[index]), here.sibling
+        ).wait_recv()
+
     def layer(k):
         return lax.rem(z + layers - k, layers)
 
@@ -956,111 +997,171 @@
     for copy in own:
         copy.start()
 
-    def first(k):
-        for a in range(count):
+    for index, peer in enumerate(here.rank_peers):
+        aside(index, small.at[pl.ds(0, 8)], ranks_in.at[rank], peer)
+    first_place = len(here.rank_peers)
+    for index, peer in enumerate(here.place_peers):
+        aside(first_place + index, small.at[pl.ds(8, 8)], places_in.at[place], peer)
+    last = first_place + len(here.place_peers)
+    ranks_in[rank] = small[0:8]
+    places_in[place] = small[8:16]
+
+    def along(arrays, k):
+        for a in arrays:
+            start(a, k, ins[a], outs[a].at[y, x, z, core], here.up[k])
+
+    def first(arrays, k):
+        for a in arrays:
             spot = outs[a].at[y, x, layer(k), core]
             source = ins[a] if k == 0 else spot
             if k:
                 arrive(a, k, spot)
-            start(a, layers + k, source, spot, sides(a)[0])
-            start(a, 2 * layers + k, source, spot, sides(a)[1])
-
-    def second(k):
-        for a in range(count):
-            side = sides(a)[2]
+            start(a, layers + k, source, spot, sides(a + k)[0])
+            start(a, 2 * layers + k, source, spot, sides(a + k)[1])
+
+    def second(arrays, k):
+        for a in arrays:
+            side = sides(a + k)[2]
             spot = outs[a].at[side[0], side[1], layer(k), core]
             arrive(a, layers + k, spot)
-            start(a, 3 * layers + k, spot, spot, sides(a)[1])
-
-    def third(k):
-        for a in range(count):
-            for turn_of, side in enumerate(sides(a)[3]):
+            start(a, 3 * layers + k, spot, spot, sides(a + k)[1])
+
+    def third(arrays, k):
+        for a in arrays:
+            for turn_of, side in enumerate(sides(a + k)[3]):
                 arrive(a, (2 + turn_of) * layers + k, outs[a].at[side[0], side[1], layer(k), core])
             if k == 0:
                 own[a].wait()
             spot = outs[a].at[:, :, layer(k), core]
             start(a, 4 * layers + k, spot, spot, here.sibling)
 
-    def z_sends(k):
-        for a in range(count):
-            start(a, k, ins[a], outs[a].at[y, x, z, core], here.up[k])
-
-    for a in range(count):
-        for k in range(1, layers):
-            start(a, k, ins[a], outs[a].at[y, x, z, core], here.up[k])
-    for k in range(layers + 2):
-        if k < layers:
-            first(k)
-        if 1 <= k <= layers:
-            second(k - 1)
-        if k >= 2:
-            third(k - 2)
-    for k in range(layers):
-        for a in range(count):
-            arrive(a, 4 * layers + k, outs[a].at[:, :, layer(k), 1 - core])
+    def complete(arrays):
+        for k in range(layers):
+            for a in arrays:
+                arrive(a, 4 * layers + k, outs[a].at[:, :, layer(k), 1 - core])
+
+    works = dict(f=first, s=second, t=third)
+
+    def compute(word):
+        if word == "marks":
+            unpack_marks()
+        elif word == "pre":
+            complete((0,))
+            pre_kernel(
+                cols, state, gains[0], Pieces(outs[0]), cosine, sine, normed, queries,
+                pair, qbuf, kbuf,
+            )
+            aside(last + 1, pair, partner, here.partner)
+        elif word == "own":
+            own_kernel(0, queries, pair, info, part, columns, own_bias)
+        else:
+            arrive_aside(last + 1, partner)
+            rest_kernel(0, queries, partner, info, part, attended, logs, columns, rest_bias)
+
+    def unpack_marks():
+        second_pack = jnp.where(core == 0, y == 1, x == 1)
+        outer = is_outer()
+        rows, block = gains[0].shape[1] // (2 * layers), state.shape[0] // 2
+        for index in range(len(here.rank_peers)):
+            arrive_aside(index, ranks_in.at[rank])
+        for index in range(len(here.place_peers)):
+            arrive_aside(first_place + index, places_in.at[place])
+        for index in range(2 * layers):
+            for row, ref in enumerate(gains):
+                ref[:, index * rows : (index + 1) * rows] = ranks_in[index][row : row + 1, :rows]
+        info[...] = jnp.zeros(info.shape, F32)
+        for index, (one, two) in enumerate(zip((0, 3, 1, 2), (1, 2, 0, 3))):
+            marks = places_in[jnp.where(outer, one, two)][:, :block]
+            for row in range(2):
+                info[row : row + 1, index * block : (index + 1) * block] = jnp.where(
+                    second_pack, marks[row * micros + 1 : row * micros + 2], marks[row * micros : row * micros + 1]
+                )
+        columns[...] = info[...].T
+        for r in range(RECUR):
+            active[r][...] = jnp.broadcast_to(
+                jnp.where(columns[0 : 2 * block, 1:2] > r, 1.0, 0.0), (2 * block, LANE)
+            )
+        arrive_aside(last, state_in)
+        high = y == 1
+        state[pl.ds(pl.multiple_of(jnp.where(high, block, 0), block), block)] = own_state[...]
+        state[pl.ds(pl.multiple_of(jnp.where(high, 0, block), block), block)] = state_in[...].astype(F32)
+
+    for word in PLAN:
+        if len(word) > 2:
+            compute(word)
+            continue
+        arrays = (0,) if word[0].isupper() else (1, 2, 3)
+        kind = word[0].lower()
+        if kind == "z":
+            for k in range(1, layers) if len(word) == 1 else (int(word[1]),):
+                along(arrays, k)
+        elif kind == "x":
+            aside(last, other_state, state_in, here.across)
+        else:
+            works[kind](arrays, int(word[1]))
+    complete((1, 2, 3))
     for copy in sent:
         copy.wait_send()
 
 
-def gather_all(parts, layers):
-    count = len(parts)
-    return pl.pallas_call(
-        functools.partial(gather_kernel, count, layers),
-        out_shape=tuple(pltpu.VMEM((2, 2, layers, 2) + part.shape, part.dtype) for part in parts),
-        in_specs=[anywhere] * count,
-        out_specs=(anywhere,) * count,
+PLAN = (
+    "Z", "F0", "x", "F1", "S0", "F2", "S1", "F3", "f0", "z", "S2", "T0", "marks", "S3", "T1", "f1",
+    "T2", "s0", "T3", "pre", "f2", "s1", "t0", "own", "f3", "s2", "t1", "rest", "s3", "t2", "t3",
+)
+
+
+def open_all(parts, small, own_state, other_state, tables, micros, cols):
+    count, tokens, width = len(parts), 2 * own_state.shape[0], own_state.shape[1]
+    ranks = lax.axis_size("dp")
+    layers, seq = ranks // 2, 4
+    wide = ceil_to(KW, LANE)
+    made = pl.pallas_call(
+        functools.partial(open_kernel, layers, micros, cols),
+        out_shape=tuple(pltpu.VMEM((2, 2, layers, 2) + part.shape, part.dtype) for part in parts)
+        + (
+            *[shape((1, width), F32)] * (2 + RECUR),
+            *[shape((tokens, LANE), F32)] * RECUR,
+            shape((8, 2 * tokens), F32),
+            shape((tokens, width), F32),
+            shape((tokens, width), BF),
+            shape((tokens, QW), BF),
+            shape((tokens, 2 * KW), BF),
+            shape((tokens, 2 * KW), BF),
+            shape((tokens, QW), BF),
+            shape((ceil_to(HEADS, 8), tokens), F32),
+        ),
+        in_specs=[vmem] + [anywhere] * (count - 1) + [vmem] * 5,
+        out_specs=(vmem,) + (anywhere,) * (count - 1) + (vmem,) * (10 + 2 * RECUR),
         scratch_shapes=[
+            pltpu.VMEM((ranks, 8) + small.shape[1:], F32),
+            pltpu.VMEM((seq, 8) + small.shape[1:], F32),
+            pltpu.VMEM(other_state.shape, BF),
+            pltpu.VMEM((KV_HEADS, HEAD_DIM + 16, GROUP * tokens), F32),
+            pltpu.VMEM((tokens, ceil_to(QW, LANE)), F32),
+            pltpu.VMEM((tokens, wide), F32),
+            pltpu.VMEM((2 * tokens, 8), F32),
+            pltpu.VMEM((3, tokens // 2, tokens // 2), F32),
+            pltpu.VMEM((2, tokens // 2, tokens // 2), F32),
             pltpu.SemaphoreType.DMA((count, 5 * layers)),
             pltpu.SemaphoreType.DMA((count, 5 * layers)),
             pltpu.SemaphoreType.DMA((count,)),
+            pltpu.SemaphoreType.DMA((ranks + seq,)),
+            pltpu.SemaphoreType.DMA((ranks + seq,)),
         ],
         compiler_params=pltpu.CompilerParams(
-            collective_id=0, has_side_effects=True, vmem_limit_bytes=4 * MIB
+            collective_id=0, has_side_effects=True, vmem_limit_bytes=OPEN_LIMIT * MIB
         ),
-        name="gather_all",
-    )(*parts)
-
-
-def unpack_kernel(rows, down_rows, micros, down, gains, info, active):
-    spot = down.shape[2] - LANE
-    first = LANE - BESIDE
-    late = second_micro()
-    outer = is_outer()
-    here = pl.ds(pl.multiple_of(lax.axis_index("dp") * down_rows, BESIDE), active.shape[1] // 2)
-    block = active.shape[1] // 2
-    for rank in range(down.shape[1] // down_rows):
-        tile = down[0, rank * down_rows : rank * down_rows + LANE, spot:].astype(F32).T
-        gains[:, rank * rows : (rank + 1) * rows] = tile[first : first + gains.shape[0], :rows]
-    info[...] = jnp.zeros(info.shape, F32)
-    for index, (one, two) in enumerate(zip((0, 3, 1, 2), (1, 2, 0, 3))):
-        tile = down[jnp.where(outer, one, two), here, spot:].astype(F32)
-        turned = tile.T
-        span = slice(index * block, (index + 1) * block)
-        for row in range(2):
-            start = first + 2 + RECUR + row * micros
-            info[row : row + 1, span] = jnp.where(
-                late, turned[start + 1 : start + 2], turned[start : start + 1]
-            )
-        if index < 2:
-            depth = jnp.where(late, tile[:, start + 1 : start + 2], tile[:, start : start + 1])
-            for r in range(RECUR):
-                active[r, span] = jnp.broadcast_to(jnp.where(depth > r, 1.0, 0.0), (block, LANE))
-
-
-def unpack(down, rows, tokens, ranks, micros):
-    down_rows = down.shape[1] // ranks
-    return pl.pallas_call(
-        functools.partial(unpack_kernel, rows, down_rows, micros),
-        out_shape=(
-            shape((8, rows * ranks), F32),
-            shape((8, 4 * tokens), F32),
-            shape((RECUR, 2 * tokens, LANE), F32),
-        ),
-        in_specs=[vmem],
-        out_specs=(vmem,) * 3,
-        compiler_params=params(8),
-        name="unpack",
-    )(pin(down))
+        name="open_all",
+    )(*parts, small, own_state, other_state, *tables)
+    gathered, gains, actives = made[:count], made[count : count + 2 + RECUR], made[count + 2 + RECUR :]
+    names = ("info", "state", "normed", "queries", "pair", "partner", "attended", "logs")
+    return gathered, gains, actives[:RECUR], dict(zip(names, actives[RECUR:]))
+
+
+OPEN_LIMIT = 32
+
+
+SECOND_AT, THIRD_AT = 2, 2
 
 
 def finish_kernel(layers, count, low_col, *refs):
@@ -1076,22 +1177,16 @@
     )
     (small,) = pop(1)
     outs = pop(4)
-    held, core_in, first_in, second_in, done, z_in = (pop(4) for _ in range(6))
+    held, core_in, first_in, second_in, z_in = (pop(4) for _ in range(5))
     raw, left, right, ffn_right, stage, down_stage = pop(6)
-    send, recv, keep, load = refs
+    send, recv, load = refs
     here = Place(layers)
     here.greet()
     y, x, z, core = here.y, here.x, here.z, here.core
     tokens = raw.shape[0] // count
-    sent = []
 
     def slot(a, index):
         return send.at[a, index], recv.at[a, index]
-
-    def start(a, index, source, target, peer):
-        copy = remote(source, target, slot(a, index), peer)
-        copy.start()
-        sent.append(copy)
 
     def arrive(a, index, landing):
         remote(landing, landing, slot(a, index), here.sibling).wait_recv()
@@ -1132,49 +1227,67 @@
             rows = slice(i * tokens, (i + 1) * tokens)
             left[spot, :, rows] = raw[rows].T
 
-    def sends(a, piece, source):
+    def column_of(piece):
+        return lax.rem(1 - y + lax.div(piece, 2), 2), lax.rem(1 - x + lax.rem(piece, 2), 2)
+
+    def spot_of(a, piece):
         if a == 3:
-            theirs = source.at[:, :, 1 - core]
-            ours = source.at[:, :, core]
-            spot = (piece,)
-        else:
-            theirs = source.at[:, 1 - core]
-            ours = source.at[:, core]
-            spot = (slice(None), lax.div(piece, 2), lax.rem(piece, 2))
-        return (
-            remote(
-                theirs, core_in[a].at[spot], (send.at[a, piece], recv.at[a, piece]), here.sibling
-            ),
-            pltpu.make_async_copy(ours, held[a].at[spot], keep.at[a, piece]),
+            return (lax.rem(z + piece + 1, layers),)
+        return (slice(None),) + column_of(piece)
+
+    def number_of(a, piece):
+        if a == 3:
+            return lax.rem(z + piece + 1, layers)
+        row, column = column_of(piece)
+        return row * 2 + column
+
+    def staged(a, spot, whose):
+        lead = (spot, slice(None), slice(None)) if a == 3 else (spot, slice(None))
+        return (down_stage if a == 3 else stage), lead + (whose,)
+
+    def handed(a, piece):
+        ref, place = staged(a, lax.rem(piece, 2), 1 - core)
+        return remote(
+            ref.at[place], core_in[a].at[spot_of(a, piece)], (send.at[a, piece], recv.at[a, piece]),
+            here.sibling,
         )
 
-    def products(a, fetch, multiply, stages):
-        go(fetch(0, 0))
+    def add_cores(a, piece):
+        spot = spot_of(a, piece)
+        arrive(a, piece, core_in[a].at[spot])
+        ref, place = staged(a, lax.rem(piece, 2), core)
+        held[a][spot] = added(held[a], ref[place], core_in[a][spot])
+
+    def products(a, fetch, multiply, hooks):
+        go(fetch(number_of(a, 0), 0))
 
         def step(piece, carry):
             spot = lax.rem(piece, 2)
-            hold(fetch(piece, spot))
+            hold(fetch(number_of(a, piece), spot))
 
             @pl.when(piece < 3)
             def _():
-                go(fetch(piece + 1, 1 - spot))
+                go(fetch(number_of(a, piece + 1), 1 - spot))
 
             @pl.when(piece >= 2)
             def _():
-                out, own = sends(a, piece - 2, stages.at[spot])
-                out.wait_send()
-                own.wait()
-
-            multiply(piece, spot)
-            for copy in sends(a, piece, stages.at[spot]):
-                copy.start()
+                handed(a, piece - 2).wait_send()
+
+            multiply(number_of(a, piece), spot)
+            handed(a, piece).start()
+
+            @pl.when(piece >= 1)
+            def _():
+                add_cores(a, piece - 1)
+
+            for at, hook in hooks:
+                pl.when(piece == at)(hook)
             return carry
 
         lax.fori_loop(0, 4, step, 0)
+        add_cores(a, 3)
         for piece in (2, 3):
-            out, own = sends(a, piece, stages.at[piece % 2])
-            out.wait_send()
-            own.wait()
+            handed(a, piece).wait_send()
 
     def store(spot, result):
         rows = stage.shape[3]
@@ -1216,43 +1329,62 @@
                 down_stage[place] = result[index * rows : (index + 1) * rows]
                 down_stage[place + (slice(None), slice(cols, None))] = small[piece, index]
 
-    def first(a):
-        for piece in range(4):
-            spot = (piece,) if a == 3 else (slice(None), piece // 2, piece % 2)
-            arrive(a, piece, core_in[a].at[spot])
-        for k in range(layers):
-            held[a][k] = added(held[a], held[a][k], core_in[a][k])
-        for k in range(layers):
+    def over(a, k):
+        index = 4 + k
+        if k % 2 == 0:
+            source, peer = held[a].at[layer(k), :, 1 - x], here.over_x
+        else:
+            source, peer = held[a].at[layer(k), 1 - y], here.over_y
+        return remote(source, first_in[a].at[k], slot(a, index), peer)
+
+    def first_odd(a):
+        for k in range(1, layers, 2):
+            over(a, k).start()
+
+    def first_even(a):
+        for k in range(0, layers, 2):
+            over(a, k).start()
+
+    order = [*range(1, layers, 2), *range(0, layers, 2)]
+
+    def second(a):
+        for k in order:
+            second_layer(a, k)
+
+    def second_layer(a, k):
+        at = layer(k)
+        arrive(a, 4 + k, first_in[a].at[k])
+        for i in range(2):
             if k % 2 == 0:
-                start(a, 4 + k, held[a].at[layer(k), :, 1 - x], first_in[a].at[k], here.over_x)
+                held[a][at, i, x] = added(held[a], held[a][at, i, x], first_in[a][k, i])
             else:
-                start(a, 4 + k, held[a].at[layer(k), 1 - y], first_in[a].at[k], here.over_y)
-
-    def second(a):
-        for k in range(layers):
-            at = layer(k)
-            arrive(a, 4 + k, first_in[a].at[k])
-            for i in range(2):
-                if k % 2 == 0:
-                    held[a][at, i, x] = added(held[a], held[a][at, i, x], first_in[a][k, i])
-                else:
-                    held[a][at, y, i] = added(held[a], held[a][at, y, i], first_in[a][k, i])
-            index = 4 + layers + k
-            if k % 2 == 0:
-                start(a, index, held[a].at[at, 1 - y, x], second_in[a].at[k], here.over_y)
-            else:
-                start(a, index, held[a].at[at, y, 1 - x], second_in[a].at[k], here.over_x)
+                held[a][at, y, i] = added(held[a], held[a][at, y, i], first_in[a][k, i])
+        across(a, k).start()
+
+    def across(a, k):
+        if k % 2 == 0:
+            source, peer = held[a].at[layer(k), 1 - y, x], here.over_y
+        else:
+            source, peer = held[a].at[layer(k), y, 1 - x], here.over_x
+        return remote(source, second_in[a].at[k], slot(a, 4 + layers + k), peer)
+
+    def along(a, k):
+        source = held[a].at[layer(k), y, x]
+        return remote(source, z_in[a].at[k], slot(a, 4 + 2 * layers + k), here.up[k + 1])
 
     def third(a):
-        for k in range(layers):
-            arrive(a, 4 + layers + k, second_in[a].at[k])
-            done[a][k] = added(held[a], held[a][layer(k), y, x], second_in[a][k])
-            if k < layers - 1:
-                index = 4 + 2 * layers + k
-                start(a, index, done[a].at[k], z_in[a].at[k], here.up[k + 1])
+        for k in order:
+            third_layer(a, k)
+
+    def third_layer(a, k):
+        arrive(a, 4 + layers + k, second_in[a].at[k])
+        spot = (layer(k), y, x)
+        held[a][spot] = added(held[a], held[a][spot], second_in[a][k])
+        if k < layers - 1:
+            along(a, k).start()
 
     def fourth(a):
-        total = done[a][layers - 1].astype(F32)
+        total = held[a][z, y, x].astype(F32)
         for k in range(layers - 1):
             arrive(a, 4 + 2 * layers + k, z_in[a].at[k])
             total = total + z_in[a][k].astype(F32)
@@ -1281,33 +1413,48 @@
     normed_left = load_left(1, normed)
     go(normed_left)
     go(down_right)
-    products(0, fetch_of(2, grad_gate), ffn_product(grad_gate), stage)
-    first(0)
+
+    def columns_out(a):
+        return [(2, lambda: first_odd(a)), (3, lambda: first_even(a))]
+
+    products(0, fetch_of(2, grad_gate), ffn_product(grad_gate), columns_out(0))
     hold(normed_left)
     turn_left(1)
     attended_left = load_left(0, attended)
     go(attended_left)
-    products(1, fetch_of(2, grad_up), ffn_product(grad_up), stage)
-    first(1)
-    second(0)
+    products(
+        1, fetch_of(2, grad_up), ffn_product(grad_up), [(SECOND_AT, lambda: second(0))] + columns_out(1)
+    )
     hold(attended_left)
     turn_left(0)
-    products(2, fetch_attn, attn_product, stage)
-    first(2)
-    second(1)
-    third(0)
+    products(
+        2, fetch_attn, attn_product,
+        [(SECOND_AT, lambda: second(1)), (THIRD_AT, lambda: third(0))] + columns_out(2),
+    )
     hold(down_right)
-    products(3, fetch_of(2, hidden), down_product, down_stage)
-    first(3)
-    second(2)
-    third(1)
-    second(3)
+    layers_out = [(k + 1, lambda k=k: over(3, k).start()) for k in range(layers - 1)]
+    products(
+        3, fetch_of(2, hidden), down_product,
+        [(SECOND_AT, lambda: second(2)), (THIRD_AT, lambda: third(1))] + layers_out,
+    )
+    over(3, layers - 1).start()
     third(2)
-    third(3)
+    second_layer(3, 0)
+    second_layer(3, 1)
+    third_layer(3, 0)
+    second_layer(3, 2)
+    third_layer(3, 1)
+    second_layer(3, 3)
+    third_layer(3, 2)
+    third_layer(3, 3)
     for a in range(4):
         fourth(a)
-    for copy in sent:
-        copy.wait_send()
+    for a in range(4):
+        for k in range(layers):
+            over(a, k).wait_send()
+            across(a, k).wait_send()
+            if k < layers - 1:
+                along(a, k).wait_send()
 
 
 def finish(normed, packed, attended, branch, ffn_in, grad_gate, grad_up, hidden, grad_ffn, small, low_col):
@@ -1337,7 +1484,6 @@
             *buffers(layers, 2, 2),
             *buffers(layers, 2),
             *buffers(layers),
-            *buffers(layers),
             *buffers(layers - 1),
             pltpu.VMEM((count * tokens, width), BF),
             pltpu.VMEM((2, width, count * tokens), BF),
@@ -1347,7 +1493,6 @@
             pltpu.VMEM((2, 2, 2, 2, down_rows, cols), BF),
             pltpu.SemaphoreType.DMA((4, 4 + 3 * layers)),
             pltpu.SemaphoreType.DMA((4, 4 + 3 * layers)),
-            pltpu.SemaphoreType.DMA((4, 4)),
             pltpu.SemaphoreType.DMA((10, count)),
         ],
         compiler_params=pltpu.CompilerParams(
@@ -1468,9 +1613,10 @@
     return split(inputs), split(cotangent), tables
 
 
-def paired_plan(prepared, info, actives, block_params):
-    (own_state, other_state), (own_grad, other_grad), (cosine, sine) = prepared
-    tokens = own_state.shape[0]
+def paired_plan(opened, actives, grads, tables, block_params):
+    (own_grad, other_grad), (cosine, sine) = grads, tables
+    info, state = opened["info"], opened["state"]
+    tokens = own_grad.shape[0]
     late = lax.axis_index("seq") >= 2
     attn_g, ffn_g, routers, attn_w, gate_w, up_w, down_w, cols, used = block_params
 
@@ -1485,17 +1631,22 @@
         second = second_micro()
         return jnp.stack([jnp.where(second, other, own), jnp.where(second, own, other)], axis=0)[:, None]
 
-    state = join(own_state, other_state)
     saved = []
     for r in range(RECUR):
         active = actives[r]
-        normed, queries, pair = pre_part(state, attn_g, attn_w, cosine, sine, cols)
-        partner = swap(pair, PARTNERS)
         if r == 0:
-            other_grad, partner = lax.optimization_barrier((other_grad, partner))
-            other_grad = swap(other_grad, ACROSS)
-        part = attend_own(queries, pair, info, r)
-        attended, logs = attend_rest(queries, partner, info, part, r)
+            normed, queries, pair, partner, attended, logs = (
+                opened[name]
+                for name in ("normed", "queries", "pair", "partner", "attended", "logs")
+            )
+        else:
+            normed, queries, pair = pre_part(state, attn_g, attn_w, cosine, sine, cols)
+            partner = swap(pair, PARTNERS)
+            if r == 1:
+                other_grad, partner = lax.optimization_barrier((other_grad, partner))
+                other_grad = swap(other_grad, ACROSS)
+            part = attend_own(queries, pair, info, r)
+            attended, logs = attend_rest(queries, partner, info, part, r)
         after = post_part(
             state, attended, attn_w, ffn_g, routers[r], active, gate_w, up_w, down_w, used
         )
@@ -1536,45 +1687,45 @@
     both = ("seq", "dp")
 
     attn_local = jnp.concatenate([query_weight, key_weight, value_weight, out_weight], axis=1)
-    down_rows, down_cols = down_weight.shape
-    marks = jnp.concatenate([segments[:, 0], depths[:, 0]], axis=0).T.astype(BF)
-    small = jnp.concatenate([attn_gain[:, None], ffn_gain[:, None], router_weight], axis=1)
+    down_cols = down_weight.shape[1]
+    span = ceil_to(max(rows, tokens), LANE)
+    small = jnp.concatenate([attn_gain[None], ffn_gain[None], router_weight.T], axis=0).astype(F32)
+    marks = jnp.concatenate([segments[:, 0], depths[:, 0]], axis=0).astype(F32)
     small = jnp.concatenate(
         [
-            jnp.pad(small, ((0, down_rows - rows), (0, 0))),
-            jnp.pad(marks, ((0, down_rows - tokens), (0, BESIDE - 2 - RECUR - 2 * micros))),
+            jnp.pad(small, ((0, 8 - small.shape[0]), (0, span - rows))),
+            jnp.pad(marks, ((0, 8 - 2 * micros), (0, span - tokens))),
         ],
-        axis=1,
+        axis=0,
     )
     parts = (
-        attn_local, gate_weight, up_weight, jnp.concatenate([down_weight, small], axis=1)
+        attn_local, gate_weight, up_weight, jnp.pad(down_weight, ((0, 0), (0, BESIDE)))
     )
     direct = micros == 2 and (seq, ranks) == (4, 8)
     if direct:
         states, grads, tables = paired_start(inputs, cotangent)
-        states = (states[0], swap(states[1], ACROSS))
-        parts, own, grads, tables = lax.optimization_barrier((parts, states[0], grads, tables))
-        gathered = gather_all(parts, ranks // 2)
-        prepared = ((own, states[1]), grads, tables)
+        parts, small, states, grads, tables = lax.optimization_barrier(
+            (parts, small, states, grads, tables)
+        )
+        gathered, gains, actives, opened = open_all(
+            parts, small, *states, tables, micros, (qc, kc)
+        )
     else:
         gathered = [lax.all_gather(part, both, axis=0, tiled=False) for part in parts]
+        small = lax.all_gather(small, both, axis=0, tiled=False)
+        small = small.reshape(seq, ranks, *small.shape[1:])
+        marks = lax.dynamic_index_in_dim(small, lax.axis_index("dp"), 1, keepdims=False)
+        marks = marks[:, 8 : 8 + 2 * micros, :tokens].reshape(seq, 2, micros, tokens)
+        small = small[0, :, : 2 + RECUR, :rows].transpose(1, 0, 2).reshape(2 + RECUR, width)
+        gains = [small[row : row + 1] for row in range(2 + RECUR)]
     attn_w, gate_w, up_w, down_w = (full.reshape(seq, -1, full.shape[-1]) for full in gathered)
-    if direct:
-        small, info, actives = unpack(down_w, rows, tokens, ranks, micros)
-    else:
-        small = down_w[:, :, down_cols:].reshape(seq, ranks, down_rows, BESIDE).astype(F32)
-        marks = lax.dynamic_index_in_dim(small, lax.axis_index("dp"), 1, keepdims=False)
-        marks = marks[:, :tokens, 2 + RECUR : 2 + RECUR + 2 * micros].transpose(0, 2, 1)
-        marks = marks.reshape(seq, 2, micros, tokens)
-        small = small[0, :, :rows, : 2 + RECUR].reshape(width, 2 + RECUR).T
-    attn_g, ffn_g = small[0:1], small[1:2]
-    routers = [small[2 + r : 3 + r] for r in range(RECUR)]
+    attn_g, ffn_g, *routers = gains
     used = qc + 2 * kc
     total_cols = attn_w.shape[2]
     low_col = used // LANE * LANE
     block_params = (attn_g, ffn_g, routers, attn_w, gate_w, up_w, down_w, (qc, kc), used)
     if direct:
-        outputs, input_grad, saved = paired_plan(prepared, info, actives, block_params)
+        outputs, input_grad, saved = paired_plan(opened, actives, grads, tables, block_params)
     else:
         outputs, input_grad, saved = row_plan(inputs, cotangent, depths, marks, block_params)
     flat = [steps[r] for r in reversed(range(RECUR)) for steps in saved]
@@ -1588,12 +1739,12 @@
     small_sum = small_sum.T.reshape(ranks, rows, 2 + RECUR)
     if direct:
         small_sum = jnp.pad(
-            small_sum, ((0, 0), (0, down_rows - rows), (0, BESIDE - 2 - RECUR))
+            small_sum, ((0, 0), (0, down_weight.shape[0] - rows), (0, BESIDE - 2 - RECUR))
         ).astype(BF)
         gate_grad, up_grad, attn_grad, down_grad = finish(
             every("normed"), every("packed"), every("attended"), every("grad_branch"),
             every("ffn_in"), every("grad_gate"), every("grad_up"), every("hidden"),
-            every("grad_ffn"), small_sum.reshape(ranks // 2, 2, down_rows, BESIDE), low_col,
+            every("grad_ffn"), small_sum.reshape(ranks // 2, 2, -1, BESIDE), low_col,
         )
         small_own = down_grad[:rows, down_cols : down_cols + 2 + RECUR].T
     else:

time: 554 us -> 522 us (0.942)
  Pallas kernels: 451 us -> 414 us
  local copies, waits for them, and re-layouts: 46.6 us -> 64.5 us
  starting transfers between devices: 18.1 us -> 9.08 us
    pallas_call x1, Pallas kernels: 139 us -> 118 us  [finish(): pl.pallas_call(functools.partial(finish_kernel, layers, count, low_col),...]
    unnamed x176 -> x207, local copies, waits for them, and re-layouts: 36.4 us -> 54.2 us
    pallas_call x2 -> x1, Pallas kernels: 101 us -> 116 us  [open_all(): pl.pallas_call(functools.partial(open_kernel, layers, micros, cols), out_...]
    pallas_call x3, Pallas kernels: 60.3 us -> 50.8 us  [post_back(): pl.pallas_call(functools.partial(post_back_kernel, used, width // pieces)...]
    ppermute x10 -> x8, starting transfers between devices: 18.1 us -> 9.08 us  [swap(): return lax.ppermute(array, ('dp', 'seq'), moves)]
    pallas_call x3, Pallas kernels: 52 us -> 44.7 us  [post_part(): pl.pallas_call(functools.partial(post_kernel, used, width // pieces), out...]
    pallas_call x3 -> x2, Pallas kernels: 15.6 us -> 10.4 us  [attend_rest(): pl.pallas_call(functools.partial(rest_kernel, recursion), out_shape=(shap...]
    pallas_call x3 -> x2, Pallas kernels: 13.2 us -> 8.68 us  [attend_own(): pl.pallas_call(functools.partial(own_kernel, recursion), out_shape=shape(...]
  transfers between devices with their start and end apart: 10 -> 8, of which waited for: 5 -> 4; matrix products, arithmetic and copies ran while one was open for 5% -> 3% of each run, Pallas kernels for 61% -> 39%
where the time goes in v5:
time: 522 us; the launch traced here: 518 us
  Pallas kernels  414 us (79%)
  local copies, waits for them, and re-layouts  64.5 us (12%)
  waiting for transfers between devices  17.4 us (3%)
  other arithmetic  11.1 us (2%)
  starting transfers between devices  9.08 us (2%)
    pallas_call x1, Pallas kernels, finish(): pl.pallas_call(functools.partial(finish_kernel, layers, count, low_col),...  118 us
    pallas_call x1, Pallas kernels, open_all(): pl.pallas_call(functools.partial(open_kernel, layers, micros, cols), out_...  116 us
    unnamed x207, local copies, waits for them, and re-layouts  54.2 us
    pallas_call x3, Pallas kernels, post_back(): pl.pallas_call(functools.partial(post_back_kernel, used, width // pieces)...  50.8 us
    pallas_call x3, Pallas kernels, post_part(): pl.pallas_call(functools.partial(post_kernel, used, width // pieces), out...  44.7 us
    pallas_call x3, Pallas kernels, attend_own_back(): pl.pallas_call(functools.partial(own_back_kernel, recursion), out_shape=(...  26 us
    pallas_call x3, Pallas kernels, attend_rest_back(): pl.pallas_call(functools.partial(rest_back_kernel, recursion), out_shape=...  19.1 us
    ppermute x8, waiting for transfers between devices, swap(): return lax.ppermute(array, ('dp', 'seq'), moves)  17.4 us
  transfers between devices with their start and end apart: 8, of which 4 were waited for; matrix products, arithmetic and copies ran while one was open for 3% of the time, Pallas kernels for 39%

profile of v5, /device:TPU:0, one launch (start us, length us, event | category | flops | bytes accessed | tf_op | source)
XLA Modules:
  0.0 517.8 jit_solution(4494443797692307475)
XLA Ops:
  3.0 2.9 fusion.18
  7.4 2.5 copy.67
  9.9 3.1 select_bitcast_fusion
  18.4 116.1 %open_all.1 = (bf16[2,2,4,2,120,640]{5,4,3,2,1,0:T(8,128)(2,1)S(1)}, bf16[2,2,4,2,120,640]{5,4,3,2,1,0:T(8,128)(2,1)S(1)}, bf16[2,2,4,2,120,640]{5,4,3,2,1,0:T(8...) custom-call(bf16[120,640]{1,0:T(8,128)(2,1)S(1)} %pad_maximum_fusion, ...), custom_call_target="tpu_custom_call" | custom-call | tf_op jit(solution)/shard_map/open_all/pallas_call | solution.py:1118
  136.8 6.0 %copy-done.5 = bf16[2,2,4,2,120,640]{5,4,3,2,1,0:T(8,128)(2,1)S(1)} copy-done((bf16[2,2,4,2,120,640]{5,4,3,2,1,0:T(8,128)(2,1)S(1)}, bf16[2,2,4,2,120,640]{5,4,3,2,1,0:T(8,128)(2,1)}, u32[]{:S(2)}) %copy-start.5) | copy-done | bytes 4915224
  145.6 14.9 %post.3 = (f32[512,960]{1,0:T(8,128)S(1)}, bf16[512,960]{1,0:T(8,128)(2,1)S(1)}, bf16[4,512,640]{2,1,0:T(8,128)(2,1)S(1)}, bf16[4,512,640]{2,1,0:T(8,128)(2,1)},...) custom-call(f32[512,960]{1,0:T(8,128)S(1)} %copy-done.10, ...), custom_call_target="tpu_custom_call" | custom-call | tf_op jit(solution)/shard_map/post/pallas_call | solution.py:572
  162.6 3.6 pre.2
  166.9 10.0 %collective-permute-done.pair = bf16[512,640]{1,0:T(8,128)(2,1)S(1)} collective-permute-done((bf16[512,640]{1,0:T(8,128)(2,1)S(1)}, bf16[512,640]{1,0:T(8,128)(2,1)S(1)}, u32[]{:S(2)}, u32[]{:S(2)}) %collective-permute-start) | collective-permute-done | bytes 655392 | tf_op jit(solution)/shard_map/ppermute | solution.py:1589
  177.8 4.4 attend_own.2.part
  182.2 5.1 attend_rest.2
  187.4 14.9 %post.4 = (f32[512,960]{1,0:T(8,128)S(1)}, bf16[512,960]{1,0:T(8,128)(2,1)S(1)}, bf16[4,512,640]{2,1,0:T(8,128)(2,1)S(1)}, bf16[4,512,640]{2,1,0:T(8,128)(2,1)},...) custom-call(f32[512,960]{1,0:T(8,128)S(1)} %get-tuple-element.149.st, ...), custom_call_target="tpu_custom_call" | custom-call | tf_op jit(solution)/shard_map/post/pallas_call | solution.py:572
  204.3 3.6 pre.3
  209.0 4.3 attend_own.3.part
  215.1 3.6 collective-permute-done.1.pair
  218.6 5.3 %attend_rest.3 = (bf16[512,960]{1,0:T(8,128)(2,1)S(1)}, f32[16,512]{1,0:T(8,128)S(1)}) custom-call(bf16[512,960]{1,0:T(8,128)(2,1)S(1)} %get-tuple-element.160.queries, bf16[512,640]{1,0:T(8,128)(2,1)S(1)} %collective-permute-done.1.pair, f32[8,1024]{1,0:T(8,128)S(1)} %get-tuple-element.155.info, f32[5,80,1536]{2,1,0:T(8,128)S(1)} %attend_own.3.part), custom_call_target="tpu_custom_call" | custom-call | tf_op jit(solution)/shard_map/attend_rest/pallas_call | solution.py:361
  224.0 14.9 %post.5 = (f32[512,960]{1,0:T(8,128)S(1)}, bf16[512,960]{1,0:T(8,128)(2,1)S(1)}, bf16[4,512,640]{2,1,0:T(8,128)(2,1)S(1)}, bf16[4,512,640]{2,1,0:T(8,128)(2,1)},...) custom-call(f32[512,960]{1,0:T(8,128)S(1)} %get-tuple-element.159.st, ...), custom_call_target="tpu_custom_call" | custom-call | tf_op jit(solution)/shard_map/post/pallas_call | solution.py:572
  248.9 16.7 %post_back.3 = (bf16[512,960]{1,0:T(8,128)(2,1)S(1)}, f32[512,960]{1,0:T(8,128)S(1)}, f32[1,960]{1,0:T(1,128)S(1)}, f32[1,960]{1,0:T(1,128)S(1)}, bf16[4,512,256...) custom-call(f32[512,960]{1,0:T(8,128)S(1)} %copy-done.19, ...), custom_call_target="tpu_custom_call" | custom-call | tf_op jit(solution)/shard_map/post_back/pallas_call | solution.py:709
  267.5 6.0 %attend_rest_back.3 = (bf16[512,640]{1,0:T(8,128)(2,1)S(1)}, f32[5,64,1536]{2,1,0:T(8,128)S(1)}, f32[16,512]{1,0:T(8,128)S(1)}) custom-call(bf16[512,960]{1,0:T(8,128)(2,1)S(1)} %get-tuple-element.160.queries, bf16[512,640]{1,0:T(8,128)(2,1)S(1)} %copy-done.35, f32[8,1024]{1,0:T(8,128)S(1)} %get-tuple-element.155.info, ...), custom_call_target="tpu_custom_call" | custom-call | tf_op jit(solution)/shard_map/attend_rest_back/pallas_call | solution.py:426
  274.5 8.7 %attend_own_back.3 = (f32[512,960]{1,0:T(8,128)S(1)}, f32[512,640]{1,0:T(8,128)S(1)}) custom-call(bf16[512,960]{1,0:T(8,128)(2,1)S(1)} %get-tuple-element.160.queries, bf16[512,640]{1,0:T(8,128)(2,1)S(1)} %get-tuple-element.161.pair, f32[8,1024]{1,0:T(8,128)S(1)} %get-tuple-element.155.info, f32[16,512]{1,0:T(8,128)S(1)} %get-tuple-element.171.logs, ...), custom_call_target="tpu_custom_call" | custom-call | tf_op jit(solution)/shard_map/attend_own_back/pallas_call | solution.py:482
  284.2 4.3 pre_back.3
  289.9 17.2 %post_back.4 = (bf16[512,960]{1,0:T(8,128)(2,1)S(1)}, f32[512,960]{1,0:T(8,128)S(1)}, f32[1,960]{1,0:T(1,128)S(1)}, f32[1,960]{1,0:T(1,128)S(1)}, bf16[4,512,256...) custom-call(f32[512,960]{1,0:T(8,128)S(1)} %get-tuple-element.186.gr, ...), custom_call_target="tpu_custom_call" | custom-call | tf_op jit(solution)/shard_map/post_back/pallas_call | solution.py:709
  307.2 6.1 %attend_rest_back.4 = (bf16[512,640]{1,0:T(8,128)(2,1)S(1)}, f32[5,64,1536]{2,1,0:T(8,128)S(1)}, f32[16,512]{1,0:T(8,128)S(1)}) custom-call(bf16[512,960]{1,0:T(8,128)(2,1)S(1)} %copy-done.13, bf16[512,640]{1,0:T(8,128)(2,1)S(1)} %copy-done.33, f32[8,1024]{1,0:T(8,128)S(1)} %get-tuple-element.155.info, bf16[512,960]{1,0:T(8,128)(2,1)S(1)} %copy-done.17, ...), custom_call_target="tpu_custom_call" | custom-call | tf_op jit(solution)/shard_map/attend_rest_back/pallas_call | solution.py:426
  316.1 8.7 %attend_own_back.4 = (f32[512,960]{1,0:T(8,128)S(1)}, f32[512,640]{1,0:T(8,128)S(1)}) custom-call(bf16[512,960]{1,0:T(8,128)(2,1)S(1)} %copy-done.13, bf16[512,640]{1,0:T(8,128)(2,1)S(1)} %copy-done.31, f32[8,1024]{1,0:T(8,128)S(1)} %get-tuple-element.155.info, f32[16,512]{1,0:T(8,128)S(1)} %get-tuple-element.170.logs, ...), custom_call_target="tpu_custom_call" | custom-call | tf_op jit(solution)/shard_map/attend_own_back/pallas_call | solution.py:482
  324.9 2.9 collective-permute-done.5.refs_2_
  327.7 4.2 pre_back.4
  333.3 16.9 %post_back.5 = (bf16[512,960]{1,0:T(8,128)(2,1)S(1)}, f32[512,960]{1,0:T(8,128)S(1)}, f32[1,960]{1,0:T(1,128)S(1)}, f32[1,960]{1,0:T(1,128)S(1)}, bf16[4,512,256...) custom-call(f32[512,960]{1,0:T(8,128)S(1)} %get-tuple-element.199.gr, ...), custom_call_target="tpu_custom_call" | custom-call | tf_op jit(solution)/shard_map/post_back/pallas_call | solution.py:709
  350.3 7.0 %attend_rest_back.5 = (bf16[512,640]{1,0:T(8,128)(2,1)}, f32[5,64,1536]{2,1,0:T(8,128)S(1)}, f32[16,512]{1,0:T(8,128)S(1)}) custom-call(bf16[512,960]{1,0:T(8,128)(2,1)S(1)} %copy-done.23, bf16[512,640]{1,0:T(8,128)(2,1)S(1)} %copy-done.71, f32[8,1024]{1,0:T(8,128)S(1)} %get-tuple-element.155.info, bf16[512,960]{1,0:T(8,128)(2,1)S(1)} %copy-done.15, ...), custom_call_target="tpu_custom_call" | custom-call | tf_op jit(solution)/shard_map/attend_rest_back/pallas_call | solution.py:426
  360.4 3.3 copy.58
  366.5 8.5 %attend_own_back.5 = (f32[512,960]{1,0:T(8,128)S(1)}, f32[512,640]{1,0:T(8,128)S(1)}) custom-call(bf16[512,960]{1,0:T(8,128)(2,1)S(1)} %copy-done.24, bf16[512,640]{1,0:T(8,128)(2,1)S(1)} %copy-done.70, f32[8,1024]{1,0:T(8,128)S(1)} %get-tuple-element.155.info, f32[16,512]{1,0:T(8,128)S(1)} %get-tuple-element.168.logs, ...), custom_call_target="tpu_custom_call" | custom-call | tf_op jit(solution)/shard_map/attend_own_back/pallas_call | solution.py:482
  375.8 2.4 copy-done.1
  379.3 4.4 pre_back.5
  388.8 117.7 %finish.1 = (f32[120,640]{1,0:T(8,128)}, f32[120,640]{1,0:T(8,128)}, f32[120,640]{1,0:T(8,128)}, f32[320,256]{1,0:T(8,128)}) custom-call(bf16[512,960]{1,0:T(8,128)(2,1)} %copy-done.56, bf16[512,960]{1,0:T(8,128)(2,1)} %copy-done.54, bf16[512,960]{1,0:T(8,128)(2,1)} %get-tuple-element.215.refs_2_, bf16[4,512,512]{2,1,0:T(8,128)(2,1)} %copy-done.37, ...), custom_call_target="tpu_custom_call" | custom-call | tf_op jit(solution)/shard_map/finish/pallas_call | solution.py:1477
  (252 shorter events, 65.3 us)
Async XLA Ops:
  136.8 23.7 %copy-start.47 = (f32[512,128]{1,0:T(8,128)}, f32[512,128]{1,0:T(8,128)S(1)}, u32[]{:S(2)}) copy-start(f32[512,128]{1,0:T(8,128)S(1)} %get-tuple-element.145.active) | copy-start | bytes 786436
  136.8 50.6 %copy-start.49 = (f32[512,128]{1,0:T(8,128)}, f32[512,128]{1,0:T(8,128)S(1)}, u32[]{:S(2)}) copy-start(f32[512,128]{1,0:T(8,128)S(1)} %get-tuple-element.158.active) | copy-start | bytes 786436
  136.8 87.2 %copy-start.2 = (bf16[2,2,4,2,120,640]{5,4,3,2,1,0:T(8,128)(2,1)}, bf16[2,2,4,2,120,640]{5,4,3,2,1,0:T(8,128)(2,1)S(1)}, u32[]{:S(2)}) copy-start(bf16[2,2,4,2,120,640]{5,4,3,2,1,0:T(8,128)(2,1)S(1)} %get-tuple-element.146) | copy-start | bytes 14745604
  136.8 87.2 %copy-start.51 = (f32[512,128]{1,0:T(8,128)}, f32[512,128]{1,0:T(8,128)S(1)}, u32[]{:S(2)}) copy-start(f32[512,128]{1,0:T(8,128)S(1)} %get-tuple-element.164.active) | copy-start | bytes 786436
  136.8 196.5 %copy-start = (bf16[2,2,4,2,120,640]{5,4,3,2,1,0:T(8,128)(2,1)}, bf16[2,2,4,2,120,640]{5,4,3,2,1,0:T(8,128)(2,1)S(1)}, u32[]{:S(2)}) copy-start(bf16[2,2,4,2,120,640]{5,4,3,2,1,0:T(8,128)(2,1)S(1)} %get-tuple-element.142) | copy-start | bytes 14745604
  162.5 24.8 %copy-start.6 = (f32[512,960]{1,0:T(8,128)}, f32[512,960]{1,0:T(8,128)S(1)}, u32[]{:S(2)}) copy-start(f32[512,960]{1,0:T(8,128)S(1)} %get-tuple-element.149.state.refs_4_) | copy-start | bytes 5898244
  162.5 14.4 %copy-start.78 = (bf16[256,960]{1,0:T(8,128)(2,1)S(1)}, bf16[256,960]{1,0:T(8,128)(2,1)}, u32[]{:S(2)}) copy-start(bf16[256,960]{1,0:T(8,128)(2,1)} %get-tuple-element.172) | copy-start | bytes 1474564
  162.6 24.8 %slice-start = ((s8[4915200]{0:T(1024)(128)(4,1)}), s8[4194304]{0:T(1024)(128)(4,1)S(1)}, s32[]{:S(2)}) async-start(s8[4915200]{0:T(1024)(128)(4,1)} %bitcast.63), calls=%async_computation | async-start | bytes 8388608
  166.2 16.0 %copy-start.12 = (bf16[512,960]{1,0:T(8,128)(2,1)}, bf16[512,960]{1,0:T(8,128)(2,1)S(1)}, u32[]{:S(2)}) copy-start(bf16[512,960]{1,0:T(8,128)(2,1)S(1)} %get-tuple-element.151.queries) | copy-start | bytes 2949124
  166.2 16.0 %copy-start.30 = (bf16[512,640]{1,0:T(8,128)(2,1)}, bf16[512,640]{1,0:T(8,128)(2,1)S(1)}, u32[]{:S(2)}) copy-start(bf16[512,640]{1,0:T(8,128)(2,1)S(1)} %get-tuple-element.153.pair) | copy-start | bytes 1966084
  166.2 16.0 %copy-start.54 = (bf16[512,960]{1,0:T(8,128)(2,1)}, bf16[512,960]{1,0:T(8,128)(2,1)S(1)}, u32[]{:S(2)}) copy-start(bf16[512,960]{1,0:T(8,128)(2,1)S(1)} %get-tuple-element.214.refs_1_) | copy-start | bytes 2949124
  166.3 10.7 %collective-permute-start = (bf16[512,640]{1,0:T(8,128)(2,1)S(1)}, bf16[512,640]{1,0:T(8,128)(2,1)S(1)}, u32[]{:S(2)}, u32[]{:S(2)}) collective-permute-start(bf16[512,640]{1,0:T(8,128)(2,1)S(1)} %get-tuple-element.153.pair), channel_id=1, source_target_pairs={{0,1},{1,0},{2,3},{3,2},{4,6},{6,4},{5,7},{7,5},{8,9},{9,8},{10,11... | collective-permute-start | bytes 1966088 | tf_op jit(solution)/shard_map/ppermute | solution.py:1589
  176.9 36.4 %collective-permute-start.3 = (bf16[256,960]{1,0:T(8,128)(2,1)S(1)}, bf16[256,960]{1,0:T(8,128)(2,1)S(1)}, u32[]{:S(2)}, u32[]{:S(2)}) collective-permute-start(bf16[256,960]{1,0:T(8,128)(2,1)S(1)} %copy-done.78), channel_id=1, source_target_pairs={{0,3},{3,0},{1,2},{2,1},{4,7},{7,4},{5,6},{6,5},{8,11},{11,8},{9,1... | collective-permute-start | bytes 1474568 | tf_op jit(solution)/shard_map/ppermute | solution.py:1589
  177.8 9.6 %slice-start.1 = ((s8[4915200]{0:T(1024)(128)(4,1)}), s8[720896]{0:T(1024)(128)(4,1)S(1)}, s32[]{:S(2)}) async-start(s8[4915200]{0:T(1024)(128)(4,1)} %bitcast.63), calls=%async_computation.1 | async-start | bytes 1441792
  187.3 15.0 %copy-start.16 = (bf16[512,960]{1,0:T(8,128)(2,1)}, bf16[512,960]{1,0:T(8,128)(2,1)S(1)}, u32[]{:S(2)}) copy-start(bf16[512,960]{1,0:T(8,128)(2,1)S(1)} %get-tuple-element.156.attended.refs_7_) | copy-start | bytes 2949124
  204.3 19.7 %copy-start.8 = (f32[512,960]{1,0:T(8,128)}, f32[512,960]{1,0:T(8,128)S(1)}, u32[]{:S(2)}) copy-start(f32[512,960]{1,0:T(8,128)S(1)} %get-tuple-element.159.state.refs_4_) | copy-start | bytes 5898244
  208.0 10.7 %collective-permute-start.1 = (bf16[512,640]{1,0:T(8,128)(2,1)S(1)}, bf16[512,640]{1,0:T(8,128)(2,1)S(1)}, u32[]{:S(2)}, u32[]{:S(2)}) collective-permute-start(bf16[512,640]{1,0:T(8,128)(2,1)S(1)} %get-tuple-element.161.pair), channel_id=1, source_target_pairs={{0,1},{1,0},{2,3},{3,2},{4,6},{6,4},{5,7},{7,5},{8,9},{9,8},{10,11... | collective-permute-start | bytes 1966088 | tf_op jit(solution)/shard_map/ppermute | solution.py:1589
  223.9 43.6 %copy-start.18 = (bf16[512,960]{1,0:T(8,128)(2,1)}, bf16[512,960]{1,0:T(8,128)(2,1)S(1)}, u32[]{:S(2)}) copy-start(bf16[512,960]{1,0:T(8,128)(2,1)S(1)} %get-tuple-element.162.attended.refs_6_) | copy-start | bytes 2949124
  248.9 18.7 %copy-start.35 = (bf16[512,640]{1,0:T(8,128)(2,1)S(1)}, bf16[512,640]{1,0:T(8,128)(2,1)}, u32[]{:S(2)}) copy-start(bf16[512,640]{1,0:T(8,128)(2,1)} %copy-done.34) | copy-start | bytes 1966084
  273.6 10.7 %collective-permute-start.4 = (bf16[512,640]{1,0:T(8,128)(2,1)S(1)}, bf16[512,640]{1,0:T(8,128)(2,1)S(1)}, u32[]{:S(2)}, u32[]{:S(2)}) collective-permute-start(bf16[512,640]{1,0:T(8,128)(2,1)S(1)} %get-tuple-element.184), channel_id=1, source_target_pairs={{0,1},{1,0},{2,3},{3,2},{4,6},{6,4},{5,7},{7,5},{8,9},{9,8},{10,11... | collective-permute-start | bytes 1966088 | tf_op jit(solution)/shard_map/ppermute | solution.py:1589
  274.5 9.7 %copy-start.9 = (f32[512,960]{1,0:T(8,128)S(1)}, f32[512,960]{1,0:T(8,128)}, u32[]{:S(2)}) copy-start(f32[512,960]{1,0:T(8,128)} %copy-done.8) | copy-start | bytes 5898244
  289.9 17.3 %copy-start.13 = (bf16[512,960]{1,0:T(8,128)(2,1)S(1)}, bf16[512,960]{1,0:T(8,128)(2,1)}, u32[]{:S(2)}) copy-start(bf16[512,960]{1,0:T(8,128)(2,1)} %copy-done.12) | copy-start | bytes 2949124
  289.9 17.3 %copy-start.17 = (bf16[512,960]{1,0:T(8,128)(2,1)S(1)}, bf16[512,960]{1,0:T(8,128)(2,1)}, u32[]{:S(2)}) copy-start(bf16[512,960]{1,0:T(8,128)(2,1)} %copy-done.16) | copy-start | bytes 2949124
  289.9 17.3 %copy-start.33 = (bf16[512,640]{1,0:T(8,128)(2,1)S(1)}, bf16[512,640]{1,0:T(8,128)(2,1)}, u32[]{:S(2)}) copy-start(bf16[512,640]{1,0:T(8,128)(2,1)} %copy-done.32) | copy-start | bytes 1966084
  313.3 14.4 %collective-permute-start.5 = (bf16[512,640]{1,0:T(8,128)(2,1)S(1)}, bf16[512,640]{1,0:T(8,128)(2,1)S(1)}, u32[]{:S(2)}, u32[]{:S(2)}) collective-permute-start(bf16[512,640]{1,0:T(8,128)(2,1)S(1)} %get-tuple-element.197), channel_id=1, source_target_pairs={{0,1},{1,0},{2,3},{3,2},{4,6},{6,4},{5,7},{7,5},{8,9},{9,8},{10,11... | collective-permute-start | bytes 1966088 | tf_op jit(solution)/shard_map/ppermute | solution.py:1589
  314.4 44.3 %collective-permute-start.2 = (bf16[256,960]{1,0:T(8,128)(2,1)S(1)}, bf16[256,960]{1,0:T(8,128)(2,1)S(1)}, u32[]{:S(2)}, u32[]{:S(2)}) collective-permute-start(bf16[256,960]{1,0:T(8,128)(2,1)S(1)} %select_convert_fusion.1), channel_id=1, source_target_pairs={{0,3},{3,0},{1,2},{2,1},{4,7},{7,4},{5,6},{6,5},{8,11},{11,8},{9,1... | collective-permute-start | bytes 1474568 | tf_op jit(solution)/shard_map/ppermute | solution.py:1589
  316.1 11.6 %copy-start.7 = (f32[512,960]{1,0:T(8,128)S(1)}, f32[512,960]{1,0:T(8,128)}, u32[]{:S(2)}) copy-start(f32[512,960]{1,0:T(8,128)} %copy-done.6) | copy-start | bytes 5898244
  333.3 17.0 %copy-start.15 = (bf16[512,960]{1,0:T(8,128)(2,1)S(1)}, bf16[512,960]{1,0:T(8,128)(2,1)}, u32[]{:S(2)}) copy-start(bf16[512,960]{1,0:T(8,128)(2,1)} %get-tuple-element.141.attended.refs_8_) | copy-start | bytes 2949124
  333.3 17.0 %copy-start.23 = (bf16[512,960]{1,0:T(8,128)(2,1)S(1)}, bf16[512,960]{1,0:T(8,128)(2,1)}, u32[]{:S(2)}) copy-start(bf16[512,960]{1,0:T(8,128)(2,1)} %get-tuple-element.166.queries) | copy-start | bytes 2949124
  333.3 17.0 %copy-start.71 = (bf16[512,640]{1,0:T(8,128)(2,1)S(1)}, bf16[512,640]{1,0:T(8,128)(2,1)}, u32[]{:S(2)}) copy-start(bf16[512,640]{1,0:T(8,128)(2,1)} %get-tuple-element.169.pair) | copy-start | bytes 1966084
  357.3 17.7 %collective-permute-start.6 = (bf16[512,640]{1,0:T(8,128)(2,1)}, bf16[512,640]{1,0:T(8,128)(2,1)S(1)}, u32[]{:S(2)}, u32[]{:S(2)}) collective-permute-start(bf16[512,640]{1,0:T(8,128)(2,1)} %get-tuple-element.210), channel_id=1, source_target_pairs={{0,1},{1,0},{2,3},{3,2},{4,6},{6,4},{5,7},{7,5},{8,9},{9,8},{10,11... | collective-permute-start | bytes 1966088 | tf_op jit(solution)/shard_map/ppermute | solution.py:1589
  386.0 127.1 %collective-permute-start.7 = (bf16[256,960]{1,0:T(8,128)(2,1)}, bf16[256,960]{1,0:T(8,128)(2,1)S(1)}, u32[]{:S(2)}, u32[]{:S(2)}) collective-permute-start(bf16[256,960]{1,0:T(8,128)(2,1)} %select_convert_fusion), channel_id=1, source_target_pairs={{0,3},{3,0},{1,2},{2,1},{4,7},{7,4},{5,6},{6,5},{8,11},{11,8},{9,1... | collective-permute-start | bytes 1474568 | tf_op jit(solution)/shard_map/ppermute | solution.py:1589
  (72 other events, 255.9 us)

commit v6 on v5

--- a/solution.py
+++ b/solution.py
@@ -1642,11 +1642,11 @@
         else:
             normed, queries, pair = pre_part(state, attn_g, attn_w, cosine, sine, cols)
             partner = swap(pair, PARTNERS)
-            if r == 1:
-                other_grad, partner = lax.optimization_barrier((other_grad, partner))
-                other_grad = swap(other_grad, ACROSS)
             part = attend_own(queries, pair, info, r)
             attended, logs = attend_rest(queries, partner, info, part, r)
+            if r == 1:
+                other_grad, attended = lax.optimization_barrier((other_grad, attended))
+                other_grad = swap(other_grad, ACROSS)
         after = post_part(
             state, attended, attn_w, ffn_g, routers[r], active, gate_w, up_w, down_w, used
         )

time: 522 us -> 518 us (level)
  no operation moved by 1% of the time
where the time goes in v6:
time: 518 us; the launch traced here: 513 us
  Pallas kernels  414 us (80%)
  local copies, waits for them, and re-layouts  64.5 us (12%)
  waiting for transfers between devices  12.9 us (2%)
  other arithmetic  11.1 us (2%)
  starting transfers between devices  9.2 us (2%)
    pallas_call x1, Pallas kernels, finish(): pl.pallas_call(functools.partial(finish_kernel, layers, count, low_col),...  118 us
    pallas_call x1, Pallas kernels, open_all(): pl.pallas_call(functools.partial(open_kernel, layers, micros, cols), out_...  116 us
    unnamed x207, local copies, waits for them, and re-layouts  54.2 us
    pallas_call x3, Pallas kernels, post_back(): pl.pallas_call(functools.partial(post_back_kernel, used, width // pieces)...  50.8 us
    pallas_call x3, Pallas kernels, post_part(): pl.pallas_call(functools.partial(post_kernel, used, width // pieces), out...  44.7 us
    pallas_call x3, Pallas kernels, attend_own_back(): pl.pallas_call(functools.partial(own_back_kernel, recursion), out_shape=(...  26 us
    pallas_call x3, Pallas kernels, attend_rest_back(): pl.pallas_call(functools.partial(rest_back_kernel, recursion), out_shape=...  19.1 us
    pallas_call x3, Pallas kernels, pre_back(): pl.pallas_call(functools.partial(pre_back_kernel, cols, len(grad_pairs)),...  13 us
  transfers between devices with their start and end apart: 8, of which 4 were waited for; matrix products, arithmetic and copies ran while one was open for 3% of the time, Pallas kernels for 39%

profile of v6, /device:TPU:0, one launch (start us, length us, event | category | flops | bytes accessed | tf_op | source)
XLA Modules:
  0.0 513.5 jit_solution(1358158565799955927)
XLA Ops:
  3.0 2.9 fusion.18
  7.4 2.5 copy.67
  9.9 3.1 select_bitcast_fusion
  18.4 116.1 %open_all.1 = (bf16[2,2,4,2,120,640]{5,4,3,2,1,0:T(8,128)(2,1)S(1)}, bf16[2,2,4,2,120,640]{5,4,3,2,1,0:T(8,128)(2,1)S(1)}, bf16[2,2,4,2,120,640]{5,4,3,2,1,0:T(8...) custom-call(bf16[120,640]{1,0:T(8,128)(2,1)S(1)} %pad_maximum_fusion, ...), custom_call_target="tpu_custom_call" | custom-call | tf_op jit(solution)/shard_map/open_all/pallas_call | solution.py:1118
  136.8 6.0 %copy-done.5 = bf16[2,2,4,2,120,640]{5,4,3,2,1,0:T(8,128)(2,1)S(1)} copy-done((bf16[2,2,4,2,120,640]{5,4,3,2,1,0:T(8,128)(2,1)S(1)}, bf16[2,2,4,2,120,640]{5,4,3,2,1,0:T(8,128)(2,1)}, u32[]{:S(2)}) %copy-start.5) | copy-done | bytes 4915224
  145.6 14.9 %post.3 = (f32[512,960]{1,0:T(8,128)S(1)}, bf16[512,960]{1,0:T(8,128)(2,1)S(1)}, bf16[4,512,640]{2,1,0:T(8,128)(2,1)S(1)}, bf16[4,512,640]{2,1,0:T(8,128)(2,1)},...) custom-call(f32[512,960]{1,0:T(8,128)S(1)} %copy-done.10, ...), custom_call_target="tpu_custom_call" | custom-call | tf_op jit(solution)/shard_map/post/pallas_call | solution.py:572
  162.6 3.6 pre.2
  166.8 4.4 attend_own.2.part
  171.2 5.7 %collective-permute-done.pair = bf16[512,640]{1,0:T(8,128)(2,1)S(1)} collective-permute-done((bf16[512,640]{1,0:T(8,128)(2,1)S(1)}, bf16[512,640]{1,0:T(8,128)(2,1)S(1)}, u32[]{:S(2)}, u32[]{:S(2)}) %collective-permute-start) | collective-permute-done | bytes 655392 | tf_op jit(solution)/shard_map/ppermute | solution.py:1589
  176.9 5.1 attend_rest.2
  183.0 14.9 %post.4 = (f32[512,960]{1,0:T(8,128)S(1)}, bf16[512,960]{1,0:T(8,128)(2,1)S(1)}, bf16[4,512,640]{2,1,0:T(8,128)(2,1)S(1)}, bf16[4,512,640]{2,1,0:T(8,128)(2,1)},...) custom-call(f32[512,960]{1,0:T(8,128)S(1)} %get-tuple-element.149.st, ...), custom_call_target="tpu_custom_call" | custom-call | tf_op jit(solution)/shard_map/post/pallas_call | solution.py:572
  200.0 3.6 pre.3
  204.6 4.3 attend_own.3.part
  210.7 3.5 collective-permute-done.1.pair
  214.3 5.3 %attend_rest.3 = (bf16[512,960]{1,0:T(8,128)(2,1)S(1)}, f32[16,512]{1,0:T(8,128)S(1)}) custom-call(bf16[512,960]{1,0:T(8,128)(2,1)S(1)} %get-tuple-element.160.queries, bf16[512,640]{1,0:T(8,128)(2,1)S(1)} %collective-permute-done.1.pair, f32[8,1024]{1,0:T(8,128)S(1)} %get-tuple-element.154.info, f32[5,80,1536]{2,1,0:T(8,128)S(1)} %attend_own.3.part), custom_call_target="tpu_custom_call" | custom-call | tf_op jit(solution)/shard_map/attend_rest/pallas_call | solution.py:361
  219.6 14.9 %post.5 = (f32[512,960]{1,0:T(8,128)S(1)}, bf16[512,960]{1,0:T(8,128)(2,1)S(1)}, bf16[4,512,640]{2,1,0:T(8,128)(2,1)S(1)}, bf16[4,512,640]{2,1,0:T(8,128)(2,1)},...) custom-call(f32[512,960]{1,0:T(8,128)S(1)} %get-tuple-element.159.st, ...), custom_call_target="tpu_custom_call" | custom-call | tf_op jit(solution)/shard_map/post/pallas_call | solution.py:572
  244.5 16.7 %post_back.3 = (bf16[512,960]{1,0:T(8,128)(2,1)S(1)}, f32[512,960]{1,0:T(8,128)S(1)}, f32[1,960]{1,0:T(1,128)S(1)}, f32[1,960]{1,0:T(1,128)S(1)}, bf16[4,512,256...) custom-call(f32[512,960]{1,0:T(8,128)S(1)} %copy-done.19, ...), custom_call_target="tpu_custom_call" | custom-call | tf_op jit(solution)/shard_map/post_back/pallas_call | solution.py:709
  263.2 6.0 %attend_rest_back.3 = (bf16[512,640]{1,0:T(8,128)(2,1)S(1)}, f32[5,64,1536]{2,1,0:T(8,128)S(1)}, f32[16,512]{1,0:T(8,128)S(1)}) custom-call(bf16[512,960]{1,0:T(8,128)(2,1)S(1)} %get-tuple-element.160.queries, bf16[512,640]{1,0:T(8,128)(2,1)S(1)} %copy-done.35, f32[8,1024]{1,0:T(8,128)S(1)} %get-tuple-element.154.info, ...), custom_call_target="tpu_custom_call" | custom-call | tf_op jit(solution)/shard_map/attend_rest_back/pallas_call | solution.py:426
  270.2 8.7 %attend_own_back.3 = (f32[512,960]{1,0:T(8,128)S(1)}, f32[512,640]{1,0:T(8,128)S(1)}) custom-call(bf16[512,960]{1,0:T(8,128)(2,1)S(1)} %get-tuple-element.160.queries, bf16[512,640]{1,0:T(8,128)(2,1)S(1)} %get-tuple-element.161.pair, f32[8,1024]{1,0:T(8,128)S(1)} %get-tuple-element.154.info, f32[16,512]{1,0:T(8,128)S(1)} %get-tuple-element.171.logs, ...), custom_call_target="tpu_custom_call" | custom-call | tf_op jit(solution)/shard_map/attend_own_back/pallas_call | solution.py:482
  279.9 4.3 pre_back.3
  285.5 17.2 %post_back.4 = (bf16[512,960]{1,0:T(8,128)(2,1)S(1)}, f32[512,960]{1,0:T(8,128)S(1)}, f32[1,960]{1,0:T(1,128)S(1)}, f32[1,960]{1,0:T(1,128)S(1)}, bf16[4,512,256...) custom-call(f32[512,960]{1,0:T(8,128)S(1)} %get-tuple-element.186.gr, ...), custom_call_target="tpu_custom_call" | custom-call | tf_op jit(solution)/shard_map/post_back/pallas_call | solution.py:709
  302.8 6.1 %attend_rest_back.4 = (bf16[512,640]{1,0:T(8,128)(2,1)S(1)}, f32[5,64,1536]{2,1,0:T(8,128)S(1)}, f32[16,512]{1,0:T(8,128)S(1)}) custom-call(bf16[512,960]{1,0:T(8,128)(2,1)S(1)} %copy-done.13, bf16[512,640]{1,0:T(8,128)(2,1)S(1)} %copy-done.33, f32[8,1024]{1,0:T(8,128)S(1)} %get-tuple-element.154.info, bf16[512,960]{1,0:T(8,128)(2,1)S(1)} %copy-done.17, ...), custom_call_target="tpu_custom_call" | custom-call | tf_op jit(solution)/shard_map/attend_rest_back/pallas_call | solution.py:426
  311.7 8.7 %attend_own_back.4 = (f32[512,960]{1,0:T(8,128)S(1)}, f32[512,640]{1,0:T(8,128)S(1)}) custom-call(bf16[512,960]{1,0:T(8,128)(2,1)S(1)} %copy-done.13, bf16[512,640]{1,0:T(8,128)(2,1)S(1)} %copy-done.31, f32[8,1024]{1,0:T(8,128)S(1)} %get-tuple-element.154.info, f32[16,512]{1,0:T(8,128)S(1)} %get-tuple-element.170.logs, ...), custom_call_target="tpu_custom_call" | custom-call | tf_op jit(solution)/shard_map/attend_own_back/pallas_call | solution.py:482
  320.5 2.8 collective-permute-done.5.refs_2_
  323.3 4.2 pre_back.4
  328.9 16.9 %post_back.5 = (bf16[512,960]{1,0:T(8,128)(2,1)S(1)}, f32[512,960]{1,0:T(8,128)S(1)}, f32[1,960]{1,0:T(1,128)S(1)}, f32[1,960]{1,0:T(1,128)S(1)}, bf16[4,512,256...) custom-call(f32[512,960]{1,0:T(8,128)S(1)} %get-tuple-element.199.gr, ...), custom_call_target="tpu_custom_call" | custom-call | tf_op jit(solution)/shard_map/post_back/pallas_call | solution.py:709
  346.0 7.0 %attend_rest_back.5 = (bf16[512,640]{1,0:T(8,128)(2,1)}, f32[5,64,1536]{2,1,0:T(8,128)S(1)}, f32[16,512]{1,0:T(8,128)S(1)}) custom-call(bf16[512,960]{1,0:T(8,128)(2,1)S(1)} %copy-done.23, bf16[512,640]{1,0:T(8,128)(2,1)S(1)} %copy-done.71, f32[8,1024]{1,0:T(8,128)S(1)} %get-tuple-element.154.info, bf16[512,960]{1,0:T(8,128)(2,1)S(1)} %copy-done.15, ...), custom_call_target="tpu_custom_call" | custom-call | tf_op jit(solution)/shard_map/attend_rest_back/pallas_call | solution.py:426
  356.1 3.3 copy.58
  362.1 8.5 %attend_own_back.5 = (f32[512,960]{1,0:T(8,128)S(1)}, f32[512,640]{1,0:T(8,128)S(1)}) custom-call(bf16[512,960]{1,0:T(8,128)(2,1)S(1)} %copy-done.24, bf16[512,640]{1,0:T(8,128)(2,1)S(1)} %copy-done.70, f32[8,1024]{1,0:T(8,128)S(1)} %get-tuple-element.154.info, f32[16,512]{1,0:T(8,128)S(1)} %get-tuple-element.168.logs, ...), custom_call_target="tpu_custom_call" | custom-call | tf_op jit(solution)/shard_map/attend_own_back/pallas_call | solution.py:482
  371.5 2.4 copy-done.1
  375.0 4.4 pre_back.5
  384.4 117.7 %finish.1 = (f32[120,640]{1,0:T(8,128)}, f32[120,640]{1,0:T(8,128)}, f32[120,640]{1,0:T(8,128)}, f32[320,256]{1,0:T(8,128)}) custom-call(bf16[512,960]{1,0:T(8,128)(2,1)} %copy-done.56, bf16[512,960]{1,0:T(8,128)(2,1)} %copy-done.54, bf16[512,960]{1,0:T(8,128)(2,1)} %get-tuple-element.215.refs_2_, bf16[4,512,512]{2,1,0:T(8,128)(2,1)} %copy-done.37, ...), custom_call_target="tpu_custom_call" | custom-call | tf_op jit(solution)/shard_map/finish/pallas_call | solution.py:1477
  (252 shorter events, 65.4 us)
Async XLA Ops:
  136.8 23.7 %copy-start.47 = (f32[512,128]{1,0:T(8,128)}, f32[512,128]{1,0:T(8,128)S(1)}, u32[]{:S(2)}) copy-start(f32[512,128]{1,0:T(8,128)S(1)} %get-tuple-element.145.active) | copy-start | bytes 786436
  136.8 46.2 %copy-start.49 = (f32[512,128]{1,0:T(8,128)}, f32[512,128]{1,0:T(8,128)S(1)}, u32[]{:S(2)}) copy-start(f32[512,128]{1,0:T(8,128)S(1)} %get-tuple-element.158.active) | copy-start | bytes 786436
  136.8 82.8 %copy-start.2 = (bf16[2,2,4,2,120,640]{5,4,3,2,1,0:T(8,128)(2,1)}, bf16[2,2,4,2,120,640]{5,4,3,2,1,0:T(8,128)(2,1)S(1)}, u32[]{:S(2)}) copy-start(bf16[2,2,4,2,120,640]{5,4,3,2,1,0:T(8,128)(2,1)S(1)} %get-tuple-element.146) | copy-start | bytes 14745604
  136.8 82.8 %copy-start.51 = (f32[512,128]{1,0:T(8,128)}, f32[512,128]{1,0:T(8,128)S(1)}, u32[]{:S(2)}) copy-start(f32[512,128]{1,0:T(8,128)S(1)} %get-tuple-element.164.active) | copy-start | bytes 786436
  136.8 192.1 %copy-start = (bf16[2,2,4,2,120,640]{5,4,3,2,1,0:T(8,128)(2,1)}, bf16[2,2,4,2,120,640]{5,4,3,2,1,0:T(8,128)(2,1)S(1)}, u32[]{:S(2)}) copy-start(bf16[2,2,4,2,120,640]{5,4,3,2,1,0:T(8,128)(2,1)S(1)} %get-tuple-element.142) | copy-start | bytes 14745604
  162.5 20.5 %copy-start.6 = (f32[512,960]{1,0:T(8,128)}, f32[512,960]{1,0:T(8,128)S(1)}, u32[]{:S(2)}) copy-start(f32[512,960]{1,0:T(8,128)S(1)} %get-tuple-element.149.state.refs_4_) | copy-start | bytes 5898244
  162.5 20.5 %slice-start = ((s8[4915200]{0:T(1024)(128)(4,1)}), s8[4194304]{0:T(1024)(128)(4,1)S(1)}, s32[]{:S(2)}) async-start(s8[4915200]{0:T(1024)(128)(4,1)} %bitcast.63), calls=%async_computation | async-start | bytes 8388608
  166.2 10.7 %copy-start.12 = (bf16[512,960]{1,0:T(8,128)(2,1)}, bf16[512,960]{1,0:T(8,128)(2,1)S(1)}, u32[]{:S(2)}) copy-start(bf16[512,960]{1,0:T(8,128)(2,1)S(1)} %get-tuple-element.152.queries) | copy-start | bytes 2949124
  166.2 10.7 %collective-permute-start = (bf16[512,640]{1,0:T(8,128)(2,1)S(1)}, bf16[512,640]{1,0:T(8,128)(2,1)S(1)}, u32[]{:S(2)}, u32[]{:S(2)}) collective-permute-start(bf16[512,640]{1,0:T(8,128)(2,1)S(1)} %get-tuple-element.153.pair), channel_id=1, source_target_pairs={{0,1},{1,0},{2,3},{3,2},{4,6},{6,4},{5,7},{7,5},{8,9},{9,8},{10,11... | collective-permute-start | bytes 1966088 | tf_op jit(solution)/shard_map/ppermute | solution.py:1589
  166.8 16.2 %slice-start.1 = ((s8[4915200]{0:T(1024)(128)(4,1)}), s8[720896]{0:T(1024)(128)(4,1)S(1)}, s32[]{:S(2)}) async-start(s8[4915200]{0:T(1024)(128)(4,1)} %bitcast.63), calls=%async_computation.1 | async-start | bytes 1441792
  171.2 10.8 %copy-start.78 = (bf16[256,960]{1,0:T(8,128)(2,1)S(1)}, bf16[256,960]{1,0:T(8,128)(2,1)}, u32[]{:S(2)}) copy-start(bf16[256,960]{1,0:T(8,128)(2,1)} %get-tuple-element.172) | copy-start | bytes 1474564
  182.0 16.0 %copy-start.16 = (bf16[512,960]{1,0:T(8,128)(2,1)}, bf16[512,960]{1,0:T(8,128)(2,1)S(1)}, u32[]{:S(2)}) copy-start(bf16[512,960]{1,0:T(8,128)(2,1)S(1)} %get-tuple-element.156.attended.refs_7_) | copy-start | bytes 2949124
  182.0 26.9 %collective-permute-start.3 = (bf16[256,960]{1,0:T(8,128)(2,1)S(1)}, bf16[256,960]{1,0:T(8,128)(2,1)S(1)}, u32[]{:S(2)}, u32[]{:S(2)}) collective-permute-start(bf16[256,960]{1,0:T(8,128)(2,1)S(1)} %copy-done.78), channel_id=1, source_target_pairs={{0,3},{3,0},{1,2},{2,1},{4,7},{7,4},{5,6},{6,5},{8,11},{11,8},{9,1... | collective-permute-start | bytes 1474568 | tf_op jit(solution)/shard_map/ppermute | solution.py:1589
  200.0 19.7 %copy-start.8 = (f32[512,960]{1,0:T(8,128)}, f32[512,960]{1,0:T(8,128)S(1)}, u32[]{:S(2)}) copy-start(f32[512,960]{1,0:T(8,128)S(1)} %get-tuple-element.159.state.refs_4_) | copy-start | bytes 5898244
  203.6 10.7 %collective-permute-start.1 = (bf16[512,640]{1,0:T(8,128)(2,1)S(1)}, bf16[512,640]{1,0:T(8,128)(2,1)S(1)}, u32[]{:S(2)}, u32[]{:S(2)}) collective-permute-start(bf16[512,640]{1,0:T(8,128)(2,1)S(1)} %get-tuple-element.161.pair), channel_id=1, source_target_pairs={{0,1},{1,0},{2,3},{3,2},{4,6},{6,4},{5,7},{7,5},{8,9},{9,8},{10,11... | collective-permute-start | bytes 1966088 | tf_op jit(solution)/shard_map/ppermute | solution.py:1589
  219.6 43.6 %copy-start.18 = (bf16[512,960]{1,0:T(8,128)(2,1)}, bf16[512,960]{1,0:T(8,128)(2,1)S(1)}, u32[]{:S(2)}) copy-start(bf16[512,960]{1,0:T(8,128)(2,1)S(1)} %get-tuple-element.162.attended.refs_6_) | copy-start | bytes 2949124
  244.5 18.7 %copy-start.35 = (bf16[512,640]{1,0:T(8,128)(2,1)S(1)}, bf16[512,640]{1,0:T(8,128)(2,1)}, u32[]{:S(2)}) copy-start(bf16[512,640]{1,0:T(8,128)(2,1)} %copy-done.34) | copy-start | bytes 1966084
  269.2 10.7 %collective-permute-start.4 = (bf16[512,640]{1,0:T(8,128)(2,1)S(1)}, bf16[512,640]{1,0:T(8,128)(2,1)S(1)}, u32[]{:S(2)}, u32[]{:S(2)}) collective-permute-start(bf16[512,640]{1,0:T(8,128)(2,1)S(1)} %get-tuple-element.184), channel_id=1, source_target_pairs={{0,1},{1,0},{2,3},{3,2},{4,6},{6,4},{5,7},{7,5},{8,9},{9,8},{10,11... | collective-permute-start | bytes 1966088 | tf_op jit(solution)/shard_map/ppermute | solution.py:1589
  270.2 9.7 %copy-start.9 = (f32[512,960]{1,0:T(8,128)S(1)}, f32[512,960]{1,0:T(8,128)}, u32[]{:S(2)}) copy-start(f32[512,960]{1,0:T(8,128)} %copy-done.8) | copy-start | bytes 5898244
  285.5 17.3 %copy-start.13 = (bf16[512,960]{1,0:T(8,128)(2,1)S(1)}, bf16[512,960]{1,0:T(8,128)(2,1)}, u32[]{:S(2)}) copy-start(bf16[512,960]{1,0:T(8,128)(2,1)} %copy-done.12) | copy-start | bytes 2949124
  285.5 17.3 %copy-start.17 = (bf16[512,960]{1,0:T(8,128)(2,1)S(1)}, bf16[512,960]{1,0:T(8,128)(2,1)}, u32[]{:S(2)}) copy-start(bf16[512,960]{1,0:T(8,128)(2,1)} %copy-done.16) | copy-start | bytes 2949124
  285.5 17.3 %copy-start.33 = (bf16[512,640]{1,0:T(8,128)(2,1)S(1)}, bf16[512,640]{1,0:T(8,128)(2,1)}, u32[]{:S(2)}) copy-start(bf16[512,640]{1,0:T(8,128)(2,1)} %copy-done.32) | copy-start | bytes 1966084
  308.9 14.4 %collective-permute-start.5 = (bf16[512,640]{1,0:T(8,128)(2,1)S(1)}, bf16[512,640]{1,0:T(8,128)(2,1)S(1)}, u32[]{:S(2)}, u32[]{:S(2)}) collective-permute-start(bf16[512,640]{1,0:T(8,128)(2,1)S(1)} %get-tuple-element.197), channel_id=1, source_target_pairs={{0,1},{1,0},{2,3},{3,2},{4,6},{6,4},{5,7},{7,5},{8,9},{9,8},{10,11... | collective-permute-start | bytes 1966088 | tf_op jit(solution)/shard_map/ppermute | solution.py:1589
  310.0 44.3 %collective-permute-start.2 = (bf16[256,960]{1,0:T(8,128)(2,1)S(1)}, bf16[256,960]{1,0:T(8,128)(2,1)S(1)}, u32[]{:S(2)}, u32[]{:S(2)}) collective-permute-start(bf16[256,960]{1,0:T(8,128)(2,1)S(1)} %select_convert_fusion.1), channel_id=1, source_target_pairs={{0,3},{3,0},{1,2},{2,1},{4,7},{7,4},{5,6},{6,5},{8,11},{11,8},{9,1... | collective-permute-start | bytes 1474568 | tf_op jit(solution)/shard_map/ppermute | solution.py:1589
  311.7 11.6 %copy-start.7 = (f32[512,960]{1,0:T(8,128)S(1)}, f32[512,960]{1,0:T(8,128)}, u32[]{:S(2)}) copy-start(f32[512,960]{1,0:T(8,128)} %copy-done.6) | copy-start | bytes 5898244
  328.9 17.0 %copy-start.15 = (bf16[512,960]{1,0:T(8,128)(2,1)S(1)}, bf16[512,960]{1,0:T(8,128)(2,1)}, u32[]{:S(2)}) copy-start(bf16[512,960]{1,0:T(8,128)(2,1)} %get-tuple-element.141.attended.refs_8_) | copy-start | bytes 2949124
  328.9 17.0 %copy-start.23 = (bf16[512,960]{1,0:T(8,128)(2,1)S(1)}, bf16[512,960]{1,0:T(8,128)(2,1)}, u32[]{:S(2)}) copy-start(bf16[512,960]{1,0:T(8,128)(2,1)} %get-tuple-element.166.queries) | copy-start | bytes 2949124
  328.9 17.0 %copy-start.71 = (bf16[512,640]{1,0:T(8,128)(2,1)S(1)}, bf16[512,640]{1,0:T(8,128)(2,1)}, u32[]{:S(2)}) copy-start(bf16[512,640]{1,0:T(8,128)(2,1)} %get-tuple-element.169.pair) | copy-start | bytes 1966084
  352.9 17.7 %collective-permute-start.6 = (bf16[512,640]{1,0:T(8,128)(2,1)}, bf16[512,640]{1,0:T(8,128)(2,1)S(1)}, u32[]{:S(2)}, u32[]{:S(2)}) collective-permute-start(bf16[512,640]{1,0:T(8,128)(2,1)} %get-tuple-element.210), channel_id=1, source_target_pairs={{0,1},{1,0},{2,3},{3,2},{4,6},{6,4},{5,7},{7,5},{8,9},{9,8},{10,11... | collective-permute-start | bytes 1966088 | tf_op jit(solution)/shard_map/ppermute | solution.py:1589
  362.1 9.4 %copy-start.11 = (f32[512,960]{1,0:T(8,128)S(1)}, f32[512,960]{1,0:T(8,128)}, u32[]{:S(2)}) copy-start(f32[512,960]{1,0:T(8,128)} %get-tuple-element.140.state.refs_4_) | copy-start | bytes 5898244
  362.1 9.4 %copy-start.41 = (f32[512,960]{1,0:T(8,128)S(1)}, f32[512,960]{1,0:T(8,128)}, u32[]{:S(2)}) copy-start(f32[512,960]{1,0:T(8,128)} %copy-done.40) | copy-start | bytes 5898244
  381.6 127.1 %collective-permute-start.7 = (bf16[256,960]{1,0:T(8,128)(2,1)}, bf16[256,960]{1,0:T(8,128)(2,1)S(1)}, u32[]{:S(2)}, u32[]{:S(2)}) collective-permute-start(bf16[256,960]{1,0:T(8,128)(2,1)} %select_convert_fusion), channel_id=1, source_target_pairs={{0,3},{3,0},{1,2},{2,1},{4,7},{7,4},{5,6},{6,5},{8,11},{11,8},{9,1... | collective-permute-start | bytes 1474568 | tf_op jit(solution)/shard_map/ppermute | solution.py:1589
  (72 other events, 247.1 us)
